TPU v7x, 32 devices: a whole 2x2x4 slice. The times are simulated.
32 devices in a mesh: pipe: 4 (over y, core), expert: 8 (over z, x).
Axes of the slice: x: 2, y: 2, z: 4, core: 2. Of those that a mesh axis runs over, the one named last changes fastest.
Arguments:
- next_input: bfloat16 [4, 2048, 2048], P('pipe', 'expert'), may hold values from -6 to 6
- prev_input: bfloat16 [4, 2048, 2048], P('pipe', 'expert'), may hold values from -6 to 6
- next_cot: bfloat16 [4, 2048, 2048], P('pipe', 'expert'), may hold values from -6 to 6
- gate_weight: bfloat16 [4, 8, 2048, 768], P('pipe', 'expert'), may hold values from -0.125 to 0.125
- up_weight: bfloat16 [4, 8, 2048, 768], P('pipe', 'expert'), may hold values from -0.125 to 0.125
- down_weight: bfloat16 [4, 8, 768, 2048], P('pipe', 'expert'), may hold values from -0.21875 to 0.21875
- router: bfloat16 [4, 2048, 8], P('pipe'), may hold values from -0.125 to 0.125
- gain: float32 [4, 2048], P('pipe'), may hold values from 0.1 to 1.9
- next_routes: int32 [4, 2048, 2], P('pipe', 'expert'), may hold values from 0 to 7, all different within a row
- prev_routes: int32 [4, 2048, 2], P('pipe', 'expert'), may hold values from 0 to 7, all different within a row
- next_priority: int32 [4, 2048], P('pipe', 'expert'), may hold values from 0 to 2047, each once within a row
- prev_priority: int32 [4, 2048], P('pipe', 'expert'), may hold values from 0 to 2047, each once within a row
Outputs:
- forward_out: bfloat16 [4, 2048, 2048], P('pipe', 'expert')
- input_grad: bfloat16 [4, 2048, 2048], P('pipe', 'expert')
- gate_grad: bfloat16 [4, 8, 2048, 768], P('pipe', 'expert')
- up_grad: bfloat16 [4, 8, 2048, 768], P('pipe', 'expert')
- down_grad: bfloat16 [4, 8, 768, 2048], P('pipe', 'expert')
- router_grad: float32 [4, 2048, 8], P('pipe')
- gain_grad: float32 [4, 2048], P('pipe')
All inputs are finite; a program needn't handle non-finite values.
Results may differ from a plain program's by a relative error of at most 0.0085.
Values may be sent and summed in bfloat16 or wider, within the bound.
No kernel may reach another device: no remote copies, remote signals or barrier semaphores. Data moves between devices by JAX's collectives and lax.ppermute only.
A program may use at most 128 MiB of HBM per device.

v0:
```python
import functools

import jax
import jax.numpy as jnp
from jax import lax
from jax.experimental import pallas as pl
from jax.experimental.pallas import tpu as pltpu
from jax.sharding import PartitionSpec as P

EPS = 1e-06
F32 = jnp.float32
BF16 = jnp.bfloat16
VMEM_BYTES = 56 * 1024 * 1024
LANES = 128
SCALE = 64


def hop(block, pipe_step, flip, name):
    pipes, experts = lax.axis_size("pipe"), lax.axis_size("expert")
    with jax.named_scope(name):
        if pipe_step == 0:
            return lax.ppermute(block, "expert", [(e, e ^ flip) for e in range(experts)])
        route = [
            (p * experts + e, ((p + pipe_step) % pipes) * experts + (e ^ flip))
            for p in range(pipes)
            for e in range(experts)
        ]
        return lax.ppermute(block, ("pipe", "expert"), route)


def after(block, *earlier):
    return lax.optimization_barrier((block,) + earlier)[0]


def dot(a, b):
    return jnp.dot(a, b, preferred_element_type=F32)


def dot_t(a, b):
    return lax.dot_general(a, b, (((1,), (1,)), ((), ())), preferred_element_type=F32)


def t_dot(a, b, precision=None):
    dims = (((0,), (0,)), ((), ()))
    return lax.dot_general(a, b, dims, preferred_element_type=F32, precision=precision)


def iota(shape, dim):
    return lax.broadcasted_iota(jnp.int32, shape, dim)


def call(kernel, name, outs, ins, grid=(), in_specs=None, out_specs=None, scratch=(), flops=0):
    whole = pl.BlockSpec(memory_space=pltpu.VMEM)
    moved = sum(a.size * a.dtype.itemsize for a in list(outs) + list(ins))
    return pl.pallas_call(
        kernel,
        out_shape=[jax.ShapeDtypeStruct(o.shape, o.dtype) for o in outs],
        grid=grid,
        in_specs=in_specs or [whole] * len(ins),
        out_specs=out_specs or [whole] * len(outs),
        scratch_shapes=list(scratch),
        compiler_params=pltpu.CompilerParams(vmem_limit_bytes=VMEM_BYTES),
        cost_estimate=pl.CostEstimate(flops=flops // SCALE, bytes_accessed=moved // SCALE, transcendentals=0),
        name=name,
    )(*ins)


def shape(dims, dtype=BF16):
    return jax.ShapeDtypeStruct(tuple(dims), dtype)


def rank_kernel(capacity, top, table_ref, *rank_refs):
    experts, tokens = rank_refs[0].shape
    for batch, rank_ref in enumerate(rank_refs):
        row = 2 * top + batch
        order = jnp.broadcast_to(table_ref[row : row + 1, :], (tokens, tokens))
        before = (order.T < order).astype(F32).astype(BF16)
        chosen = iota((experts, tokens), 0) < 0
        for routes in route_rows(table_ref, batch, top):
            chosen = chosen | (routes == iota((experts, tokens), 0))
        count = dot(chosen.astype(F32).astype(BF16), before)
        rank_ref[...] = jnp.where(chosen & (count < capacity), count.astype(jnp.int32), -1)


def route_rows(ref, batch, top):
    return [ref[batch * top + j : batch * top + j + 1, :] for j in range(top)]


def slot_mask(rank_ref, e, slots):
    rank = rank_ref[e : e + 1, :]
    return iota((slots, rank.shape[1]), 0) == rank


def one_hot(mask):
    return jnp.where(mask, 1.0, 0.0).astype(BF16)


def normalise(x_ref, gain_ref, normed_ref, step=32):
    def part(i, carry):
        rows = pl.ds(pl.multiple_of(i * step, step), step)
        values = x_ref[rows, :].astype(F32)
        scale = lax.rsqrt(jnp.mean(values * values, axis=-1, keepdims=True) + EPS)
        normed_ref[rows, :] = (values * scale * gain_ref[...]).astype(BF16)
        return carry

    lax.fori_loop(0, x_ref.shape[0] // step, part, 0)


def gates(normed_ref, router_ref, routes, lifted_ref, weight_ref):
    logits = dot_t(router_ref[...], normed_ref[...])
    everyone = iota(logits.shape, 0)
    lifted = [
        jax.nn.sigmoid(jnp.sum(jnp.where(r == everyone, logits, 0.0), axis=0, keepdims=True))
        for r in routes
    ]
    total = functools.reduce(jnp.add, lifted)
    weight = jnp.zeros(weight_ref.shape, F32)
    for j, (r, value) in enumerate(zip(routes, lifted)):
        if lifted_ref is not None:
            lifted_ref[j : j + 1, :] = value
        weight = weight + jnp.where(r == everyone, value / total, 0.0)
    weight_ref[...] = weight


def put_rows(rank_ref, block_ref, message_ref):
    for e in range(message_ref.shape[0]):
        hot = one_hot(slot_mask(rank_ref, e, message_ref.shape[1]))
        message_ref[e] = dot(hot, block_ref[...]).astype(BF16)


def rows_kernel(batch, top, *refs):
    x_ref, gain_ref, router_ref, table_ref, rank_ref = refs[:5]
    message_ref, weight_ref, normed_ref, lifted_ref = (*refs[5:], None)[:4]
    normalise(x_ref, gain_ref, normed_ref)
    put_rows(rank_ref, normed_ref, message_ref)
    gates(normed_ref, router_ref, route_rows(table_ref, batch, top), lifted_ref, weight_ref)


def cots_kernel(rank_ref, weight_ref, x_ref, message_ref):
    width = x_ref.shape[1]
    for e in range(message_ref.shape[0]):
        hot = one_hot(slot_mask(rank_ref, e, message_ref.shape[1]))
        message_ref[e, :, :width] = dot(hot, x_ref[...]).astype(BF16)
        weight = weight_ref[e : e + 1, :].astype(BF16)
        weight = jnp.broadcast_to(weight, (LANES, weight.shape[1]))
        message_ref[e, :, width:] = dot_t(hot, weight).astype(BF16)


def flat_of(ref):
    return ref[...].reshape(-1, ref.shape[-1])


def add(acc, value):
    step = pl.program_id(0)

    @pl.when(step == 0)
    def _():
        acc[...] = value

    @pl.when(step > 0)
    def _():
        acc[...] += value


def expert_kernel(rows_ref, cot_ref, gate_w, up_w, down_w, *refs):
    message_ref, scaled_ref, active_ref, gate_part_ref, up_part_ref, acc_out, acc_grad = refs
    senders, slots, width = rows_ref.shape

    @pl.when(pl.program_id(0) == 0)
    def _():
        for k in range(senders):
            scale = cot_ref[k, :, width:].astype(F32)[:, :1]
            scaled = (scale * cot_ref[k, :, :width].astype(F32)).astype(BF16)
            scaled_ref[k * slots : (k + 1) * slots, :] = scaled

    rows = flat_of(rows_ref)
    gate = dot(rows, gate_w[...])
    upper = dot(rows, up_w[...])
    sig = jax.nn.sigmoid(gate)
    active = (gate * sig * upper).astype(BF16)
    active_ref[...] = active
    act_grad = dot_t(scaled_ref[...], down_w[...])
    gate_part = (act_grad * upper * sig * (1.0 + gate * (1.0 - sig))).astype(BF16)
    up_part = (act_grad * (gate * sig)).astype(BF16)
    gate_part_ref[...] = gate_part
    up_part_ref[...] = up_part
    add(acc_grad, dot_t(gate_part, gate_w[...]) + dot_t(up_part, up_w[...]))
    add(acc_out, dot(active, down_w[...]))

    @pl.when(pl.program_id(0) == pl.num_programs(0) - 1)
    def _():
        for k in range(senders):
            part = slice(k * slots, (k + 1) * slots)
            message_ref[k, :, :width] = acc_grad[part, :].astype(BF16)
            result = acc_out[part, :].astype(BF16).astype(F32)
            cot = cot_ref[k, :, :width].astype(F32)
            inner = jnp.sum(cot * result, axis=1, keepdims=True).astype(BF16)
            message_ref[k, :, width:] = jnp.broadcast_to(inner, (slots, LANES))


def forward_kernel(rows_ref, gate_w, up_w, down_w, out_ref, acc):
    rows = flat_of(rows_ref)
    gate = dot(rows, gate_w[...])
    active = (gate * jax.nn.sigmoid(gate) * dot(rows, up_w[...])).astype(BF16)
    add(acc, dot(active, down_w[...]))

    @pl.when(pl.program_id(0) == pl.num_programs(0) - 1)
    def _():
        out_ref[...] = acc[...].astype(BF16).reshape(out_ref.shape)


def out_kernel(rank_ref, weight_ref, x_ref, rows_ref, out_ref, high_ref, low_ref):
    slots = rows_ref.shape[1]
    for e in range(rank_ref.shape[0]):
        part = slice(e * slots, (e + 1) * slots)
        value = jnp.where(slot_mask(rank_ref, e, slots), weight_ref[e : e + 1, :], 0.0)
        high = value.astype(BF16)
        high_ref[part, :] = high
        low_ref[part, :] = (value - high.astype(F32)).astype(BF16)
    rows = flat_of(rows_ref)
    total = t_dot(high_ref[...], rows) + t_dot(low_ref[...], rows)
    out_ref[...] = (x_ref[...].astype(F32) + total).astype(BF16)


def source_kernel(top, *refs):
    rank_ref, grads_ref, table_ref, lifted_ref = refs[:4]
    router_ref, normed_ref, xp_ref, dy_ref, gain_ref = refs[4:9]
    grad_ref, sums_ref, hot_ref, terms_ref = refs[9:]
    experts, tokens = rank_ref.shape
    slots, width = grads_ref.shape[1], xp_ref.shape[1]
    for e in range(experts):
        hot = one_hot(slot_mask(rank_ref, e, slots))
        hot_ref[e * slots : (e + 1) * slots, :] = hot
        terms_ref[e : e + 1, :] = t_dot(grads_ref[e, :, width:], hot)[:1, :]
    routes = route_rows(table_ref, 1, top)
    everyone = iota((experts, tokens), 0)
    lifted = [lifted_ref[j : j + 1, :] for j in range(top)]
    dweight = [
        jnp.sum(jnp.where(r == everyone, terms_ref[...], 0.0), axis=0, keepdims=True)
        for r in routes
    ]
    total = functools.reduce(jnp.add, lifted)
    both = functools.reduce(jnp.add, [d * l for d, l in zip(dweight, lifted)])
    dlogits = jnp.zeros((experts, tokens), F32)
    for r, d, l in zip(routes, dweight, lifted):
        dsel = (d / total - both / (total * total)) * l * (1.0 - l)
        dlogits = dlogits + jnp.where(r == everyone, dsel, 0.0)
    exact = lax.Precision.HIGHEST
    normed = normed_ref[...].astype(F32)
    sums_ref[...] = jnp.zeros_like(sums_ref)
    sums_ref[:experts, :] = jnp.dot(dlogits, normed, precision=exact, preferred_element_type=F32)
    dnormed = t_dot(hot_ref[...], grads_ref[:, :, :width].reshape(-1, width))
    dnormed = dnormed + t_dot(dlogits, router_ref[...].astype(F32), precision=exact)
    values = xp_ref[...].astype(F32)
    scale = lax.rsqrt(jnp.mean(values * values, axis=-1, keepdims=True) + EPS)
    bare = values * scale
    sums_ref[experts : experts + 1, :] = jnp.sum(dnormed * bare, axis=0, keepdims=True)
    lifted_grad = dnormed * gain_ref[...]
    slope = jnp.mean(lifted_grad * bare, axis=-1, keepdims=True)
    grad_ref[...] = (dy_ref[...].astype(F32) + scale * (lifted_grad - bare * slope)).astype(BF16)


def per_device(
    next_input,
    prev_input,
    next_cot,
    gate_weight,
    up_weight,
    down_weight,
    router,
    gain,
    next_routes,
    prev_routes,
    next_priority,
    prev_priority,
):
    experts = router.shape[-1]
    tokens, width = next_input.shape[1:]
    hidden = gate_weight.shape[-1]
    top = next_routes.shape[-1]
    capacity = (5 * top * tokens + 4 * experts - 1) // (4 * experts)
    slots = -(-capacity // 16) * 16
    mats = [gate_weight[0, 0], up_weight[0, 0], down_weight[0, 0]]
    gain_row, router_t = (gain, router[0].T)
    partial = functools.partial
    block, message = shape((tokens, width)), shape((experts, slots, width))
    per_token, longer = shape((experts, tokens), F32), shape((experts, slots, width + LANES))

    def exchange(array, name):
        with jax.named_scope(name):
            return lax.all_to_all(array, "expert", 0, 0, tiled=True)

    dy_in = hop(next_cot[0], -1, 0, "dy_in")
    x_in = hop(next_input[0], 1, 0, "x_in")
    xp = prev_input[0]
    table = jnp.concatenate(
        [next_routes[0].T, prev_routes[0].T, next_priority, prev_priority], axis=0
    )
    frank, rank = call(
        partial(rank_kernel, capacity, top), "ranks", [shape((experts, tokens), jnp.int32)] * 2, [table]
    )
    rows, weight, normed, lifted = call(
        partial(rows_kernel, 1, top),
        "rows",
        [message, per_token, block, shape((top, tokens), F32)],
        [xp, gain_row, router_t, table, rank],
    )
    rows = exchange(rows, "rows")
    (cots,) = call(cots_kernel, "cots", [longer], [rank, weight, dy_in])
    cots = exchange(after(cots, rows), "cots")
    frows, fweight = call(
        partial(rows_kernel, 0, top),
        "frows",
        [message, per_token],
        [x_in, gain_row, router_t, table, frank],
        scratch=[pltpu.VMEM((tokens, width), BF16)],
    )
    frows = exchange(after(frows, cots), "frows")

    part = 256 if hidden % 256 == 0 else hidden
    grid = (hidden // part,)
    across = pl.BlockSpec((width, part), lambda f: (0, f))
    mat_specs = [across, across, pl.BlockSpec((part, width), lambda f: (f, 0))]
    count = experts * slots
    flops = 2 * count * width * hidden

    def whole(array):
        dims = array.shape
        return pl.BlockSpec(dims, lambda f: (0,) * len(dims), pipeline_mode=pl.Buffered(1))

    hidden_spec = pl.BlockSpec((count, part), lambda f: (0, f))
    wide = pltpu.VMEM((count, width), F32)
    flat = shape((count, width))
    grads, scaled, active, gate_part, up_part = call(
        expert_kernel,
        "expert",
        [longer, flat] + [shape((count, hidden))] * 3,
        [rows, cots] + mats,
        grid=grid,
        in_specs=[whole(message), whole(longer)] + mat_specs,
        out_specs=[whole(longer), whole(flat)] + [hidden_spec] * 3,
        scratch=[wide] * 2,
        flops=6 * flops,
    )
    grads = exchange(after(grads, frows), "grads")
    (outs,) = call(
        forward_kernel,
        "forward",
        [message],
        [frows] + mats,
        grid=grid,
        in_specs=[whole(message)] + mat_specs,
        out_specs=[whole(message)],
        scratch=[wide],
        flops=3 * flops,
    )
    outs = exchange(after(outs, grads), "outs")
    flat_rows = rows.reshape(count, width)
    gate_wgrad = t_dot(flat_rows, gate_part).astype(BF16)
    up_wgrad = t_dot(flat_rows, up_part).astype(BF16)
    down_wgrad = t_dot(active, scaled).astype(BF16)

    grad_in, sums = call(
        partial(source_kernel, top),
        "source",
        [block, shape((-(-(experts + 1) // 8) * 8, width), F32)],
        [rank, grads, table, lifted, router_t, normed, xp, dy_in, gain_row],
        scratch=[pltpu.VMEM((count, tokens), BF16), pltpu.VMEM((experts, tokens), F32)],
    )
    step = 1
    while step < lax.axis_size("expert"):
        sums = sums + hop(sums, 0, step, "sums")
        step *= 2
    (forward,) = call(
        out_kernel,
        "out",
        [block],
        [frank, fweight, x_in, outs],
        scratch=[pltpu.VMEM((count, tokens), BF16)] * 2,
    )
    return (
        forward[None],
        grad_in[None],
        gate_wgrad[None, None],
        up_wgrad[None, None],
        down_wgrad[None, None],
        sums[:experts].T[None],
        sums[experts][None],
    )


def solution(mesh):
    rows = P("pipe", "expert", None)
    weights = P("pipe", "expert", None, None)
    shared = P("pipe", None, None)
    return jax.shard_map(
        per_device,
        mesh=mesh,
        in_specs=(rows,) * 3
        + (weights,) * 3
        + (shared, P("pipe", None), rows, rows, P("pipe", "expert"), P("pipe", "expert")),
        out_specs=(rows, rows, weights, weights, weights, shared, P("pipe", None)),
        check_vma=False,
    )
```

profile of v0, /device:TPU:0, one launch (start us, length us, event | category | flops | bytes accessed | tf_op | source)
XLA Modules:
  0.0 349.6 jit_solution(6107187699220221839)
XLA Ops:
  0.6 1.3 pad_add_fusion.table_ref.refs_3_.refs_2_
  2.0 1.6 ranks.1
  3.5 5.8 %rows.1 = (bf16[8,80,2048]{2,1,0:T(8,128)(2,1)}, f32[8,256]{1,0:T(8,128)}, bf16[256,2048]{1,0:T(8,128)(2,1)}, f32[2,256]{1,0:T(2,128)}) custom-call(bf16[256,2048]{1,0:T(8,128)(2,1)} %bitcast.42, f32[1,2048]{1,0:T(1,128)} %refs_8_.1, bf16[8,2048]{1,0:T(8,128)(2,1)} %bitcast.45, s32[6,256]{1,0:T(8,128)} %pad_add_fusion.table_ref.refs_3_.refs_2_, ...), custom_call_target="tpu_custom_call" | custom-call | bytes 74752 | tf_op jit(solution)/shard_map/rows/pallas_call | solution.py:55
  9.3 7.3 %all-to-all-start = ((bf16[8,80,2048]{2,1,0:T(8,128)(2,1)}), bf16[8,80,2048]{2,1,0:T(8,128)(2,1)S(1)}, u32[]{:S(2)}, u32[]{:S(2)}) async-start(bf16[8,80,2048]{2,1,0:T(8,128)(2,1)} %get-tuple-element.31), calls=%async_computation | async-start | bytes 5242880 | tf_op jit(solution)/shard_map/rows/all_to_all | solution.py:291
  16.5 0.7 collective-permute-start.1
  17.2 12.6 %collective-permute-done.1.x_ref.refs_7_ = bf16[256,2048]{1,0:T(8,128)(2,1)S(1)} collective-permute-done((bf16[256,2048]{1,0:T(8,128)(2,1)}, bf16[256,2048]{1,0:T(8,128)(2,1)S(1)}, u32[]{:S(2)}, u32[]{:S(2)}) %collective-permute-start.1) | collective-permute-done | bytes 1048608 | tf_op jit(solution)/shard_map/dy_in/ppermute | solution.py:28
  29.8 0.0 copy-start.5
  29.8 1.0 copy-done.5
  30.9 4.6 %cots.1 = bf16[8,80,2176]{2,1,0:T(8,128)(2,1)} custom-call(s32[8,256]{1,0:T(8,128)} %get-tuple-element.29.refs_4_.rank_ref.refs_0_, f32[8,256]{1,0:T(8,128)} %get-tuple-element.30.weight_ref, bf16[256,2048]{1,0:T(8,128)(2,1)} %copy-done.5), custom_call_target="tpu_custom_call" | custom-call | bytes 60160 | tf_op jit(solution)/shard_map/cots/pallas_call | solution.py:55
  35.4 40.6 %all-to-all-done.rows_ref = bf16[8,80,2048]{2,1,0:T(8,128)(2,1)S(1)} async-done(((bf16[8,80,2048]{2,1,0:T(8,128)(2,1)}), bf16[8,80,2048]{2,1,0:T(8,128)(2,1)S(1)}, u32[]{:S(2)}, u32[]{:S(2)}) %all-to-all-start) | async-done | bytes 2621472 | tf_op jit(solution)/shard_map/rows/all_to_all | solution.py:291
  76.0 0.0 copy-start.2
  76.0 1.5 copy-done.2
  77.5 3.6 %all-to-all-start.1 = ((bf16[8,80,2176]{2,1,0:T(8,128)(2,1)}), bf16[8,80,2176]{2,1,0:T(8,128)(2,1)S(1)}, u32[]{:S(2)}, u32[]{:S(2)}) async-start(bf16[8,80,2176]{2,1,0:T(8,128)(2,1)} %cots.1), calls=%async_computation.1 | async-start | bytes 5570560 | tf_op jit(solution)/shard_map/cots/all_to_all | solution.py:291
  81.2 0.1 collective-permute-start
  81.2 14.4 %collective-permute-done.refs_0_.x_ref = bf16[256,2048]{1,0:T(8,128)(2,1)S(1)} collective-permute-done((bf16[256,2048]{1,0:T(8,128)(2,1)}, bf16[256,2048]{1,0:T(8,128)(2,1)S(1)}, u32[]{:S(2)}, u32[]{:S(2)}) %collective-permute-start) | collective-permute-done | bytes 1048608 | tf_op jit(solution)/shard_map/x_in/ppermute | solution.py:28
  95.6 0.0 copy-start.4
  95.7 1.0 copy-done.4
  96.6 5.4 %frows.1 = (bf16[8,80,2048]{2,1,0:T(8,128)(2,1)}, f32[8,256]{1,0:T(8,128)}) custom-call(bf16[256,2048]{1,0:T(8,128)(2,1)} %copy-done.4, f32[1,2048]{1,0:T(1,128)} %refs_8_.1, bf16[8,2048]{1,0:T(8,128)(2,1)} %bitcast.46, s32[6,256]{1,0:T(8,128)} %pad_add_fusion.table_ref.refs_3_.refs_2_, s32[8,256]{1,0:T(8,128)} %get-tuple-element.26.refs_4_.rank_ref), custom_call_target="tpu_custom_call" | custom-call | bytes 58336 | tf_op jit(solution)/shard_map/frows/pallas_call | solution.py:55
  102.0 42.3 %all-to-all-done.1.cot_ref = bf16[8,80,2176]{2,1,0:T(8,128)(2,1)S(1)} async-done(((bf16[8,80,2176]{2,1,0:T(8,128)(2,1)}), bf16[8,80,2176]{2,1,0:T(8,128)(2,1)S(1)}, u32[]{:S(2)}, u32[]{:S(2)}) %all-to-all-start.1) | async-done | bytes 2785312 | tf_op jit(solution)/shard_map/cots/all_to_all | solution.py:291
  144.3 0.0 copy-start
  144.3 4.6 %all-to-all-start.2 = ((bf16[8,80,2048]{2,1,0:T(8,128)(2,1)}), bf16[8,80,2048]{2,1,0:T(8,128)(2,1)}, u32[]{:S(2)}, u32[]{:S(2)}) async-start(bf16[8,80,2048]{2,1,0:T(8,128)(2,1)} %get-tuple-element.33), calls=%async_computation.2 | async-start | bytes 5242880 | tf_op jit(solution)/shard_map/frows/all_to_all | solution.py:291
  148.9 0.0 copy-done
  148.9 32.3 %expert.1 = (bf16[8,80,2176]{2,1,0:T(8,128)(2,1)}, bf16[640,2048]{1,0:T(8,128)(2,1)}, bf16[640,768]{1,0:T(8,128)(2,1)}, bf16[640,768]{1,0:T(8,128)(2,1)}, bf16[640,768]{1,0:T(8,128)(2,1)}) custom-call(bf16[8,80,2048]{2,1,0:T(8,128)(2,1)} %copy-done.2, bf16[8,80,2176]{2,1,0:T(8,128)(2,1)} %copy-done, bf16[2048,768]{1,0:T(8,128)(2,1)} %bitcast.34, ...), custom_call_target="tpu_custom_call" | custom-call | flops 188743680 | bytes 362496 | tf_op jit(solution)/shard_map/expert/pallas_call | solution.py:55
  181.3 26.5 %all-to-all-done.2.rows_ref = bf16[8,80,2048]{2,1,0:T(8,128)(2,1)} async-done(((bf16[8,80,2048]{2,1,0:T(8,128)(2,1)}), bf16[8,80,2048]{2,1,0:T(8,128)(2,1)}, u32[]{:S(2)}, u32[]{:S(2)}) %all-to-all-start.2) | async-done | bytes 2621472 | tf_op jit(solution)/shard_map/frows/all_to_all | solution.py:291
  207.8 3.6 %all-to-all-start.3 = ((bf16[8,80,2176]{2,1,0:T(8,128)(2,1)}), bf16[8,80,2176]{2,1,0:T(8,128)(2,1)S(1)}, u32[]{:S(2)}, u32[]{:S(2)}) async-start(bf16[8,80,2176]{2,1,0:T(8,128)(2,1)} %get-tuple-element.35), calls=%async_computation.3 | async-start | bytes 5570560 | tf_op jit(solution)/shard_map/grads/all_to_all | solution.py:291
  211.4 12.9 %forward.1 = bf16[8,80,2048]{2,1,0:T(8,128)(2,1)} custom-call(bf16[8,80,2048]{2,1,0:T(8,128)(2,1)} %all-to-all-done.2.rows_ref, bf16[2048,768]{1,0:T(8,128)(2,1)} %bitcast.35, bf16[2048,768]{1,0:T(8,128)(2,1)} %bitcast.37, bf16[768,2048]{1,0:T(8,128)(2,1)} %bitcast.39), custom_call_target="tpu_custom_call" | custom-call | flops 94371840 | bytes 229376 | tf_op jit(solution)/shard_map/forward/pallas_call | solution.py:55
  224.3 50.2 %all-to-all-done.3.refs_1_ = bf16[8,80,2176]{2,1,0:T(8,128)(2,1)S(1)} async-done(((bf16[8,80,2176]{2,1,0:T(8,128)(2,1)}), bf16[8,80,2176]{2,1,0:T(8,128)(2,1)S(1)}, u32[]{:S(2)}, u32[]{:S(2)}) %all-to-all-start.3) | async-done | bytes 2785312 | tf_op jit(solution)/shard_map/grads/all_to_all | solution.py:291
  274.5 0.0 copy-start.1
  274.5 4.6 %all-to-all-start.4 = ((bf16[8,80,2048]{2,1,0:T(8,128)(2,1)}), bf16[8,80,2048]{2,1,0:T(8,128)(2,1)}, u32[]{:S(2)}, u32[]{:S(2)}) async-start(bf16[8,80,2048]{2,1,0:T(8,128)(2,1)} %forward.1), calls=%async_computation.4 | async-start | bytes 5242880 | tf_op jit(solution)/shard_map/outs/all_to_all | solution.py:291
  279.2 0.0 copy-done.1
  279.2 0.0 copy-start.3
  279.2 0.0 copy-start.10
  279.2 8.3 %source.1 = (bf16[256,2048]{1,0:T(8,128)(2,1)}, f32[16,2048]{1,0:T(8,128)}) custom-call(s32[8,256]{1,0:T(8,128)} %get-tuple-element.29.refs_4_.rank_ref.refs_0_, bf16[8,80,2176]{2,1,0:T(8,128)(2,1)} %copy-done.1, s32[6,256]{1,0:T(8,128)} %pad_add_fusion.table_ref.refs_3_.refs_2_, f32[2,256]{1,0:T(2,128)} %get-tuple-element.37.refs_3_, ...), custom_call_target="tpu_custom_call" | custom-call | bytes 112000 | tf_op jit(solution)/shard_map/source/pallas_call | solution.py:55
  287.5 1.7 collective-permute-start.2
  289.2 0.0 copy-done.3
  289.2 0.0 copy-done.10
  289.2 0.0 copy-start.6
  289.2 0.0 copy-start.9
  289.2 4.0 %fusion.1 = bf16[1,1,2048,768]{3,2,1,0:T(8,128)(2,1)} fusion(bf16[640,2048]{1,0:T(8,128)(2,1)S(1)} %bitcast.40, bf16[640,768]{1,0:T(8,128)(2,1)S(1)} %copy-done.10), kind=kOutput, calls=%fused_computation.4 | convolution fusion | flops 2014838784 | bytes 6750208 | tf_op jit(solution)/shard_map/dot_general | solution.py:45
  293.2 10.6 %collective-permute-done.2 = f32[16,2048]{1,0:T(8,128)S(1)} collective-permute-done((f32[16,2048]{1,0:T(8,128)}, f32[16,2048]{1,0:T(8,128)S(1)}, u32[]{:S(2)}, u32[]{:S(2)}) %collective-permute-start.2) | collective-permute-done | bytes 131104 | tf_op jit(solution)/shard_map/sums/ppermute | solution.py:22
  303.8 0.0 copy-done.6
  303.8 0.5 collective-permute-start.3
  304.3 0.0 copy-done.9
  304.3 0.0 copy-start.7
  304.3 0.0 copy-start.8
  304.3 4.1 %fusion = bf16[1,1,2048,768]{3,2,1,0:T(8,128)(2,1)} fusion(bf16[640,2048]{1,0:T(8,128)(2,1)S(1)} %bitcast.41, bf16[640,768]{1,0:T(8,128)(2,1)S(1)} %copy-done.9), kind=kOutput, calls=%fused_computation.3 | convolution fusion | flops 2014838784 | bytes 6750208 | tf_op jit(solution)/shard_map/dot_general | solution.py:45
  308.4 15.9 %collective-permute-done.3 = f32[16,2048]{1,0:T(8,128)S(1)} collective-permute-done((f32[16,2048]{1,0:T(8,128)S(1)}, f32[16,2048]{1,0:T(8,128)S(1)}, u32[]{:S(2)}, u32[]{:S(2)}) %collective-permute-start.3) | collective-permute-done | bytes 131104 | tf_op jit(solution)/shard_map/sums/ppermute | solution.py:22
  324.3 3.9 %collective-permute-start.4 = (f32[16,2048]{1,0:T(8,128)S(1)}, f32[16,2048]{1,0:T(8,128)S(1)}, u32[]{:S(2)}, u32[]{:S(2)}) collective-permute-start(f32[16,2048]{1,0:T(8,128)S(1)} %add.10), channel_id=1, source_target_pairs={{0,4},{1,5},{2,6},{3,7},{4,0},{5,1},{6,2},{7,3},{8,12},{9,13},{10,... | collective-permute-start | bytes 393224 | tf_op jit(solution)/shard_map/sums/ppermute | solution.py:22
  328.2 0.0 copy-done.7
  328.2 0.0 copy-done.8
  328.2 4.0 %fusion.2 = bf16[1,1,768,2048]{3,2,1,0:T(8,128)(2,1)} fusion(bf16[640,768]{1,0:T(8,128)(2,1)S(1)} %copy-done.8, bf16[640,2048]{1,0:T(8,128)(2,1)S(1)} %copy-done.7), kind=kOutput, calls=%fused_computation.5 | convolution fusion | flops 2014838784 | bytes 6750208 | tf_op jit(solution)/shard_map/dot_general | solution.py:45
  332.3 11.2 %collective-permute-done.4 = f32[16,2048]{1,0:T(8,128)S(1)} collective-permute-done((f32[16,2048]{1,0:T(8,128)S(1)}, f32[16,2048]{1,0:T(8,128)S(1)}, u32[]{:S(2)}, u32[]{:S(2)}) %collective-permute-start.4) | collective-permute-done | bytes 131104 | tf_op jit(solution)/shard_map/sums/ppermute | solution.py:22
  343.5 0.6 slice.9
  344.1 0.6 slice_bitcast_fusion
  344.7 0.0 all-to-all-done.4.rows_ref
  344.7 4.9 %out.1 = bf16[256,2048]{1,0:T(8,128)(2,1)} custom-call(s32[8,256]{1,0:T(8,128)} %get-tuple-element.26.refs_4_.rank_ref, f32[8,256]{1,0:T(8,128)} %get-tuple-element.27.weight_ref, bf16[256,2048]{1,0:T(8,128)(2,1)} %copy-done.4, bf16[8,80,2048]{2,1,0:T(8,128)(2,1)} %all-to-all-done.4.rows_ref), custom_call_target="tpu_custom_call" | custom-call | bytes 73984 | tf_op jit(solution)/shard_map/out/pallas_call | solution.py:55
  (3 shorter events, 0.0 us)
Async XLA Ops:
  9.3 66.7 %all-to-all-start = ((bf16[8,80,2048]{2,1,0:T(8,128)(2,1)}), bf16[8,80,2048]{2,1,0:T(8,128)(2,1)S(1)}, u32[]{:S(2)}, u32[]{:S(2)}) async-start(bf16[8,80,2048]{2,1,0:T(8,128)(2,1)} %get-tuple-element.31), calls=%async_computation | async-start | bytes 5242880 | tf_op jit(solution)/shard_map/rows/all_to_all | solution.py:291
  16.5 13.3 %collective-permute-start.1 = (bf16[256,2048]{1,0:T(8,128)(2,1)}, bf16[256,2048]{1,0:T(8,128)(2,1)S(1)}, u32[]{:S(2)}, u32[]{:S(2)}) collective-permute-start(bf16[256,2048]{1,0:T(8,128)(2,1)} %bitcast.50), channel_id=1, source_target_pairs={{0,24},{1,25},{2,26},{3,27},{4,28},{5,29},{6,30},{7,31},{8,0},{9,1... | collective-permute-start | bytes 3145736 | tf_op jit(solution)/shard_map/dy_in/ppermute | solution.py:28
  29.8 1.0 copy-start.5
  76.0 1.5 copy-start.2
  77.5 66.8 %all-to-all-start.1 = ((bf16[8,80,2176]{2,1,0:T(8,128)(2,1)}), bf16[8,80,2176]{2,1,0:T(8,128)(2,1)S(1)}, u32[]{:S(2)}, u32[]{:S(2)}) async-start(bf16[8,80,2176]{2,1,0:T(8,128)(2,1)} %cots.1), calls=%async_computation.1 | async-start | bytes 5570560 | tf_op jit(solution)/shard_map/cots/all_to_all | solution.py:291
  81.2 14.5 %collective-permute-start = (bf16[256,2048]{1,0:T(8,128)(2,1)}, bf16[256,2048]{1,0:T(8,128)(2,1)S(1)}, u32[]{:S(2)}, u32[]{:S(2)}) collective-permute-start(bf16[256,2048]{1,0:T(8,128)(2,1)} %bitcast.51), channel_id=1, source_target_pairs={{0,8},{1,9},{2,10},{3,11},{4,12},{5,13},{6,14},{7,15},{8,16},{9,17... | collective-permute-start | bytes 3145736 | tf_op jit(solution)/shard_map/x_in/ppermute | solution.py:28
  95.6 1.0 copy-start.4
  144.3 4.6 %copy-start = (bf16[8,80,2176]{2,1,0:T(8,128)(2,1)}, bf16[8,80,2176]{2,1,0:T(8,128)(2,1)S(1)}, u32[]{:S(2)}) copy-start(bf16[8,80,2176]{2,1,0:T(8,128)(2,1)S(1)} %all-to-all-done.1.cot_ref) | copy-start | bytes 8355844
  144.3 63.5 %all-to-all-start.2 = ((bf16[8,80,2048]{2,1,0:T(8,128)(2,1)}), bf16[8,80,2048]{2,1,0:T(8,128)(2,1)}, u32[]{:S(2)}, u32[]{:S(2)}) async-start(bf16[8,80,2048]{2,1,0:T(8,128)(2,1)} %get-tuple-element.33), calls=%async_computation.2 | async-start | bytes 5242880 | tf_op jit(solution)/shard_map/frows/all_to_all | solution.py:291
  207.8 66.7 %all-to-all-start.3 = ((bf16[8,80,2176]{2,1,0:T(8,128)(2,1)}), bf16[8,80,2176]{2,1,0:T(8,128)(2,1)S(1)}, u32[]{:S(2)}, u32[]{:S(2)}) async-start(bf16[8,80,2176]{2,1,0:T(8,128)(2,1)} %get-tuple-element.35), calls=%async_computation.3 | async-start | bytes 5570560 | tf_op jit(solution)/shard_map/grads/all_to_all | solution.py:291
  274.5 4.6 %copy-start.1 = (bf16[8,80,2176]{2,1,0:T(8,128)(2,1)}, bf16[8,80,2176]{2,1,0:T(8,128)(2,1)S(1)}, u32[]{:S(2)}) copy-start(bf16[8,80,2176]{2,1,0:T(8,128)(2,1)S(1)} %all-to-all-done.3.refs_1_) | copy-start | bytes 8355844
  274.5 70.2 %all-to-all-start.4 = ((bf16[8,80,2048]{2,1,0:T(8,128)(2,1)}), bf16[8,80,2048]{2,1,0:T(8,128)(2,1)}, u32[]{:S(2)}, u32[]{:S(2)}) async-start(bf16[8,80,2048]{2,1,0:T(8,128)(2,1)} %forward.1), calls=%async_computation.4 | async-start | bytes 5242880 | tf_op jit(solution)/shard_map/outs/all_to_all | solution.py:291
  279.2 10.0 %copy-start.3 = (bf16[8,80,2048]{2,1,0:T(8,128)(2,1)S(1)}, bf16[8,80,2048]{2,1,0:T(8,128)(2,1)}, u32[]{:S(2)}) copy-start(bf16[8,80,2048]{2,1,0:T(8,128)(2,1)} %copy-done.2) | copy-start | bytes 7864324
  279.2 10.0 %copy-start.10 = (bf16[640,768]{1,0:T(8,128)(2,1)S(1)}, bf16[640,768]{1,0:T(8,128)(2,1)}, u32[]{:S(2)}) copy-start(bf16[640,768]{1,0:T(8,128)(2,1)} %get-tuple-element.41) | copy-start | bytes 2949124
  287.5 16.3 %collective-permute-start.2 = (f32[16,2048]{1,0:T(8,128)}, f32[16,2048]{1,0:T(8,128)S(1)}, u32[]{:S(2)}, u32[]{:S(2)}) collective-permute-start(f32[16,2048]{1,0:T(8,128)} %get-tuple-element.44), channel_id=1, source_target_pairs={{0,1},{1,0},{2,3},{3,2},{4,5},{5,4},{6,7},{7,6},{8,9},{9,8},{10,11... | collective-permute-start | bytes 393224 | tf_op jit(solution)/shard_map/sums/ppermute | solution.py:22
  289.2 14.6 %copy-start.6 = (f32[16,2048]{1,0:T(8,128)S(1)}, f32[16,2048]{1,0:T(8,128)}, u32[]{:S(2)}) copy-start(f32[16,2048]{1,0:T(8,128)} %get-tuple-element.44) | copy-start | bytes 393220
  289.2 15.1 %copy-start.9 = (bf16[640,768]{1,0:T(8,128)(2,1)S(1)}, bf16[640,768]{1,0:T(8,128)(2,1)}, u32[]{:S(2)}) copy-start(bf16[640,768]{1,0:T(8,128)(2,1)} %get-tuple-element.40) | copy-start | bytes 2949124
  303.8 20.5 %collective-permute-start.3 = (f32[16,2048]{1,0:T(8,128)S(1)}, f32[16,2048]{1,0:T(8,128)S(1)}, u32[]{:S(2)}, u32[]{:S(2)}) collective-permute-start(f32[16,2048]{1,0:T(8,128)S(1)} %add.9), channel_id=1, source_target_pairs={{0,2},{1,3},{2,0},{3,1},{4,6},{5,7},{6,4},{7,5},{8,10},{9,11},{10,... | collective-permute-start | bytes 393224 | tf_op jit(solution)/shard_map/sums/ppermute | solution.py:22
  304.3 23.9 %copy-start.7 = (bf16[640,2048]{1,0:T(8,128)(2,1)S(1)}, bf16[640,2048]{1,0:T(8,128)(2,1)}, u32[]{:S(2)}) copy-start(bf16[640,2048]{1,0:T(8,128)(2,1)} %get-tuple-element.43) | copy-start | bytes 7864324
  304.3 23.9 %copy-start.8 = (bf16[640,768]{1,0:T(8,128)(2,1)S(1)}, bf16[640,768]{1,0:T(8,128)(2,1)}, u32[]{:S(2)}) copy-start(bf16[640,768]{1,0:T(8,128)(2,1)} %get-tuple-element.42) | copy-start | bytes 2949124
  324.3 19.2 %collective-permute-start.4 = (f32[16,2048]{1,0:T(8,128)S(1)}, f32[16,2048]{1,0:T(8,128)S(1)}, u32[]{:S(2)}, u32[]{:S(2)}) collective-permute-start(f32[16,2048]{1,0:T(8,128)S(1)} %add.10), channel_id=1, source_target_pairs={{0,4},{1,5},{2,6},{3,7},{4,0},{5,1},{6,2},{7,3},{8,12},{9,13},{10,... | collective-permute-start | bytes 393224 | tf_op jit(solution)/shard_map/sums/ppermute | solution.py:22
where the time goes:
time: 350 us
  waiting for transfers between devices  224 us (64%)
  Pallas kernels  75.6 us (22%)
  starting transfers between devices  30.6 us (9%)
  matrix products  12.1 us (3%)
  local copies, waits for them, and re-layouts  4.78 us (1%)
    all_to_all x5, waiting for transfers between devices, exchange(): return lax.all_to_all(array, 'expert', 0, 0, tiled=True)  160 us
    pallas_call x8, Pallas kernels, call(): pl.pallas_call(kernel, out_shape=[jax.ShapeDtypeStruct(o.shape, o.dtype)...  75.6 us
    ppermute x3, waiting for transfers between devices, hop(): lax.ppermute(block, 'expert', [(e, e ^ flip) for e in range(experts)])  37.7 us
    ppermute x2, waiting for transfers between devices, hop(): return lax.ppermute(block, ('pipe', 'expert'), route)  27.1 us
    all_to_all x5, starting transfers between devices, exchange(): return lax.all_to_all(array, 'expert', 0, 0, tiled=True)  23.7 us
    dot_general x3, matrix products, t_dot(): lax.dot_general(a, b, dims, preferred_element_type=F32, precision=precision)  12.1 us
  transfers between devices with their start and end apart: 10, of which 9 were waited for; matrix products, arithmetic and copies ran while one was open for 4% of the time, Pallas kernels for 18%

commit v1 on v0

--- a/solution.py
+++ b/solution.py
@@ -122,104 +122,130 @@
     weight_ref[...] = weight
 
 
-def put_rows(rank_ref, block_ref, message_ref):
+def put_pieces(me_ref, rank_ref, block_ref, weight_ref, pieces):
+    width = block_ref.shape[1]
+    for k, piece in enumerate(pieces):
+        expert = pl.ds(me_ref[0] ^ k, 1)
+        rank = rank_ref[expert, :]
+        hot = one_hot(iota((piece.shape[0], rank.shape[1]), 0) == rank)
+        piece[:, :width] = dot(hot, block_ref[...]).astype(BF16)
+        if weight_ref is not None:
+            weight = weight_ref[expert, :].astype(BF16)
+            weight = jnp.broadcast_to(weight, (LANES, weight.shape[1]))
+            piece[:, width:] = dot_t(hot, weight).astype(BF16)
+
+
+def own_kernel(half, batch, top, *refs):
+    me_ref, x_ref, gain_ref, router_ref, table_ref, rank_ref = refs[:6]
+    pieces, (weight_ref, normed_ref, lifted_ref) = refs[6 : 6 + half], (*refs[6 + half :], None)[:3]
+    normalise(x_ref, gain_ref, normed_ref)
+    gates(normed_ref, router_ref, route_rows(table_ref, batch, top), lifted_ref, weight_ref)
+    put_pieces(me_ref, rank_ref, normed_ref, weight_ref if batch else None, pieces)
+
+
+def far_kernel(half, batch, top, *refs):
+    me_ref, x_ref, gain_ref, router_ref, table_ref, rank_ref = refs[:6]
+    pieces, (normed_ref, weight_ref) = refs[6 : 6 + half], refs[6 + half :]
+    normalise(x_ref, gain_ref, normed_ref)
+    if batch:
+        gates(normed_ref, router_ref, route_rows(table_ref, batch, top), None, weight_ref)
+    put_pieces(me_ref, rank_ref, normed_ref, weight_ref if batch else None, pieces)
+
+
+def rows_kernel(top, *refs):
+    x_ref, gain_ref, router_ref, table_ref, rank_ref, message_ref, weight_ref, normed_ref = refs
+    normalise(x_ref, gain_ref, normed_ref)
+    cots_kernel(rank_ref, normed_ref, message_ref)
+    gates(normed_ref, router_ref, route_rows(table_ref, 0, top), None, weight_ref)
+
+
+def cots_kernel(rank_ref, x_ref, message_ref):
     for e in range(message_ref.shape[0]):
         hot = one_hot(slot_mask(rank_ref, e, message_ref.shape[1]))
-        message_ref[e] = dot(hot, block_ref[...]).astype(BF16)
-
-
-def rows_kernel(batch, top, *refs):
-    x_ref, gain_ref, router_ref, table_ref, rank_ref = refs[:5]
-    message_ref, weight_ref, normed_ref, lifted_ref = (*refs[5:], None)[:4]
-    normalise(x_ref, gain_ref, normed_ref)
-    put_rows(rank_ref, normed_ref, message_ref)
-    gates(normed_ref, router_ref, route_rows(table_ref, batch, top), lifted_ref, weight_ref)
-
-
-def cots_kernel(rank_ref, weight_ref, x_ref, message_ref):
-    width = x_ref.shape[1]
-    for e in range(message_ref.shape[0]):
-        hot = one_hot(slot_mask(rank_ref, e, message_ref.shape[1]))
-        message_ref[e, :, :width] = dot(hot, x_ref[...]).astype(BF16)
-        weight = weight_ref[e : e + 1, :].astype(BF16)
-        weight = jnp.broadcast_to(weight, (LANES, weight.shape[1]))
-        message_ref[e, :, width:] = dot_t(hot, weight).astype(BF16)
+        message_ref[e] = dot(hot, x_ref[...]).astype(BF16)
 
 
 def flat_of(ref):
     return ref[...].reshape(-1, ref.shape[-1])
 
 
-def add(acc, value):
+def each_sender(me_ref, count, slots):
+    for k in range(count):
+        sender = me_ref[0] ^ k
+        yield k, sender, pl.ds(pl.multiple_of(sender * slots, 16), slots)
+
+
+def expert_kernel(steps, half, *refs):
+    me_ref, gate_a, up_a, down_a, gate_b, up_b, down_b, cot_ref = refs[:8]
+    pieces, refs = refs[8 : 8 + 2 * half], refs[8 + 2 * half :]
+    message_ref, rows_ref, scaled_ref, active_ref, gate_part_ref, up_part_ref, inner_ref = refs
+    slots = pieces[0].shape[0]
+    width = rows_ref.shape[1]
     step = pl.program_id(0)
 
     @pl.when(step == 0)
     def _():
-        acc[...] = value
-
-    @pl.when(step > 0)
-    def _():
-        acc[...] += value
-
-
-def expert_kernel(rows_ref, cot_ref, gate_w, up_w, down_w, *refs):
-    message_ref, scaled_ref, active_ref, gate_part_ref, up_part_ref, acc_out, acc_grad = refs
-    senders, slots, width = rows_ref.shape
-
-    @pl.when(pl.program_id(0) == 0)
-    def _():
-        for k in range(senders):
-            scale = cot_ref[k, :, width:].astype(F32)[:, :1]
-            scaled = (scale * cot_ref[k, :, :width].astype(F32)).astype(BF16)
-            scaled_ref[k * slots : (k + 1) * slots, :] = scaled
-
-    rows = flat_of(rows_ref)
-    gate = dot(rows, gate_w[...])
-    upper = dot(rows, up_w[...])
-    sig = jax.nn.sigmoid(gate)
-    active = (gate * sig * upper).astype(BF16)
-    active_ref[...] = active
-    act_grad = dot_t(scaled_ref[...], down_w[...])
-    gate_part = (act_grad * upper * sig * (1.0 + gate * (1.0 - sig))).astype(BF16)
-    up_part = (act_grad * (gate * sig)).astype(BF16)
-    gate_part_ref[...] = gate_part
-    up_part_ref[...] = up_part
-    add(acc_grad, dot_t(gate_part, gate_w[...]) + dot_t(up_part, up_w[...]))
-    add(acc_out, dot(active, down_w[...]))
-
-    @pl.when(pl.program_id(0) == pl.num_programs(0) - 1)
-    def _():
-        for k in range(senders):
-            part = slice(k * slots, (k + 1) * slots)
-            message_ref[k, :, :width] = acc_grad[part, :].astype(BF16)
-            result = acc_out[part, :].astype(BF16).astype(F32)
-            cot = cot_ref[k, :, :width].astype(F32)
-            inner = jnp.sum(cot * result, axis=1, keepdims=True).astype(BF16)
-            message_ref[k, :, width:] = jnp.broadcast_to(inner, (slots, LANES))
-
-
-def forward_kernel(rows_ref, gate_w, up_w, down_w, out_ref, acc):
-    rows = flat_of(rows_ref)
-    gate = dot(rows, gate_w[...])
-    active = (gate * jax.nn.sigmoid(gate) * dot(rows, up_w[...])).astype(BF16)
-    add(acc, dot(active, down_w[...]))
-
-    @pl.when(pl.program_id(0) == pl.num_programs(0) - 1)
-    def _():
-        out_ref[...] = acc[...].astype(BF16).reshape(out_ref.shape)
-
-
-def out_kernel(rank_ref, weight_ref, x_ref, rows_ref, out_ref, high_ref, low_ref):
-    slots = rows_ref.shape[1]
+        for k, sender, part in each_sender(me_ref, 2 * half, slots):
+            rows_ref[part, :] = pieces[k][:, :width]
+            scale = pieces[k][:, width:].astype(F32)[:, :1]
+            scaled_ref[part, :] = (scale * cot_ref[sender].astype(F32)).astype(BF16)
+        inner_ref[...] = jnp.zeros_like(inner_ref)
+
+    @pl.when(step < steps)
+    def _():
+        gate = dot(rows_ref[...], gate_a[...])
+        upper = dot(rows_ref[...], up_a[...])
+        sig = jax.nn.sigmoid(gate)
+        act_grad = dot_t(scaled_ref[...], down_a[...])
+        active_ref[step] = (gate * sig * upper).astype(BF16)
+        gate_part_ref[step] = (act_grad * upper * sig * (1.0 + gate * (1.0 - sig))).astype(BF16)
+        up_part_ref[step] = (act_grad * (gate * sig)).astype(BF16)
+
+    @pl.when(step >= steps)
+    def _():
+        part = gate_a.shape[1]
+        columns = pl.ds(pl.multiple_of((step - steps) * gate_b.shape[0], 128), gate_b.shape[0])
+        total = jnp.zeros((rows_ref.shape[0], gate_b.shape[0]), F32)
+        result = total
+        for f in range(steps):
+            hidden = slice(f * part, (f + 1) * part)
+            total = total + dot_t(gate_part_ref[f], gate_b[:, hidden])
+            total = total + dot_t(up_part_ref[f], up_b[:, hidden])
+            result = result + dot(active_ref[f], down_b[hidden, :])
+        message_ref[:, columns] = total.astype(BF16)
+        cot = cot_ref[:, :, columns].reshape(total.shape).astype(F32)
+        result = result.astype(BF16).astype(F32)
+        inner_ref[...] += jnp.sum(cot * result, axis=1, keepdims=True)
+
+    @pl.when(step == pl.num_programs(0) - 1)
+    def _():
+        inner = inner_ref[...].astype(BF16)
+        message_ref[:, width:] = jnp.broadcast_to(inner, (inner.shape[0], LANES))
+
+
+def forward_kernel(steps, rows_ref, gate_a, up_a, down_b, out_ref, active_ref):
+    step = pl.program_id(0)
+
+    @pl.when(step < steps)
+    def _():
+        rows = flat_of(rows_ref)
+        gate = dot(rows, gate_a[...])
+        active_ref[step] = (gate * jax.nn.sigmoid(gate) * dot(rows, up_a[...])).astype(BF16)
+
+    @pl.when(step >= steps)
+    def _():
+        part = gate_a.shape[1]
+        result = jnp.zeros(active_ref.shape[1:2] + down_b.shape[1:], F32)
+        for f in range(steps):
+            result = result + dot(active_ref[f], down_b[f * part : (f + 1) * part, :])
+        out_ref[...] = result.astype(BF16).reshape(out_ref.shape)
+
+
+def spread_kernel(slots, rank_ref, weight_ref, spread_ref, flat_ref):
     for e in range(rank_ref.shape[0]):
-        part = slice(e * slots, (e + 1) * slots)
-        value = jnp.where(slot_mask(rank_ref, e, slots), weight_ref[e : e + 1, :], 0.0)
-        high = value.astype(BF16)
-        high_ref[part, :] = high
-        low_ref[part, :] = (value - high.astype(F32)).astype(BF16)
-    rows = flat_of(rows_ref)
-    total = t_dot(high_ref[...], rows) + t_dot(low_ref[...], rows)
-    out_ref[...] = (x_ref[...].astype(F32) + total).astype(BF16)
+        mask = slot_mask(rank_ref, e, slots)
+        flat_ref[e * slots : (e + 1) * slots, :] = jnp.where(mask, weight_ref[e : e + 1, :], 0.0)
+    spread_ref[...] = flat_ref[...].T.astype(BF16)
 
 
 def source_kernel(top, *refs):
@@ -284,100 +310,147 @@
     gain_row, router_t = (gain, router[0].T)
     partial = functools.partial
     block, message = shape((tokens, width)), shape((experts, slots, width))
-    per_token, longer = shape((experts, tokens), F32), shape((experts, slots, width + LANES))
-
-    def exchange(array, name):
+    per_token = shape((experts, tokens), F32)
+
+    def exchange(array, name, groups=None):
         with jax.named_scope(name):
-            return lax.all_to_all(array, "expert", 0, 0, tiled=True)
-
+            return lax.all_to_all(array, "expert", 0, 0, tiled=True, axis_index_groups=groups)
+
+    def swap(pieces, name):
+        return [piece if k == 0 else hop(piece, 0, k, name) for k, piece in enumerate(pieces)]
+
+    half = lax.axis_size("expert") // 2
+    me = lax.axis_index("expert").astype(jnp.int32).reshape(1)
+    smem, vmem = pl.BlockSpec(memory_space=pltpu.SMEM), pl.BlockSpec(memory_space=pltpu.VMEM)
+    xp = prev_input[0]
+    xp_far = hop(xp, 0, half, "xp_far")
     dy_in = hop(next_cot[0], -1, 0, "dy_in")
     x_in = hop(next_input[0], 1, 0, "x_in")
-    xp = prev_input[0]
     table = jnp.concatenate(
         [next_routes[0].T, prev_routes[0].T, next_priority, prev_priority], axis=0
     )
-    frank, rank = call(
-        partial(rank_kernel, capacity, top), "ranks", [shape((experts, tokens), jnp.int32)] * 2, [table]
-    )
-    rows, weight, normed, lifted = call(
-        partial(rows_kernel, 1, top),
-        "rows",
-        [message, per_token, block, shape((top, tokens), F32)],
-        [xp, gain_row, router_t, table, rank],
-    )
-    rows = exchange(rows, "rows")
-    (cots,) = call(cots_kernel, "cots", [longer], [rank, weight, dy_in])
-    cots = exchange(after(cots, rows), "cots")
+    far_table = hop(table, 0, half, "tables")
+
+    def ranks(table, name):
+        dims = shape((experts, tokens), jnp.int32)
+        return call(partial(rank_kernel, capacity, top), name, [dims] * 2, [table])
+
+    frank, rank = ranks(table, "ranks")
+    piece, normed_scratch = shape((slots, width)), pltpu.VMEM((tokens, width), BF16)
+    frank_far, rank_far = ranks(far_table, "far_ranks")
+    longer_piece = shape((slots, width + LANES))
+
+    def own_rows(x, batch, rank, name):
+        extra = [per_token] + [block, shape((top, tokens), F32)] * batch
+        outs = call(
+            partial(own_kernel, half, batch, top),
+            name,
+            [longer_piece if batch else piece] * half + extra,
+            [me, x, gain_row, router_t, table, rank],
+            in_specs=[smem] + [vmem] * 5,
+            scratch=[] if batch else [normed_scratch],
+        )
+        return swap(outs[:half], name), *outs[half:]
+
+    def far_rows(x, batch, rank, name):
+        outs = call(
+            partial(far_kernel, half, batch, top),
+            name,
+            [longer_piece if batch else piece] * half,
+            [me, x, gain_row, router_t, far_table, rank],
+            in_specs=[smem] + [vmem] * 5,
+            scratch=[normed_scratch, pltpu.VMEM((experts, tokens), F32)],
+        )
+        return swap(outs, name)
+
+    own, _, normed, lifted = own_rows(xp, 1, rank, "own_rows")
+    (cots,) = call(cots_kernel, "cots", [message], [rank, dy_in])
+    cots = exchange(after(cots, xp_far, far_table, *own[1:]), "cots")
+    far = far_rows(xp_far, 1, rank_far, "far_rows")
     frows, fweight = call(
-        partial(rows_kernel, 0, top),
+        partial(rows_kernel, top),
         "frows",
         [message, per_token],
         [x_in, gain_row, router_t, table, frank],
-        scratch=[pltpu.VMEM((tokens, width), BF16)],
-    )
-    frows = exchange(after(frows, cots), "frows")
-
+        scratch=[normed_scratch],
+    )
+    frows = exchange(after(frows, cots, *far[1:]), "frows")
+
+    count = experts * slots
     part = 256 if hidden % 256 == 0 else hidden
-    grid = (hidden // part,)
-    across = pl.BlockSpec((width, part), lambda f: (0, f))
-    mat_specs = [across, across, pl.BlockSpec((part, width), lambda f: (f, 0))]
-    count = experts * slots
+    columns = 512 if width % 512 == 0 else width
+    steps = hidden // part
+    grid = (steps + width // columns,)
+
+    def whole(dims):
+        return pl.BlockSpec(dims.shape, lambda i: (0,) * len(dims.shape), pipeline_mode=pl.Buffered(1))
+
+    def early(i):
+        return jnp.minimum(i, steps - 1)
+
+    def late(i):
+        return jnp.maximum(i - steps, 0)
+
+    across_a = pl.BlockSpec((width, part), lambda i: (0, early(i)))
+    down_a = pl.BlockSpec((part, width), lambda i: (early(i), 0))
+    across_b = pl.BlockSpec((columns, hidden), lambda i: (late(i), 0))
+    down_b = pl.BlockSpec((hidden, columns), lambda i: (0, late(i)))
     flops = 2 * count * width * hidden
-
-    def whole(array):
-        dims = array.shape
-        return pl.BlockSpec(dims, lambda f: (0,) * len(dims), pipeline_mode=pl.Buffered(1))
-
-    hidden_spec = pl.BlockSpec((count, part), lambda f: (0, f))
-    wide = pltpu.VMEM((count, width), F32)
-    flat = shape((count, width))
-    grads, scaled, active, gate_part, up_part = call(
-        expert_kernel,
+    flat, hidden_shape = shape((count, width)), shape((steps, count, part))
+    flat_longer = shape((count, width + LANES))
+    grads, flat_rows, scaled, *parts = call(
+        partial(expert_kernel, steps, half),
         "expert",
-        [longer, flat] + [shape((count, hidden))] * 3,
-        [rows, cots] + mats,
+        [flat_longer, flat, flat] + [hidden_shape] * 3,
+        [me] + mats + mats + [cots] + own + far,
         grid=grid,
-        in_specs=[whole(message), whole(longer)] + mat_specs,
-        out_specs=[whole(longer), whole(flat)] + [hidden_spec] * 3,
-        scratch=[wide] * 2,
+        in_specs=[smem, across_a, across_a, down_a, across_b, across_b, down_b, whole(message)]
+        + [whole(longer_piece)] * experts,
+        out_specs=[whole(flat_longer)] + [whole(flat)] * 2 + [whole(hidden_shape)] * 3,
+        scratch=[pltpu.VMEM((count, 1), F32)],
         flops=6 * flops,
     )
+    active, gate_part, up_part = (jnp.swapaxes(a, 0, 1).reshape(count, hidden) for a in parts)
+    grads = grads.reshape(experts, slots, width + LANES)
     grads = exchange(after(grads, frows), "grads")
     (outs,) = call(
-        forward_kernel,
+        partial(forward_kernel, steps),
         "forward",
         [message],
         [frows] + mats,
         grid=grid,
-        in_specs=[whole(message)] + mat_specs,
-        out_specs=[whole(message)],
-        scratch=[wide],
+        in_specs=[whole(message), across_a, across_a, down_b],
+        out_specs=[pl.BlockSpec((experts, slots, columns), lambda i: (0, 0, late(i)))],
+        scratch=[pltpu.VMEM(hidden_shape.shape, BF16)],
         flops=3 * flops,
     )
-    outs = exchange(after(outs, grads), "outs")
-    flat_rows = rows.reshape(count, width)
     gate_wgrad = t_dot(flat_rows, gate_part).astype(BF16)
     up_wgrad = t_dot(flat_rows, up_part).astype(BF16)
     down_wgrad = t_dot(active, scaled).astype(BF16)
+    outs = exchange(after(outs, grads, gate_wgrad, up_wgrad, down_wgrad), "outs")
 
     grad_in, sums = call(
         partial(source_kernel, top),
         "source",
         [block, shape((-(-(experts + 1) // 8) * 8, width), F32)],
         [rank, grads, table, lifted, router_t, normed, xp, dy_in, gain_row],
-        scratch=[pltpu.VMEM((count, tokens), BF16), pltpu.VMEM((experts, tokens), F32)],
-    )
-    step = 1
-    while step < lax.axis_size("expert"):
-        sums = sums + hop(sums, 0, step, "sums")
-        step *= 2
-    (forward,) = call(
-        out_kernel,
-        "out",
-        [block],
-        [frank, fweight, x_in, outs],
-        scratch=[pltpu.VMEM((count, tokens), BF16)] * 2,
-    )
+        scratch=[
+            pltpu.VMEM((count, tokens), BF16),
+            pltpu.VMEM((experts, tokens), F32),
+        ],
+    )
+    sums = swap([sums] * half, "sums")
+    while len(sums) > 1:
+        sums = [a + b for a, b in zip(sums[::2], sums[1::2])]
+    sums = sums[0] + hop(sums[0], 0, half, "sums_far")
+    (spread,) = call(
+        partial(spread_kernel, slots),
+        "spread",
+        [shape((tokens, count))],
+        [frank, fweight],
+        scratch=[pltpu.VMEM((count, tokens), F32)],
+    )
+    forward = (x_in.astype(F32) + dot(spread, outs.reshape(count, width))).astype(BF16)
     return (
         forward[None],
         grad_in[None],

time: 350 us -> 328 us (0.937)
  waiting for transfers between devices: 224 us -> 180 us
  starting transfers between devices: 30.6 us -> 41.4 us
  local copies, waits for them, and re-layouts: 4.78 us -> 15.4 us
  Pallas kernels: 75.6 us -> 69.1 us
  matrix products: 12.1 us -> 18.3 us
    all_to_all x5 -> x4, waiting for transfers between devices: 160 us -> 64.3 us  [exchange(): lax.all_to_all(array, 'expert', 0, 0, tiled=True, axis_index_groups=groups)]
    ppermute x3 -> x12, waiting for transfers between devices: 37.7 us -> 111 us  [hop(): lax.ppermute(block, 'expert', [(e, e ^ flip) for e in range(experts)])]
    ppermute x2, waiting for transfers between devices: 27.1 us -> 4.76 us  [hop(): return lax.ppermute(block, ('pipe', 'expert'), route)]
    ppermute x3 -> x12, starting transfers between devices: 6.1 us -> 21.1 us  [hop(): lax.ppermute(block, 'expert', [(e, e ^ flip) for e in range(experts)])]
    transpose x0 -> x3, local copies, waits for them, and re-layouts: none -> 6.76 us  [per_device(): jnp.swapaxes(a, 0, 1).reshape(count, hidden)]
    pallas_call x8 -> x10, Pallas kernels: 75.6 us -> 69.1 us  [call(): pl.pallas_call(kernel, out_shape=[jax.ShapeDtypeStruct(o.shape, o.dtype)...]
    all_to_all x5 -> x4, starting transfers between devices: 23.7 us -> 17.8 us  [exchange(): lax.all_to_all(array, 'expert', 0, 0, tiled=True, axis_index_groups=groups)]
    unnamed x22 -> x34, local copies, waits for them, and re-layouts: 3.54 us -> 7.41 us
  transfers between devices with their start and end apart: 10 -> 18, of which waited for: 9 -> 13; matrix products, arithmetic and copies ran while one was open for 4% -> 8% of each run, Pallas kernels for 18% -> 21%
where the time goes in v1:
time: 328 us; the launch traced here: 327 us
  waiting for transfers between devices  180 us (55%)
  Pallas kernels  69.1 us (21%)
  starting transfers between devices  41.4 us (13%)
  matrix products  18.3 us (6%)
  local copies, waits for them, and re-layouts  15.4 us (5%)
    ppermute x12, waiting for transfers between devices, hop(): lax.ppermute(block, 'expert', [(e, e ^ flip) for e in range(experts)])  111 us
    pallas_call x10, Pallas kernels, call(): pl.pallas_call(kernel, out_shape=[jax.ShapeDtypeStruct(o.shape, o.dtype)...  69.1 us
    all_to_all x4, waiting for transfers between devices, exchange(): lax.all_to_all(array, 'expert', 0, 0, tiled=True, axis_index_groups=groups)  64.3 us
    ppermute x12, starting transfers between devices, hop(): lax.ppermute(block, 'expert', [(e, e ^ flip) for e in range(experts)])  21.1 us
    all_to_all x4, starting transfers between devices, exchange(): lax.all_to_all(array, 'expert', 0, 0, tiled=True, axis_index_groups=groups)  17.8 us
    dot_general x3, matrix products, t_dot(): lax.dot_general(a, b, dims, preferred_element_type=F32, precision=precision)  14.5 us
    unnamed x34, local copies, waits for them, and re-layouts  7.41 us
    transpose x3, local copies, waits for them, and re-layouts, per_device(): jnp.swapaxes(a, 0, 1).reshape(count, hidden)  6.76 us
  transfers between devices with their start and end apart: 18, of which 13 were waited for; matrix products, arithmetic and copies ran while one was open for 8% of the time, Pallas kernels for 21%

profile of v1, /device:TPU:0, one launch (start us, length us, event | category | flops | bytes accessed | tf_op | source)
XLA Modules:
  0.0 326.9 jit_solution(15185638710514941161)
XLA Ops:
  0.6 2.5 collective-permute-start.1
  3.1 2.6 collective-permute-start.2
  5.7 1.3 pad_add_fusion.table_ref.refs_3_.refs_4_.refs_2_
  7.0 1.5 ranks.1
  8.6 4.6 %own_rows.1 = (bf16[80,2176]{1,0:T(8,128)(2,1)}, bf16[80,2176]{1,0:T(8,128)(2,1)}, bf16[80,2176]{1,0:T(8,128)(2,1)}, bf16[80,2176]{1,0:T(8,128)(2,1)}, f32[8,256...) custom-call(s32[1]{0:T(128)} %bitcast.9.refs_0_, bf16[256,2048]{1,0:T(8,128)(2,1)} %bitcast.52, ...), custom_call_target="tpu_custom_call" | custom-call | bytes 55552 | tf_op jit(solution)/shard_map/own_rows/pallas_call | solution.py:55
  13.2 1.5 collective-permute-start.4
  14.7 1.6 collective-permute-start.5
  16.3 0.4 collective-permute-start.6
  16.7 0.0 collective-permute-done.1.x_ref.refs_7_
  16.7 1.6 collective-permute-start.3
  18.3 4.3 %cots.1 = bf16[8,80,2048]{2,1,0:T(8,128)(2,1)} custom-call(s32[8,256]{1,0:T(8,128)} %get-tuple-element.37.rank_ref.refs_5_.refs_0_, bf16[256,2048]{1,0:T(8,128)(2,1)} %copy-done.5), custom_call_target="tpu_custom_call" | custom-call | bytes 57472 | tf_op jit(solution)/shard_map/cots/pallas_call | solution.py:55
  22.6 29.0 %collective-permute-done.3.table_ref.refs_4_ = s32[6,256]{1,0:T(8,128)S(1)} collective-permute-done((s32[6,256]{1,0:T(8,128)}, s32[6,256]{1,0:T(8,128)S(1)}, u32[]{:S(2)}, u32[]{:S(2)}) %collective-permute-start.3) | collective-permute-done | bytes 6176 | tf_op jit(solution)/shard_map/tables/ppermute | solution.py:22
  51.6 0.0 collective-permute-done.4.refs_9_
  51.6 0.0 collective-permute-done.5.refs_10_
  51.7 1.2 collective-permute-done.6.refs_11_
  52.9 0.0 collective-permute-done.2.refs_1_
  52.9 0.7 copy-done.11
  53.6 0.3 copy-done.6
  54.0 4.7 %all-to-all-start = ((bf16[8,80,2048]{2,1,0:T(8,128)(2,1)}), bf16[8,80,2048]{2,1,0:T(8,128)(2,1)S(1)}, u32[]{:S(2)}, u32[]{:S(2)}) async-start(bf16[8,80,2048]{2,1,0:T(8,128)(2,1)} %cots.1), calls=%async_computation | async-start | bytes 5242880 | tf_op jit(solution)/shard_map/cots/all_to_all | solution.py:317
  58.7 0.0 collective-permute-start
  58.7 1.6 far_ranks.1
  60.2 4.6 %far_rows.1 = (bf16[80,2176]{1,0:T(8,128)(2,1)}, bf16[80,2176]{1,0:T(8,128)(2,1)}, bf16[80,2176]{1,0:T(8,128)(2,1)}, bf16[80,2176]{1,0:T(8,128)(2,1)}) custom-call(s32[1]{0:T(128)} %bitcast.9.refs_0_, bf16[256,2048]{1,0:T(8,128)(2,1)} %copy-done.6, f32[1,2048]{1,0:T(1,128)} %refs_8_.1, bf16[8,2048]{1,0:T(8,128)(2,1)} %bitcast.62, s32[6,256]{1,0:T(8,128)} %copy-done.14, ...), custom_call_target="tpu_custom_call" | custom-call | bytes 39008 | tf_op jit(solution)/shard_map/far_rows/pallas_call | solution.py:55
  64.8 2.0 collective-permute-start.7
  66.9 1.5 collective-permute-start.8
  68.3 0.0 collective-permute-start.9
  68.3 4.8 %collective-permute-done.refs_0_ = bf16[256,2048]{1,0:T(8,128)(2,1)S(1)} collective-permute-done((bf16[256,2048]{1,0:T(8,128)(2,1)}, bf16[256,2048]{1,0:T(8,128)(2,1)S(1)}, u32[]{:S(2)}, u32[]{:S(2)}) %collective-permute-start) | collective-permute-done | bytes 1048608 | tf_op jit(solution)/shard_map/x_in/ppermute | solution.py:28
  73.1 1.0 copy-done.3
  74.1 5.4 %frows.1 = (bf16[8,80,2048]{2,1,0:T(8,128)(2,1)}, f32[8,256]{1,0:T(8,128)}) custom-call(bf16[256,2048]{1,0:T(8,128)(2,1)} %copy-done.3, f32[1,2048]{1,0:T(1,128)} %refs_8_.1, bf16[8,2048]{1,0:T(8,128)(2,1)} %bitcast.63, s32[6,256]{1,0:T(8,128)} %pad_add_fusion.table_ref.refs_3_.refs_4_.refs_2_, s32[8,256]{1,0:T(8,128)} %get-tuple-element.34.refs_4_.rank_ref), custom_call_target="tpu_custom_call" | custom-call | bytes 58336 | tf_op jit(solution)/shard_map/frows/pallas_call | solution.py:55
  79.5 9.2 %collective-permute-done.7.refs_13_ = bf16[80,2176]{1,0:T(8,128)(2,1)S(1)} collective-permute-done((bf16[80,2176]{1,0:T(8,128)(2,1)}, bf16[80,2176]{1,0:T(8,128)(2,1)S(1)}, u32[]{:S(2)}, u32[]{:S(2)}) %collective-permute-start.7) | collective-permute-done | bytes 348192 | tf_op jit(solution)/shard_map/far_rows/ppermute | solution.py:22
  88.7 22.1 %collective-permute-done.8.refs_14_ = bf16[80,2176]{1,0:T(8,128)(2,1)S(1)} collective-permute-done((bf16[80,2176]{1,0:T(8,128)(2,1)}, bf16[80,2176]{1,0:T(8,128)(2,1)S(1)}, u32[]{:S(2)}, u32[]{:S(2)}) %collective-permute-start.8) | collective-permute-done | bytes 348192 | tf_op jit(solution)/shard_map/far_rows/ppermute | solution.py:22
  110.8 0.8 copy-done.13
  111.5 5.6 %collective-permute-done.9.refs_15_ = bf16[80,2176]{1,0:T(8,128)(2,1)} collective-permute-done((bf16[80,2176]{1,0:T(8,128)(2,1)}, bf16[80,2176]{1,0:T(8,128)(2,1)}, u32[]{:S(2)}, u32[]{:S(2)}) %collective-permute-start.9) | collective-permute-done | bytes 348192 | tf_op jit(solution)/shard_map/far_rows/ppermute | solution.py:22
  117.1 1.0 all-to-all-done.refs_7_
  118.1 1.5 copy-done.2
  119.6 4.7 %all-to-all-start.1 = ((bf16[8,80,2048]{2,1,0:T(8,128)(2,1)}), bf16[8,80,2048]{2,1,0:T(8,128)(2,1)S(1)}, u32[]{:S(2)}, u32[]{:S(2)}) async-start(bf16[8,80,2048]{2,1,0:T(8,128)(2,1)} %get-tuple-element.46), calls=%async_computation.1 | async-start | bytes 5242880 | tf_op jit(solution)/shard_map/frows/all_to_all | solution.py:317
  124.4 24.6 %expert.1 = (bf16[640,2176]{1,0:T(8,128)(2,1)}, bf16[640,2048]{1,0:T(8,128)(2,1)}, bf16[640,2048]{1,0:T(8,128)(2,1)}, bf16[3,640,256]{2,1,0:T(8,128)(2,1)}, bf16...) custom-call(s32[1]{0:T(128)} %bitcast.9.refs_0_, bf16[2048,768]{1,0:T(8,128)(2,1)} %bitcast.42, ...), custom_call_target="tpu_custom_call" | custom-call | flops 188743680 | bytes 550912 | tf_op jit(solution)/shard_map/expert/pallas_call | solution.py:55
  149.0 34.0 %all-to-all-done.1.rows_ref = bf16[8,80,2048]{2,1,0:T(8,128)(2,1)S(1)} async-done(((bf16[8,80,2048]{2,1,0:T(8,128)(2,1)}), bf16[8,80,2048]{2,1,0:T(8,128)(2,1)S(1)}, u32[]{:S(2)}, u32[]{:S(2)}) %all-to-all-start.1) | async-done | bytes 2621472 | tf_op jit(solution)/shard_map/frows/all_to_all | solution.py:317
  183.0 1.5 copy-done.1
  184.5 3.8 %all-to-all-start.2 = ((bf16[8,80,2176]{2,1,0:T(8,128)(2,1)}), bf16[8,80,2176]{2,1,0:T(8,128)(2,1)S(1)}, u32[]{:S(2)}, u32[]{:S(2)}) async-start(bf16[8,80,2176]{2,1,0:T(8,128)(2,1)} %bitcast.54), calls=%async_computation.2 | async-start | bytes 5570560 | tf_op jit(solution)/shard_map/grads/all_to_all | solution.py:317
  188.4 2.3 copy.21
  190.7 2.2 copy.20
  192.9 2.2 copy.19
  195.1 6.5 %convolution_convert_fusion.1 = bf16[2048,768]{1,0:T(8,128)(2,1)} fusion(bf16[640,2048]{1,0:T(8,128)(2,1)} %get-tuple-element.51, bf16[640,768]{0,1:T(8,128)(2,1)} %bitcast.60), kind=kOutput, calls=%fused_computation.1 | convolution fusion | flops 2014838784 | bytes 6750208 | tf_op jit(solution)/shard_map/dot_general | solution.py:45
  201.6 4.1 %convolution_convert_fusion.2 = bf16[2048,768]{1,0:T(8,128)(2,1)} fusion(bf16[640,2048]{1,0:T(8,128)(2,1)S(1)} %copy-done.16, bf16[640,768]{0,1:T(8,128)(2,1)S(1)} %bitcast.59), kind=kOutput, calls=%fused_computation.2 | convolution fusion | flops 2014838784 | bytes 6750208 | tf_op jit(solution)/shard_map/dot_general | solution.py:45
  205.7 3.9 %convolution_convert_fusion = bf16[768,2048]{1,0:T(8,128)(2,1)} fusion(bf16[640,768]{0,1:T(8,128)(2,1)S(1)} %bitcast.58, bf16[640,2048]{1,0:T(8,128)(2,1)S(1)} %copy-done.15), kind=kOutput, calls=%fused_computation | convolution fusion | flops 2014838784 | bytes 6750208 | tf_op jit(solution)/shard_map/dot_general | solution.py:45
  209.6 12.5 %forward.1 = bf16[8,80,2048]{2,1,0:T(8,128)(2,1)} custom-call(bf16[8,80,2048]{2,1,0:T(8,128)(2,1)} %copy-done.1, bf16[2048,768]{1,0:T(8,128)(2,1)} %bitcast.44, bf16[2048,768]{1,0:T(8,128)(2,1)} %bitcast.47, bf16[768,2048]{1,0:T(8,128)(2,1)} %bitcast.50), custom_call_target="tpu_custom_call" | custom-call | flops 94371840 | bytes 229376 | tf_op jit(solution)/shard_map/forward/pallas_call | solution.py:55
  222.2 29.2 %all-to-all-done.2.refs_1_ = bf16[8,80,2176]{2,1,0:T(8,128)(2,1)S(1)} async-done(((bf16[8,80,2176]{2,1,0:T(8,128)(2,1)}), bf16[8,80,2176]{2,1,0:T(8,128)(2,1)S(1)}, u32[]{:S(2)}, u32[]{:S(2)}) %all-to-all-start.2) | async-done | bytes 2785312 | tf_op jit(solution)/shard_map/grads/all_to_all | solution.py:317
  251.4 1.5 copy-done
  252.9 4.6 %all-to-all-start.3 = ((bf16[8,80,2048]{2,1,0:T(8,128)(2,1)}), bf16[8,80,2048]{2,1,0:T(8,128)(2,1)}, u32[]{:S(2)}, u32[]{:S(2)}) async-start(bf16[8,80,2048]{2,1,0:T(8,128)(2,1)} %forward.1), calls=%async_computation.3 | async-start | bytes 5242880 | tf_op jit(solution)/shard_map/outs/all_to_all | solution.py:317
  257.6 0.0 copy-start.4
  257.6 8.2 %source.1 = (bf16[256,2048]{1,0:T(8,128)(2,1)}, f32[16,2048]{1,0:T(8,128)}) custom-call(s32[8,256]{1,0:T(8,128)} %get-tuple-element.37.rank_ref.refs_5_.refs_0_, bf16[8,80,2176]{2,1,0:T(8,128)(2,1)} %copy-done, s32[6,256]{1,0:T(8,128)} %pad_add_fusion.table_ref.refs_3_.refs_4_.refs_2_, f32[2,256]{1,0:T(2,128)} %get-tuple-element.57.refs_3_, ...), custom_call_target="tpu_custom_call" | custom-call | bytes 112000 | tf_op jit(solution)/shard_map/source/pallas_call | solution.py:55
  265.8 1.7 collective-permute-start.10
  267.5 1.5 collective-permute-start.11
  268.9 0.4 collective-permute-start.12
  269.3 12.9 %collective-permute-done.10 = f32[16,2048]{1,0:T(8,128)S(1)} collective-permute-done((f32[16,2048]{1,0:T(8,128)}, f32[16,2048]{1,0:T(8,128)S(1)}, u32[]{:S(2)}, u32[]{:S(2)}) %collective-permute-start.10) | collective-permute-done | bytes 131104 | tf_op jit(solution)/shard_map/sums/ppermute | solution.py:22
  282.2 21.9 %collective-permute-done.11 = f32[16,2048]{1,0:T(8,128)S(1)} collective-permute-done((f32[16,2048]{1,0:T(8,128)}, f32[16,2048]{1,0:T(8,128)S(1)}, u32[]{:S(2)}, u32[]{:S(2)}) %collective-permute-start.11) | collective-permute-done | bytes 131104 | tf_op jit(solution)/shard_map/sums/ppermute | solution.py:22
  304.2 1.4 collective-permute-done.12
  305.6 0.9 add_add_fusion
  306.5 6.4 %collective-permute-start.13 = (f32[16,2048]{1,0:T(8,128)S(1)}, f32[16,2048]{1,0:T(8,128)S(1)}, u32[]{:S(2)}, u32[]{:S(2)}) collective-permute-start(f32[16,2048]{1,0:T(8,128)S(1)} %add_add_fusion), channel_id=1, source_target_pairs={{0,4},{1,5},{2,6},{3,7},{4,0},{5,1},{6,2},{7,3},{8,12},{9,13},{10,... | collective-permute-start | bytes 393224 | tf_op jit(solution)/shard_map/sums_far/ppermute | solution.py:22
  312.9 1.6 spread.1
  314.5 7.3 %collective-permute-done.13 = f32[16,2048]{1,0:T(8,128)S(1)} collective-permute-done((f32[16,2048]{1,0:T(8,128)S(1)}, f32[16,2048]{1,0:T(8,128)S(1)}, u32[]{:S(2)}, u32[]{:S(2)}) %collective-permute-start.13) | collective-permute-done | bytes 131104 | tf_op jit(solution)/shard_map/sums_far/ppermute | solution.py:22
  321.8 0.6 slice.9
  322.4 0.6 slice_bitcast_fusion
  323.1 3.8 %fusion = bf16[1,256,2048]{2,1,0:T(8,128)(2,1)} fusion(bf16[256,2048]{1,0:T(8,128)(2,1)S(1)} %copy-done.4, bf16[256,640]{1,0:T(8,128)(2,1)} %spread.1, bf16[640,2048]{1,0:T(8,128)(2,1)} %bitcast.21), kind=kOutput, calls=%fused_computation.4 | convolution fusion | flops 672661504 | bytes 5046272 | tf_op jit(solution)/shard_map/dot_general | solution.py:36
  (28 shorter events, 0.1 us)
Async XLA Ops:
  0.6 16.0 %collective-permute-start.1 = (bf16[256,2048]{1,0:T(8,128)(2,1)}, bf16[256,2048]{1,0:T(8,128)(2,1)S(1)}, u32[]{:S(2)}, u32[]{:S(2)}) collective-permute-start(bf16[256,2048]{1,0:T(8,128)(2,1)} %bitcast.67), channel_id=1, source_target_pairs={{0,24},{1,25},{2,26},{3,27},{4,28},{5,29},{6,30},{7,31},{8,0},{9,1... | collective-permute-start | bytes 3145736 | tf_op jit(solution)/shard_map/dy_in/ppermute | solution.py:28
  3.1 49.8 %collective-permute-start.2 = (bf16[256,2048]{1,0:T(8,128)(2,1)}, bf16[256,2048]{1,0:T(8,128)(2,1)S(1)}, u32[]{:S(2)}, u32[]{:S(2)}) collective-permute-start(bf16[256,2048]{1,0:T(8,128)(2,1)} %bitcast.51), channel_id=1, source_target_pairs={{0,4},{1,5},{2,6},{3,7},{4,0},{5,1},{6,2},{7,3},{8,12},{9,13},{10,... | collective-permute-start | bytes 3145736 | tf_op jit(solution)/shard_map/xp_far/ppermute | solution.py:22
  13.2 38.5 %collective-permute-start.4 = (bf16[80,2176]{1,0:T(8,128)(2,1)}, bf16[80,2176]{1,0:T(8,128)(2,1)S(1)}, u32[]{:S(2)}, u32[]{:S(2)}) collective-permute-start(bf16[80,2176]{1,0:T(8,128)(2,1)} %get-tuple-element.38), channel_id=1, source_target_pairs={{0,1},{1,0},{2,3},{3,2},{4,5},{5,4},{6,7},{7,6},{8,9},{9,8},{10,11... | collective-permute-start | bytes 1044488 | tf_op jit(solution)/shard_map/own_rows/ppermute | solution.py:22
  14.7 37.0 %collective-permute-start.5 = (bf16[80,2176]{1,0:T(8,128)(2,1)}, bf16[80,2176]{1,0:T(8,128)(2,1)S(1)}, u32[]{:S(2)}, u32[]{:S(2)}) collective-permute-start(bf16[80,2176]{1,0:T(8,128)(2,1)} %get-tuple-element.39), channel_id=1, source_target_pairs={{0,2},{1,3},{2,0},{3,1},{4,6},{5,7},{6,4},{7,5},{8,10},{9,11},{10,... | collective-permute-start | bytes 1044488 | tf_op jit(solution)/shard_map/own_rows/ppermute | solution.py:22
  16.3 36.6 %collective-permute-start.6 = (bf16[80,2176]{1,0:T(8,128)(2,1)}, bf16[80,2176]{1,0:T(8,128)(2,1)S(1)}, u32[]{:S(2)}, u32[]{:S(2)}) collective-permute-start(bf16[80,2176]{1,0:T(8,128)(2,1)} %get-tuple-element.40), channel_id=1, source_target_pairs={{0,3},{1,2},{2,1},{3,0},{4,7},{5,6},{6,5},{7,4},{8,11},{9,10},{10,... | collective-permute-start | bytes 1044488 | tf_op jit(solution)/shard_map/own_rows/ppermute | solution.py:22
  16.7 1.6 copy-start.5
  16.7 35.0 %collective-permute-start.3 = (s32[6,256]{1,0:T(8,128)}, s32[6,256]{1,0:T(8,128)S(1)}, u32[]{:S(2)}, u32[]{:S(2)}) collective-permute-start(s32[6,256]{1,0:T(8,128)} %pad_add_fusion.table_ref.refs_3_.refs_4_.refs_2_), channel_id=1, source_target_pairs={{0,4},{1,5},{2,6},{3,7},{4,0},{5,1},{6,2},{7,3},{8,12},{9,13},{10,... | collective-permute-start | bytes 18440 | tf_op jit(solution)/shard_map/tables/ppermute | solution.py:22
  51.6 7.0 %copy-start.14 = (s32[6,256]{1,0:T(8,128)}, s32[6,256]{1,0:T(8,128)S(1)}, u32[]{:S(2)}) copy-start(s32[6,256]{1,0:T(8,128)S(1)} %collective-permute-done.3.table_ref.refs_4_) | copy-start | bytes 18436
  51.6 72.7 %copy-start.9 = (bf16[80,2176]{1,0:T(8,128)(2,1)}, bf16[80,2176]{1,0:T(8,128)(2,1)S(1)}, u32[]{:S(2)}) copy-start(bf16[80,2176]{1,0:T(8,128)(2,1)S(1)} %collective-permute-done.4.refs_9_) | copy-start | bytes 1044484
  51.6 72.7 %copy-start.10 = (bf16[80,2176]{1,0:T(8,128)(2,1)}, bf16[80,2176]{1,0:T(8,128)(2,1)S(1)}, u32[]{:S(2)}) copy-start(bf16[80,2176]{1,0:T(8,128)(2,1)S(1)} %collective-permute-done.5.refs_10_) | copy-start | bytes 1044484
  52.9 0.7 copy-start.11
  52.9 1.1 copy-start.6
  54.0 64.2 %all-to-all-start = ((bf16[8,80,2048]{2,1,0:T(8,128)(2,1)}), bf16[8,80,2048]{2,1,0:T(8,128)(2,1)S(1)}, u32[]{:S(2)}, u32[]{:S(2)}) async-start(bf16[8,80,2048]{2,1,0:T(8,128)(2,1)} %cots.1), calls=%async_computation | async-start | bytes 5242880 | tf_op jit(solution)/shard_map/cots/all_to_all | solution.py:317
  58.7 14.4 %collective-permute-start = (bf16[256,2048]{1,0:T(8,128)(2,1)}, bf16[256,2048]{1,0:T(8,128)(2,1)S(1)}, u32[]{:S(2)}, u32[]{:S(2)}) collective-permute-start(bf16[256,2048]{1,0:T(8,128)(2,1)} %bitcast.68), channel_id=1, source_target_pairs={{0,8},{1,9},{2,10},{3,11},{4,12},{5,13},{6,14},{7,15},{8,16},{9,17... | collective-permute-start | bytes 3145736 | tf_op jit(solution)/shard_map/x_in/ppermute | solution.py:28
  64.8 23.8 %collective-permute-start.7 = (bf16[80,2176]{1,0:T(8,128)(2,1)}, bf16[80,2176]{1,0:T(8,128)(2,1)S(1)}, u32[]{:S(2)}, u32[]{:S(2)}) collective-permute-start(bf16[80,2176]{1,0:T(8,128)(2,1)} %get-tuple-element.43), channel_id=1, source_target_pairs={{0,1},{1,0},{2,3},{3,2},{4,5},{5,4},{6,7},{7,6},{8,9},{9,8},{10,11... | collective-permute-start | bytes 1044488 | tf_op jit(solution)/shard_map/far_rows/ppermute | solution.py:22
  66.9 43.9 %collective-permute-start.8 = (bf16[80,2176]{1,0:T(8,128)(2,1)}, bf16[80,2176]{1,0:T(8,128)(2,1)S(1)}, u32[]{:S(2)}, u32[]{:S(2)}) collective-permute-start(bf16[80,2176]{1,0:T(8,128)(2,1)} %get-tuple-element.44), channel_id=1, source_target_pairs={{0,2},{1,3},{2,0},{3,1},{4,6},{5,7},{6,4},{7,5},{8,10},{9,11},{10,... | collective-permute-start | bytes 1044488 | tf_op jit(solution)/shard_map/far_rows/ppermute | solution.py:22
  68.3 48.8 %collective-permute-start.9 = (bf16[80,2176]{1,0:T(8,128)(2,1)}, bf16[80,2176]{1,0:T(8,128)(2,1)}, u32[]{:S(2)}, u32[]{:S(2)}) collective-permute-start(bf16[80,2176]{1,0:T(8,128)(2,1)} %get-tuple-element.45), channel_id=1, source_target_pairs={{0,3},{1,2},{2,1},{3,0},{4,7},{5,6},{6,5},{7,4},{8,11},{9,10},{10,... | collective-permute-start | bytes 1044488 | tf_op jit(solution)/shard_map/far_rows/ppermute | solution.py:22
  73.1 1.0 copy-start.3
  88.7 22.1 %copy-start.12 = (bf16[80,2176]{1,0:T(8,128)(2,1)}, bf16[80,2176]{1,0:T(8,128)(2,1)S(1)}, u32[]{:S(2)}) copy-start(bf16[80,2176]{1,0:T(8,128)(2,1)S(1)} %collective-permute-done.7.refs_13_) | copy-start | bytes 1044484
  110.8 0.8 copy-start.13
  118.1 1.5 copy-start.2
  119.6 63.4 %all-to-all-start.1 = ((bf16[8,80,2048]{2,1,0:T(8,128)(2,1)}), bf16[8,80,2048]{2,1,0:T(8,128)(2,1)S(1)}, u32[]{:S(2)}, u32[]{:S(2)}) async-start(bf16[8,80,2048]{2,1,0:T(8,128)(2,1)} %get-tuple-element.46), calls=%async_computation.1 | async-start | bytes 5242880 | tf_op jit(solution)/shard_map/frows/all_to_all | solution.py:317
  183.0 1.5 copy-start.1
  184.5 66.9 %all-to-all-start.2 = ((bf16[8,80,2176]{2,1,0:T(8,128)(2,1)}), bf16[8,80,2176]{2,1,0:T(8,128)(2,1)S(1)}, u32[]{:S(2)}, u32[]{:S(2)}) async-start(bf16[8,80,2176]{2,1,0:T(8,128)(2,1)} %bitcast.54), calls=%async_computation.2 | async-start | bytes 5570560 | tf_op jit(solution)/shard_map/grads/all_to_all | solution.py:317
  195.1 6.5 %copy-start.8 = (bf16[640,3,256]{0,2,1:T(8,128)(2,1)S(1)}, bf16[640,3,256]{0,2,1:T(8,128)(2,1)}, u32[]{:S(2)}) copy-start(bf16[640,3,256]{0,2,1:T(8,128)(2,1)} %copy.19) | copy-start | bytes 2949124
  195.1 6.5 %copy-start.16 = (bf16[640,2048]{1,0:T(8,128)(2,1)S(1)}, bf16[640,2048]{1,0:T(8,128)(2,1)}, u32[]{:S(2)}) copy-start(bf16[640,2048]{1,0:T(8,128)(2,1)} %get-tuple-element.51) | copy-start | bytes 7864324
  201.6 4.1 %copy-start.7 = (bf16[640,3,256]{0,2,1:T(8,128)(2,1)S(1)}, bf16[640,3,256]{0,2,1:T(8,128)(2,1)}, u32[]{:S(2)}) copy-start(bf16[640,3,256]{0,2,1:T(8,128)(2,1)} %copy.21) | copy-start | bytes 2949124
  201.6 4.1 %copy-start.15 = (bf16[640,2048]{1,0:T(8,128)(2,1)S(1)}, bf16[640,2048]{1,0:T(8,128)(2,1)}, u32[]{:S(2)}) copy-start(bf16[640,2048]{1,0:T(8,128)(2,1)} %get-tuple-element.55) | copy-start | bytes 7864324
  251.4 1.5 copy-start
  252.9 70.1 %all-to-all-start.3 = ((bf16[8,80,2048]{2,1,0:T(8,128)(2,1)}), bf16[8,80,2048]{2,1,0:T(8,128)(2,1)}, u32[]{:S(2)}, u32[]{:S(2)}) async-start(bf16[8,80,2048]{2,1,0:T(8,128)(2,1)} %forward.1), calls=%async_computation.3 | async-start | bytes 5242880 | tf_op jit(solution)/shard_map/outs/all_to_all | solution.py:317
  257.6 65.5 %copy-start.4 = (bf16[256,2048]{1,0:T(8,128)(2,1)S(1)}, bf16[256,2048]{1,0:T(8,128)(2,1)}, u32[]{:S(2)}) copy-start(bf16[256,2048]{1,0:T(8,128)(2,1)} %copy-done.3) | copy-start | bytes 3145732
  265.8 16.4 %collective-permute-start.10 = (f32[16,2048]{1,0:T(8,128)}, f32[16,2048]{1,0:T(8,128)S(1)}, u32[]{:S(2)}, u32[]{:S(2)}) collective-permute-start(f32[16,2048]{1,0:T(8,128)} %get-tuple-element.60), channel_id=1, source_target_pairs={{0,1},{1,0},{2,3},{3,2},{4,5},{5,4},{6,7},{7,6},{8,9},{9,8},{10,11... | collective-permute-start | bytes 393224 | tf_op jit(solution)/shard_map/sums/ppermute | solution.py:22
  267.5 36.7 %collective-permute-start.11 = (f32[16,2048]{1,0:T(8,128)}, f32[16,2048]{1,0:T(8,128)S(1)}, u32[]{:S(2)}, u32[]{:S(2)}) collective-permute-start(f32[16,2048]{1,0:T(8,128)} %get-tuple-element.60), channel_id=1, source_target_pairs={{0,2},{1,3},{2,0},{3,1},{4,6},{5,7},{6,4},{7,5},{8,10},{9,11},{10,... | collective-permute-start | bytes 393224 | tf_op jit(solution)/shard_map/sums/ppermute | solution.py:22
  268.9 36.6 %collective-permute-start.12 = (f32[16,2048]{1,0:T(8,128)}, f32[16,2048]{1,0:T(8,128)S(1)}, u32[]{:S(2)}, u32[]{:S(2)}) collective-permute-start(f32[16,2048]{1,0:T(8,128)} %get-tuple-element.60), channel_id=1, source_target_pairs={{0,3},{1,2},{2,1},{3,0},{4,7},{5,6},{6,5},{7,4},{8,11},{9,10},{10,... | collective-permute-start | bytes 393224 | tf_op jit(solution)/shard_map/sums/ppermute | solution.py:22
  306.5 15.3 %collective-permute-start.13 = (f32[16,2048]{1,0:T(8,128)S(1)}, f32[16,2048]{1,0:T(8,128)S(1)}, u32[]{:S(2)}, u32[]{:S(2)}) collective-permute-start(f32[16,2048]{1,0:T(8,128)S(1)} %add_add_fusion), channel_id=1, source_target_pairs={{0,4},{1,5},{2,6},{3,7},{4,0},{5,1},{6,2},{7,3},{8,12},{9,13},{10,... | collective-permute-start | bytes 393224 | tf_op jit(solution)/shard_map/sums_far/ppermute | solution.py:22

commit v2 on v1

--- a/solution.py
+++ b/solution.py
@@ -150,13 +150,6 @@
     if batch:
         gates(normed_ref, router_ref, route_rows(table_ref, batch, top), None, weight_ref)
     put_pieces(me_ref, rank_ref, normed_ref, weight_ref if batch else None, pieces)
-
-
-def rows_kernel(top, *refs):
-    x_ref, gain_ref, router_ref, table_ref, rank_ref, message_ref, weight_ref, normed_ref = refs
-    normalise(x_ref, gain_ref, normed_ref)
-    cots_kernel(rank_ref, normed_ref, message_ref)
-    gates(normed_ref, router_ref, route_rows(table_ref, 0, top), None, weight_ref)
 
 
 def cots_kernel(rank_ref, x_ref, message_ref):
@@ -223,22 +216,18 @@
         message_ref[:, width:] = jnp.broadcast_to(inner, (inner.shape[0], LANES))
 
 
-def forward_kernel(steps, rows_ref, gate_a, up_a, down_b, out_ref, active_ref):
-    step = pl.program_id(0)
-
-    @pl.when(step < steps)
-    def _():
-        rows = flat_of(rows_ref)
-        gate = dot(rows, gate_a[...])
-        active_ref[step] = (gate * jax.nn.sigmoid(gate) * dot(rows, up_a[...])).astype(BF16)
-
-    @pl.when(step >= steps)
-    def _():
-        part = gate_a.shape[1]
-        result = jnp.zeros(active_ref.shape[1:2] + down_b.shape[1:], F32)
-        for f in range(steps):
-            result = result + dot(active_ref[f], down_b[f * part : (f + 1) * part, :])
-        out_ref[...] = result.astype(BF16).reshape(out_ref.shape)
+def forward_kernel(half, me_ref, gate_w, up_w, down_w, *refs):
+    pieces, (out_ref, rows_ref) = refs[:half], refs[-2:]
+    slots = pieces[0].shape[0]
+    for k, piece in enumerate(pieces):
+        start = pl.multiple_of((me_ref[0] ^ k) % half * slots, 16)
+        rows_ref[pl.ds(start, slots), :] = piece[...]
+    gate = dot(rows_ref[...], gate_w[...])
+    active = (gate * jax.nn.sigmoid(gate) * dot(rows_ref[...], up_w[...])).astype(BF16)
+    columns = 512 if out_ref.shape[2] % 512 == 0 else out_ref.shape[2]
+    for c in range(0, out_ref.shape[2], columns):
+        result = dot(active, down_w[:, c : c + columns]).astype(BF16)
+        out_ref[:, :, c : c + columns] = result.reshape(half, slots, columns)
 
 
 def spread_kernel(slots, rank_ref, weight_ref, spread_ref, flat_ref):
@@ -248,16 +237,29 @@
     spread_ref[...] = flat_ref[...].T.astype(BF16)
 
 
-def source_kernel(top, *refs):
-    rank_ref, grads_ref, table_ref, lifted_ref = refs[:4]
-    router_ref, normed_ref, xp_ref, dy_ref, gain_ref = refs[4:9]
-    grad_ref, sums_ref, hot_ref, terms_ref = refs[9:]
+def split(value):
+    parts = []
+    for _ in range(3):
+        parts.append(value.astype(BF16).astype(F32))
+        value = value - parts[-1]
+    return jnp.concatenate(parts, axis=0).astype(BF16)
+
+
+def bare_of(x_ref):
+    values = x_ref[...].astype(F32)
+    scale = lax.rsqrt(jnp.mean(values * values, axis=-1, keepdims=True) + EPS)
+    return values * scale, scale
+
+
+def sums_kernel(top, cuts, *refs):
+    rank_ref, hot_ref, table_ref, lifted_ref, router_ref, normed_ref, xp_ref = refs[:7]
+    grads, (dnormed_ref, sums_ref, terms_ref) = refs[7 : 7 + cuts], refs[7 + cuts :]
     experts, tokens = rank_ref.shape
-    slots, width = grads_ref.shape[1], xp_ref.shape[1]
+    some, slots, _ = grads[0].shape
+    width = xp_ref.shape[1]
     for e in range(experts):
         hot = one_hot(slot_mask(rank_ref, e, slots))
-        hot_ref[e * slots : (e + 1) * slots, :] = hot
-        terms_ref[e : e + 1, :] = t_dot(grads_ref[e, :, width:], hot)[:1, :]
+        terms_ref[e : e + 1, :] = t_dot(grads[e // some][e % some, :, width:], hot)[:1, :]
     routes = route_rows(table_ref, 1, top)
     everyone = iota((experts, tokens), 0)
     lifted = [lifted_ref[j : j + 1, :] for j in range(top)]
@@ -271,17 +273,23 @@
     for r, d, l in zip(routes, dweight, lifted):
         dsel = (d / total - both / (total * total)) * l * (1.0 - l)
         dlogits = dlogits + jnp.where(r == everyone, dsel, 0.0)
-    exact = lax.Precision.HIGHEST
-    normed = normed_ref[...].astype(F32)
+    stacked = split(dlogits)
+    terms = dot(stacked, normed_ref[...])
     sums_ref[...] = jnp.zeros_like(sums_ref)
-    sums_ref[:experts, :] = jnp.dot(dlogits, normed, precision=exact, preferred_element_type=F32)
-    dnormed = t_dot(hot_ref[...], grads_ref[:, :, :width].reshape(-1, width))
-    dnormed = dnormed + t_dot(dlogits, router_ref[...].astype(F32), precision=exact)
-    values = xp_ref[...].astype(F32)
-    scale = lax.rsqrt(jnp.mean(values * values, axis=-1, keepdims=True) + EPS)
-    bare = values * scale
-    sums_ref[experts : experts + 1, :] = jnp.sum(dnormed * bare, axis=0, keepdims=True)
-    lifted_grad = dnormed * gain_ref[...]
+    sums_ref[:experts, :] = terms[:experts] + (terms[experts : 2 * experts] + terms[2 * experts :])
+    router = jnp.concatenate([router_ref[...].astype(F32)] * 3, axis=0).astype(BF16)
+    dnormed = t_dot(stacked, router)
+    for c, ref in enumerate(grads):
+        part = slice(c * some * slots, (c + 1) * some * slots)
+        dnormed = dnormed + dot(hot_ref[:, part], ref[:, :, :width].reshape(-1, width))
+    dnormed_ref[...] = dnormed
+    gain_sum = jnp.sum(dnormed * bare_of(xp_ref)[0], axis=0, keepdims=True)
+    sums_ref[experts : experts + 1, :] = gain_sum
+
+
+def source_kernel(dnormed_ref, xp_ref, dy_ref, gain_ref, grad_ref):
+    bare, scale = bare_of(xp_ref)
+    lifted_grad = dnormed_ref[...] * gain_ref[...]
     slope = jnp.mean(lifted_grad * bare, axis=-1, keepdims=True)
     grad_ref[...] = (dy_ref[...].astype(F32) + scale * (lifted_grad - bare * slope)).astype(BF16)
 
@@ -367,14 +375,9 @@
     (cots,) = call(cots_kernel, "cots", [message], [rank, dy_in])
     cots = exchange(after(cots, xp_far, far_table, *own[1:]), "cots")
     far = far_rows(xp_far, 1, rank_far, "far_rows")
-    frows, fweight = call(
-        partial(rows_kernel, top),
-        "frows",
-        [message, per_token],
-        [x_in, gain_row, router_t, table, frank],
-        scratch=[normed_scratch],
-    )
-    frows = exchange(after(frows, cots, *far[1:]), "frows")
+    x_far = hop(after(next_input[0], cots, *far[1:]), 1, half, "x_far")
+    fown, fweight = own_rows(x_in, 0, frank, "fown_rows")
+    ffar = far_rows(x_far, 0, frank_far, "ffar_rows")
 
     count = experts * slots
     part = 256 if hidden % 256 == 0 else hidden
@@ -383,7 +386,7 @@
     grid = (steps + width // columns,)
 
     def whole(dims):
-        return pl.BlockSpec(dims.shape, lambda i: (0,) * len(dims.shape), pipeline_mode=pl.Buffered(1))
+        return pl.BlockSpec(dims.shape, lambda *_: (0,) * len(dims.shape), pipeline_mode=pl.Buffered(1))
 
     def early(i):
         return jnp.minimum(i, steps - 1)
@@ -391,11 +394,22 @@
     def late(i):
         return jnp.maximum(i - steps, 0)
 
-    across_a = pl.BlockSpec((width, part), lambda i: (0, early(i)))
+    across_a = pl.BlockSpec((width, part), lambda i, *_: (0, early(i)))
     down_a = pl.BlockSpec((part, width), lambda i: (early(i), 0))
     across_b = pl.BlockSpec((columns, hidden), lambda i: (late(i), 0))
-    down_b = pl.BlockSpec((hidden, columns), lambda i: (0, late(i)))
+    down_b = pl.BlockSpec((hidden, columns), lambda i, *_: (0, late(i)))
     flops = 2 * count * width * hidden
+    def spread_of(rank, weight, name):
+        return call(
+            partial(spread_kernel, slots),
+            name,
+            [shape((tokens, count))],
+            [rank, weight],
+            scratch=[pltpu.VMEM((count, tokens), F32)],
+        )[0]
+
+    spread = spread_of(frank, fweight, "spread")
+    hot = spread_of(rank, jnp.ones((experts, tokens), F32), "hot")
     flat, hidden_shape = shape((count, width)), shape((steps, count, part))
     flat_longer = shape((count, width + LANES))
     grads, flat_rows, scaled, *parts = call(
@@ -412,45 +426,67 @@
     )
     active, gate_part, up_part = (jnp.swapaxes(a, 0, 1).reshape(count, hidden) for a in parts)
     grads = grads.reshape(experts, slots, width + LANES)
-    grads = exchange(after(grads, frows), "grads")
-    (outs,) = call(
-        partial(forward_kernel, steps),
-        "forward",
-        [message],
-        [frows] + mats,
-        grid=grid,
-        in_specs=[whole(message), across_a, across_a, down_b],
-        out_specs=[pl.BlockSpec((experts, slots, columns), lambda i: (0, 0, late(i)))],
-        scratch=[pltpu.VMEM(hidden_shape.shape, BF16)],
-        flops=3 * flops,
+    grads = exchange(after(grads, x_far, hot, spread, *fown[1:]), "grads")
+
+    def forward_of(pieces, flip, name, *filled):
+        return pl.pallas_call(
+            partial(forward_kernel, half),
+            out_shape=message,
+            grid_spec=pltpu.PrefetchScalarGridSpec(
+                num_scalar_prefetch=1,
+                grid=(1,),
+                in_specs=[whole(m) for m in mats]
+                + [whole(piece)] * half
+                + [pl.BlockSpec(memory_space=pl.ANY)] * len(filled),
+                out_specs=pl.BlockSpec(
+                    (half, slots, width), lambda i, me_ref: (me_ref[0] // half ^ flip, 0, 0)
+                ),
+                scratch_shapes=[pltpu.VMEM((count // 2, width), BF16)],
+            ),
+            input_output_aliases={4 + half: 0} if filled else {},
+            compiler_params=pltpu.CompilerParams(vmem_limit_bytes=VMEM_BYTES),
+            cost_estimate=pl.CostEstimate(
+                flops=3 * flops // 2, bytes_accessed=6 * width * hidden, transcendentals=0
+            ),
+            name=name,
+        )(me, *mats, *pieces, *filled)
+
+    outs = forward_of(fown, 0, "forward_own")
+    outs = forward_of(ffar, 1, "forward_far", outs)
+    outs = exchange(after(outs, grads), "outs")
+
+    cuts = 4 if experts % 4 == 0 else 1
+    sums_shape = shape((-(-(experts + 1) // 8) * 8, width), F32)
+
+    def full(array):
+        return pl.BlockSpec(array.shape, lambda i: (0,) * len(array.shape))
+
+    def cut_at(c):
+        return pl.BlockSpec((experts // cuts, slots, width + LANES), lambda i: (c, 0, 0))
+
+    known = [rank, hot, table, lifted, router_t, normed, xp]
+    dnormed, sums = call(
+        partial(sums_kernel, top, cuts),
+        "sums",
+        [shape((tokens, width), F32), sums_shape],
+        known + [grads] * cuts,
+        grid=(1,),
+        in_specs=[full(a) for a in known] + [cut_at(c) for c in range(cuts)],
+        out_specs=[full(shape((tokens, width))), full(sums_shape)],
+        scratch=[pltpu.VMEM((experts, tokens), F32)],
     )
+    flat_rows, active = after((flat_rows, active), sums)
     gate_wgrad = t_dot(flat_rows, gate_part).astype(BF16)
     up_wgrad = t_dot(flat_rows, up_part).astype(BF16)
     down_wgrad = t_dot(active, scaled).astype(BF16)
-    outs = exchange(after(outs, grads, gate_wgrad, up_wgrad, down_wgrad), "outs")
-
-    grad_in, sums = call(
-        partial(source_kernel, top),
-        "source",
-        [block, shape((-(-(experts + 1) // 8) * 8, width), F32)],
-        [rank, grads, table, lifted, router_t, normed, xp, dy_in, gain_row],
-        scratch=[
-            pltpu.VMEM((count, tokens), BF16),
-            pltpu.VMEM((experts, tokens), F32),
-        ],
-    )
     sums = swap([sums] * half, "sums")
     while len(sums) > 1:
         sums = [a + b for a, b in zip(sums[::2], sums[1::2])]
-    sums = sums[0] + hop(sums[0], 0, half, "sums_far")
-    (spread,) = call(
-        partial(spread_kernel, slots),
-        "spread",
-        [shape((tokens, count))],
-        [frank, fweight],
-        scratch=[pltpu.VMEM((count, tokens), F32)],
-    )
+    far_sums = hop(sums[0], 0, half, "sums_far")
+    (grad_in,) = call(source_kernel, "source", [block], [dnormed, xp, dy_in, gain_row])
     forward = (x_in.astype(F32) + dot(spread, outs.reshape(count, width))).astype(BF16)
+    far_sums, forward = lax.optimization_barrier((far_sums, forward))
+    sums = sums[0] + far_sums
     return (
         forward[None],
         grad_in[None],

time: 328 us -> 318 us (0.970)
  waiting for transfers between devices: 180 us -> 162 us
  Pallas kernels: 69.1 us -> 79.8 us
  starting transfers between devices: 41.4 us -> 48.3 us
  local copies, waits for them, and re-layouts: 15.4 us -> 9.79 us
    all_to_all x4 -> x3, waiting for transfers between devices: 64.3 us -> 10.7 us  [exchange(): lax.all_to_all(array, 'expert', 0, 0, tiled=True, axis_index_groups=groups)]
    ppermute x12 -> x18, waiting for transfers between devices: 111 us -> 140 us  [hop(): lax.ppermute(block, 'expert', [(e, e ^ flip) for e in range(experts)])]
    pallas_call x0 -> x2, Pallas kernels: none -> 16.9 us  [forward_of(): pl.pallas_call(partial(forward_kernel, half), out_shape=message, grid_spe...]
    ppermute x12 -> x18, starting transfers between devices: 21.1 us -> 28.4 us  [hop(): lax.ppermute(block, 'expert', [(e, e ^ flip) for e in range(experts)])]
    pallas_call x10 -> x12, Pallas kernels: 69.1 us -> 62.8 us  [call(): pl.pallas_call(kernel, out_shape=[jax.ShapeDtypeStruct(o.shape, o.dtype)...]
    ppermute x2 -> x3, waiting for transfers between devices: 4.76 us -> 10.8 us  [hop(): return lax.ppermute(block, ('pipe', 'expert'), route)]
    unnamed x34 -> x40, local copies, waits for them, and re-layouts: 7.41 us -> 4.16 us
    all_to_all x4 -> x3, starting transfers between devices: 17.8 us -> 15.6 us  [exchange(): lax.all_to_all(array, 'expert', 0, 0, tiled=True, axis_index_groups=groups)]
  transfers between devices with their start and end apart: 18 -> 24, of which waited for: 13 -> 13; matrix products, arithmetic and copies ran while one was open for 8% -> 7% of each run, Pallas kernels for 21% -> 25%
where the time goes in v2:
time: 318 us
  waiting for transfers between devices  162 us (51%)
  Pallas kernels  79.8 us (25%)
  starting transfers between devices  48.3 us (15%)
  matrix products  16 us (5%)
  local copies, waits for them, and re-layouts  9.79 us (3%)
    ppermute x18, waiting for transfers between devices, hop(): lax.ppermute(block, 'expert', [(e, e ^ flip) for e in range(experts)])  140 us
    pallas_call x12, Pallas kernels, call(): pl.pallas_call(kernel, out_shape=[jax.ShapeDtypeStruct(o.shape, o.dtype)...  62.8 us
    ppermute x18, starting transfers between devices, hop(): lax.ppermute(block, 'expert', [(e, e ^ flip) for e in range(experts)])  28.4 us
    pallas_call x2, Pallas kernels, forward_of(): pl.pallas_call(partial(forward_kernel, half), out_shape=message, grid_spe...  16.9 us
    all_to_all x3, starting transfers between devices, exchange(): lax.all_to_all(array, 'expert', 0, 0, tiled=True, axis_index_groups=groups)  15.6 us
    dot_general x3, matrix products, t_dot(): lax.dot_general(a, b, dims, preferred_element_type=F32, precision=precision)  12 us
    ppermute x3, waiting for transfers between devices, hop(): return lax.ppermute(block, ('pipe', 'expert'), route)  10.8 us
    all_to_all x3, waiting for transfers between devices, exchange(): lax.all_to_all(array, 'expert', 0, 0, tiled=True, axis_index_groups=groups)  10.7 us
  transfers between devices with their start and end apart: 24, of which 13 were waited for; matrix products, arithmetic and copies ran while one was open for 7% of the time, Pallas kernels for 25%

profile of v2, /device:TPU:0, one launch (start us, length us, event | category | flops | bytes accessed | tf_op | source)
XLA Modules:
  0.0 317.6 jit_solution(9918090306902773261)
XLA Ops:
  0.6 2.5 collective-permute-start
  3.1 2.6 collective-permute-start.1
  5.7 1.3 pad_add_fusion.table_ref.refs_4_.refs_2_
  7.0 1.5 ranks.1
  8.6 4.6 %own_rows.1 = (bf16[80,2176]{1,0:T(8,128)(2,1)}, bf16[80,2176]{1,0:T(8,128)(2,1)}, bf16[80,2176]{1,0:T(8,128)(2,1)}, bf16[80,2176]{1,0:T(8,128)(2,1)}, f32[8,256...) custom-call(s32[1]{0:T(128)} %bitcast.4.refs_0_.me_ref, bf16[256,2048]{1,0:T(8,128)(2,1)} %bitcast.57, ...), custom_call_target="tpu_custom_call" | custom-call | bytes 55552 | tf_op jit(solution)/shard_map/own_rows/pallas_call | solution.py:55
  13.2 1.5 collective-permute-start.3
  14.7 1.6 collective-permute-start.4
  16.3 0.4 collective-permute-start.5
  16.7 1.6 collective-permute-start.2
  18.3 4.3 %cots.1 = bf16[8,80,2048]{2,1,0:T(8,128)(2,1)} custom-call(s32[8,256]{1,0:T(8,128)} %get-tuple-element.46.rank_ref.refs_5_.refs_0_, bf16[256,2048]{1,0:T(8,128)(2,1)} %copy-done.2), custom_call_target="tpu_custom_call" | custom-call | bytes 57472 | tf_op jit(solution)/shard_map/cots/pallas_call | solution.py:55
  22.6 29.0 %collective-permute-done.2.table_ref.refs_4_ = s32[6,256]{1,0:T(8,128)S(1)} collective-permute-done((s32[6,256]{1,0:T(8,128)}, s32[6,256]{1,0:T(8,128)S(1)}, u32[]{:S(2)}, u32[]{:S(2)}) %collective-permute-start.2) | collective-permute-done | bytes 6176 | tf_op jit(solution)/shard_map/tables/ppermute | solution.py:22
  51.7 1.3 collective-permute-done.5.refs_11_
  52.9 0.7 copy-done.10
  53.7 0.3 copy-done.4
  54.0 4.7 %all-to-all-start = ((bf16[8,80,2048]{2,1,0:T(8,128)(2,1)}), bf16[8,80,2048]{2,1,0:T(8,128)(2,1)S(1)}, u32[]{:S(2)}, u32[]{:S(2)}) async-start(bf16[8,80,2048]{2,1,0:T(8,128)(2,1)} %cots.1), calls=%async_computation | async-start | bytes 5242880 | tf_op jit(solution)/shard_map/cots/all_to_all | solution.py:325
  58.7 1.6 far_ranks.1
  60.2 4.6 %far_rows.1 = (bf16[80,2176]{1,0:T(8,128)(2,1)}, bf16[80,2176]{1,0:T(8,128)(2,1)}, bf16[80,2176]{1,0:T(8,128)(2,1)}, bf16[80,2176]{1,0:T(8,128)(2,1)}) custom-call(s32[1]{0:T(128)} %bitcast.4.refs_0_.me_ref, bf16[256,2048]{1,0:T(8,128)(2,1)} %copy-done.4, f32[1,2048]{1,0:T(1,128)} %gain_ref.1, bf16[8,2048]{1,0:T(8,128)(2,1)} %bitcast.70, ...), custom_call_target="tpu_custom_call" | custom-call | bytes 39008 | tf_op jit(solution)/shard_map/far_rows/pallas_call | solution.py:55
  64.8 2.0 collective-permute-start.6
  66.9 1.5 collective-permute-start.7
  68.3 20.4 %collective-permute-done.6.refs_13_ = bf16[80,2176]{1,0:T(8,128)(2,1)S(1)} collective-permute-done((bf16[80,2176]{1,0:T(8,128)(2,1)}, bf16[80,2176]{1,0:T(8,128)(2,1)S(1)}, u32[]{:S(2)}, u32[]{:S(2)}) %collective-permute-start.6) | collective-permute-done | bytes 348192 | tf_op jit(solution)/shard_map/far_rows/ppermute | solution.py:22
  88.7 22.1 %collective-permute-done.7.refs_14_ = bf16[80,2176]{1,0:T(8,128)(2,1)S(1)} collective-permute-done((bf16[80,2176]{1,0:T(8,128)(2,1)}, bf16[80,2176]{1,0:T(8,128)(2,1)S(1)}, u32[]{:S(2)}, u32[]{:S(2)}) %collective-permute-start.7) | collective-permute-done | bytes 348192 | tf_op jit(solution)/shard_map/far_rows/ppermute | solution.py:22
  110.8 0.8 copy-done.12
  111.5 5.6 %collective-permute-done.8.refs_15_ = bf16[80,2176]{1,0:T(8,128)(2,1)} collective-permute-done((bf16[80,2176]{1,0:T(8,128)(2,1)}, bf16[80,2176]{1,0:T(8,128)(2,1)}, u32[]{:S(2)}, u32[]{:S(2)}) %collective-permute-start.8) | collective-permute-done | bytes 348192 | tf_op jit(solution)/shard_map/far_rows/ppermute | solution.py:22
  117.1 1.0 all-to-all-done.refs_7_
  118.2 1.8 collective-permute-start.9
  120.0 4.1 %fown_rows.1 = (bf16[80,2048]{1,0:T(8,128)(2,1)}, bf16[80,2048]{1,0:T(8,128)(2,1)}, bf16[80,2048]{1,0:T(8,128)(2,1)}, bf16[80,2048]{1,0:T(8,128)(2,1)}, f32[8,256]{1,0:T(8,128)}) custom-call(s32[1]{0:T(128)} %bitcast.4.refs_0_.me_ref, bf16[256,2048]{1,0:T(8,128)(2,1)} %collective-permute-done.10.refs_1_, f32[1,2048]{1,0:T(1,128)} %gain_ref.1, ...), custom_call_target="tpu_custom_call" | custom-call | bytes 37856 | tf_op jit(solution)/shard_map/fown_rows/pallas_call | solution.py:55
  124.1 0.6 collective-permute-start.11
  124.7 1.5 collective-permute-start.12
  126.2 1.4 collective-permute-start.13
  127.6 0.6 broadcast_in_dim.21.weight_ref
  128.2 1.6 hot.1.refs_1_
  129.8 1.6 spread.1
  131.5 24.7 %expert.1 = (bf16[640,2176]{1,0:T(8,128)(2,1)}, bf16[640,2048]{1,0:T(8,128)(2,1)}, bf16[640,2048]{1,0:T(8,128)(2,1)}, bf16[3,640,256]{2,1,0:T(8,128)(2,1)}, bf16...) custom-call(s32[1]{0:T(128)} %bitcast.4.refs_0_.me_ref, bf16[2048,768]{1,0:T(8,128)(2,1)} %bitcast.44, ...), custom_call_target="tpu_custom_call" | custom-call | flops 188743680 | bytes 550912 | tf_op jit(solution)/shard_map/expert/pallas_call | solution.py:55
  156.1 10.8 %collective-permute-done.9.refs_1_ = bf16[256,2048]{1,0:T(8,128)(2,1)} collective-permute-done((bf16[256,2048]{1,0:T(8,128)(2,1)}, bf16[256,2048]{1,0:T(8,128)(2,1)}, u32[]{:S(2)}, u32[]{:S(2)}) %collective-permute-start.9) | collective-permute-done | bytes 1048608 | tf_op jit(solution)/shard_map/x_far/ppermute | solution.py:28
  167.0 5.2 %all-to-all-start.1 = ((bf16[8,80,2176]{2,1,0:T(8,128)(2,1)}), bf16[8,80,2176]{2,1,0:T(8,128)(2,1)S(1)}, u32[]{:S(2)}, u32[]{:S(2)}) async-start(bf16[8,80,2176]{2,1,0:T(8,128)(2,1)} %bitcast.60), calls=%async_computation.1 | async-start | bytes 5570560 | tf_op jit(solution)/shard_map/grads/all_to_all | solution.py:325
  172.2 3.9 %ffar_rows.1 = (bf16[80,2048]{1,0:T(8,128)(2,1)}, bf16[80,2048]{1,0:T(8,128)(2,1)}, bf16[80,2048]{1,0:T(8,128)(2,1)}, bf16[80,2048]{1,0:T(8,128)(2,1)}) custom-call(s32[1]{0:T(128)} %bitcast.4.refs_0_.me_ref, bf16[256,2048]{1,0:T(8,128)(2,1)} %collective-permute-done.9.refs_1_, f32[1,2048]{1,0:T(1,128)} %gain_ref.1, bf16[8,2048]{1,0:T(8,128)(2,1)} %bitcast.72, ...), custom_call_target="tpu_custom_call" | custom-call | bytes 37728 | tf_op jit(solution)/shard_map/ffar_rows/pallas_call | solution.py:55
  176.1 2.0 collective-permute-start.18
  178.1 1.5 collective-permute-start.19
  179.6 8.5 %forward_own.1.refs_4_ = bf16[8,80,2048]{2,1,0:T(8,128)(2,1)} custom-call(s32[1]{0:T(128)} %bitcast.4.refs_0_.me_ref, bf16[2048,768]{1,0:T(8,128)(2,1)} %bitcast.46, bf16[2048,768]{1,0:T(8,128)(2,1)} %bitcast.50, bf16[768,2048]{1,0:T(8,128)(2,1)} %bitcast.54, bf16[80,2048]{1,0:T(8,128)(2,1)} %get-tuple-element.73.refs_0_, ...), custom_call_target="tpu_custom_call" | custom-call | flops 3019898880 | bytes 9437184 | tf_op jit(solution)/shard_map/forward_own/pallas_call | solution.py:432
  188.1 15.3 %collective-permute-done.18.refs_1_ = bf16[80,2048]{1,0:T(8,128)(2,1)S(1)} collective-permute-done((bf16[80,2048]{1,0:T(8,128)(2,1)}, bf16[80,2048]{1,0:T(8,128)(2,1)S(1)}, u32[]{:S(2)}, u32[]{:S(2)}) %collective-permute-start.18) | collective-permute-done | bytes 327712 | tf_op jit(solution)/shard_map/ffar_rows/ppermute | solution.py:22
  203.3 22.9 %collective-permute-done.19.refs_2_ = bf16[80,2048]{1,0:T(8,128)(2,1)S(1)} collective-permute-done((bf16[80,2048]{1,0:T(8,128)(2,1)}, bf16[80,2048]{1,0:T(8,128)(2,1)S(1)}, u32[]{:S(2)}, u32[]{:S(2)}) %collective-permute-start.19) | collective-permute-done | bytes 327712 | tf_op jit(solution)/shard_map/ffar_rows/ppermute | solution.py:22
  226.2 6.1 %collective-permute-done.20.refs_3_ = bf16[80,2048]{1,0:T(8,128)(2,1)S(1)} collective-permute-done((bf16[80,2048]{1,0:T(8,128)(2,1)}, bf16[80,2048]{1,0:T(8,128)(2,1)S(1)}, u32[]{:S(2)}, u32[]{:S(2)}) %collective-permute-start.20) | collective-permute-done | bytes 327712 | tf_op jit(solution)/shard_map/ffar_rows/ppermute | solution.py:22
  232.3 0.7 copy-done.15
  233.0 8.4 %forward_far.1 = bf16[8,80,2048]{2,1,0:T(8,128)(2,1)} custom-call(s32[1]{0:T(128)} %bitcast.4.refs_0_.me_ref, bf16[2048,768]{1,0:T(8,128)(2,1)} %bitcast.47, bf16[2048,768]{1,0:T(8,128)(2,1)} %bitcast.51, bf16[768,2048]{1,0:T(8,128)(2,1)} %bitcast.55, bf16[80,2048]{1,0:T(8,128)(2,1)} %get-tuple-element.69.refs_0_, ...), custom_call_target="tpu_custom_call", output_to_operand_aliasing={{}: (8, {})} | custom-call | flops 3019898880 | bytes 9437184 | tf_op jit(solution)/shard_map/forward_far/pallas_call | solution.py:432
  241.5 1.5 copy-done
  243.0 5.8 %all-to-all-start.2 = ((bf16[8,80,2048]{2,1,0:T(8,128)(2,1)}), bf16[8,80,2048]{2,1,0:T(8,128)(2,1)}, u32[]{:S(2)}, u32[]{:S(2)}) async-start(bf16[8,80,2048]{2,1,0:T(8,128)(2,1)} %forward_far.1), calls=%async_computation.2 | async-start | bytes 5242880 | tf_op jit(solution)/shard_map/outs/all_to_all | solution.py:325
  248.8 1.7 copy.20
  250.5 1.4 copy.21
  251.9 0.7 copy.22
  252.7 6.0 %sums.1 = (f32[256,2048]{1,0:T(8,128)}, f32[16,2048]{1,0:T(8,128)}) custom-call(s32[8,256]{1,0:T(8,128)} %get-tuple-element.46.rank_ref.refs_5_.refs_0_, bf16[256,640]{1,0:T(8,128)(2,1)} %hot.1.refs_1_, s32[6,256]{1,0:T(8,128)} %pad_add_fusion.table_ref.refs_4_.refs_2_, f32[2,256]{1,0:T(2,128)} %get-tuple-element.47.refs_3_, bf16[8,2048]{1,0:T(8,128)(2,1)} %bitcast.73, ...), custom_call_target="tpu_custom_call" | custom-call | bytes 247552 | tf_op jit(solution)/shard_map/sums/pallas_call | solution.py:55
  258.7 2.4 collective-permute-start.15
  261.1 1.0 collective-permute-start.16
  262.2 0.5 collective-permute-start.14
  262.7 4.0 %fusion = bf16[1,1,2048,768]{3,2,1,0:T(8,128)(2,1)} fusion(bf16[640,2048]{1,0:T(8,128)(2,1)S(1)} %copy-done.19, bf16[640,768]{0,1:T(8,128)(2,1)S(1)} %bitcast.68), kind=kOutput, calls=%fused_computation.3 | convolution fusion | flops 2014838784 | bytes 6750208 | tf_op jit(solution)/shard_map/dot_general | solution.py:45
  266.7 4.0 %fusion.1 = bf16[1,1,2048,768]{3,2,1,0:T(8,128)(2,1)} fusion(bf16[640,2048]{1,0:T(8,128)(2,1)S(1)} %copy-done.19, bf16[640,768]{0,1:T(8,128)(2,1)S(1)} %bitcast.67), kind=kOutput, calls=%fused_computation.4 | convolution fusion | flops 2014838784 | bytes 6750208 | tf_op jit(solution)/shard_map/dot_general | solution.py:45
  270.7 4.0 %fusion.2 = bf16[1,1,768,2048]{3,2,1,0:T(8,128)(2,1)} fusion(bf16[640,768]{0,1:T(8,128)(2,1)S(1)} %bitcast.66, bf16[640,2048]{1,0:T(8,128)(2,1)S(1)} %copy-done.18), kind=kOutput, calls=%fused_computation.5 | convolution fusion | flops 2014838784 | bytes 6750208 | tf_op jit(solution)/shard_map/dot_general | solution.py:45
  274.7 4.1 %source.1 = bf16[256,2048]{1,0:T(8,128)(2,1)} custom-call(f32[256,2048]{1,0:T(8,128)} %get-tuple-element.76.dnormed_ref, bf16[256,2048]{1,0:T(8,128)(2,1)} %bitcast.59, bf16[256,2048]{1,0:T(8,128)(2,1)} %copy-done.2, f32[1,2048]{1,0:T(1,128)} %gain_ref.1), custom_call_target="tpu_custom_call" | custom-call | bytes 82048 | tf_op jit(solution)/shard_map/source/pallas_call | solution.py:55
  278.8 16.1 %collective-permute-done.15 = f32[16,2048]{1,0:T(8,128)S(1)} collective-permute-done((f32[16,2048]{1,0:T(8,128)}, f32[16,2048]{1,0:T(8,128)S(1)}, u32[]{:S(2)}, u32[]{:S(2)}) %collective-permute-start.15) | collective-permute-done | bytes 131104 | tf_op jit(solution)/shard_map/sums/ppermute | solution.py:22
  295.0 1.4 collective-permute-done.16
  296.4 6.3 %collective-permute-start.17 = (f32[16,2048]{1,0:T(8,128)S(1)}, f32[16,2048]{1,0:T(8,128)S(1)}, u32[]{:S(2)}, u32[]{:S(2)}) collective-permute-start(f32[16,2048]{1,0:T(8,128)S(1)} %add_add_fusion), channel_id=1, source_target_pairs={{0,4},{1,5},{2,6},{3,7},{4,0},{5,1},{6,2},{7,3},{8,12},{9,13},{10,... | collective-permute-start | bytes 393224 | tf_op jit(solution)/shard_map/sums_far/ppermute | solution.py:22
  302.7 9.7 %all-to-all-done.2 = bf16[8,80,2048]{2,1,0:T(8,128)(2,1)} async-done(((bf16[8,80,2048]{2,1,0:T(8,128)(2,1)}), bf16[8,80,2048]{2,1,0:T(8,128)(2,1)}, u32[]{:S(2)}, u32[]{:S(2)}) %all-to-all-start.2) | async-done | bytes 2621472 | tf_op jit(solution)/shard_map/outs/all_to_all | solution.py:325
  312.4 4.0 %add_convert_fusion = bf16[256,2048]{1,0:T(8,128)(2,1)} fusion(bf16[256,2048]{1,0:T(8,128)(2,1)} %collective-permute-done.10.refs_1_, bf16[256,640]{1,0:T(8,128)(2,1)S(1)} %copy-done.3, bf16[640,2048]{1,0:T(8,128)(2,1)} %bitcast.15), kind=kOutput, calls=%fused_computation.6 | convolution fusion | flops 672661504 | bytes 5046272 | tf_op jit(solution)/shard_map/dot_general | solution.py:36
  316.4 0.6 slice_bitcast_fusion
  317.0 0.6 slice.9
  (51 shorter events, 0.2 us)
Async XLA Ops:
  0.6 16.1 %collective-permute-start = (bf16[256,2048]{1,0:T(8,128)(2,1)}, bf16[256,2048]{1,0:T(8,128)(2,1)S(1)}, u32[]{:S(2)}, u32[]{:S(2)}) collective-permute-start(bf16[256,2048]{1,0:T(8,128)(2,1)} %bitcast.76), channel_id=1, source_target_pairs={{0,24},{1,25},{2,26},{3,27},{4,28},{5,29},{6,30},{7,31},{8,0},{9,1... | collective-permute-start | bytes 3145736 | tf_op jit(solution)/shard_map/dy_in/ppermute | solution.py:28
  3.1 49.8 %collective-permute-start.1 = (bf16[256,2048]{1,0:T(8,128)(2,1)}, bf16[256,2048]{1,0:T(8,128)(2,1)S(1)}, u32[]{:S(2)}, u32[]{:S(2)}) collective-permute-start(bf16[256,2048]{1,0:T(8,128)(2,1)} %bitcast.56), channel_id=1, source_target_pairs={{0,4},{1,5},{2,6},{3,7},{4,0},{5,1},{6,2},{7,3},{8,12},{9,13},{10,... | collective-permute-start | bytes 3145736 | tf_op jit(solution)/shard_map/xp_far/ppermute | solution.py:22
  13.2 38.4 %collective-permute-start.3 = (bf16[80,2176]{1,0:T(8,128)(2,1)}, bf16[80,2176]{1,0:T(8,128)(2,1)S(1)}, u32[]{:S(2)}, u32[]{:S(2)}) collective-permute-start(bf16[80,2176]{1,0:T(8,128)(2,1)} %get-tuple-element.49), channel_id=1, source_target_pairs={{0,1},{1,0},{2,3},{3,2},{4,5},{5,4},{6,7},{7,6},{8,9},{9,8},{10,11... | collective-permute-start | bytes 1044488 | tf_op jit(solution)/shard_map/own_rows/ppermute | solution.py:22
  14.7 37.0 %collective-permute-start.4 = (bf16[80,2176]{1,0:T(8,128)(2,1)}, bf16[80,2176]{1,0:T(8,128)(2,1)S(1)}, u32[]{:S(2)}, u32[]{:S(2)}) collective-permute-start(bf16[80,2176]{1,0:T(8,128)(2,1)} %get-tuple-element.50), channel_id=1, source_target_pairs={{0,2},{1,3},{2,0},{3,1},{4,6},{5,7},{6,4},{7,5},{8,10},{9,11},{10,... | collective-permute-start | bytes 1044488 | tf_op jit(solution)/shard_map/own_rows/ppermute | solution.py:22
  16.3 36.6 %collective-permute-start.5 = (bf16[80,2176]{1,0:T(8,128)(2,1)}, bf16[80,2176]{1,0:T(8,128)(2,1)S(1)}, u32[]{:S(2)}, u32[]{:S(2)}) collective-permute-start(bf16[80,2176]{1,0:T(8,128)(2,1)} %get-tuple-element.51), channel_id=1, source_target_pairs={{0,3},{1,2},{2,1},{3,0},{4,7},{5,6},{6,5},{7,4},{8,11},{9,10},{10,... | collective-permute-start | bytes 1044488 | tf_op jit(solution)/shard_map/own_rows/ppermute | solution.py:22
  16.7 1.6 copy-start.2
  16.7 34.9 %collective-permute-start.2 = (s32[6,256]{1,0:T(8,128)}, s32[6,256]{1,0:T(8,128)S(1)}, u32[]{:S(2)}, u32[]{:S(2)}) collective-permute-start(s32[6,256]{1,0:T(8,128)} %pad_add_fusion.table_ref.refs_4_.refs_2_), channel_id=1, source_target_pairs={{0,4},{1,5},{2,6},{3,7},{4,0},{5,1},{6,2},{7,3},{8,12},{9,13},{10,... | collective-permute-start | bytes 18440 | tf_op jit(solution)/shard_map/tables/ppermute | solution.py:22
  51.6 7.0 %copy-start.17 = (s32[6,256]{1,0:T(8,128)}, s32[6,256]{1,0:T(8,128)S(1)}, u32[]{:S(2)}) copy-start(s32[6,256]{1,0:T(8,128)S(1)} %collective-permute-done.2.table_ref.refs_4_) | copy-start | bytes 18436
  51.6 79.8 %copy-start.8 = (bf16[80,2176]{1,0:T(8,128)(2,1)}, bf16[80,2176]{1,0:T(8,128)(2,1)S(1)}, u32[]{:S(2)}) copy-start(bf16[80,2176]{1,0:T(8,128)(2,1)S(1)} %collective-permute-done.3.refs_9_) | copy-start | bytes 1044484
  51.6 79.8 %copy-start.9 = (bf16[80,2176]{1,0:T(8,128)(2,1)}, bf16[80,2176]{1,0:T(8,128)(2,1)S(1)}, u32[]{:S(2)}) copy-start(bf16[80,2176]{1,0:T(8,128)(2,1)S(1)} %collective-permute-done.4.refs_10_) | copy-start | bytes 1044484
  52.9 0.7 copy-start.10
  52.9 1.1 copy-start.4
  54.0 64.2 %all-to-all-start = ((bf16[8,80,2048]{2,1,0:T(8,128)(2,1)}), bf16[8,80,2048]{2,1,0:T(8,128)(2,1)S(1)}, u32[]{:S(2)}, u32[]{:S(2)}) async-start(bf16[8,80,2048]{2,1,0:T(8,128)(2,1)} %cots.1), calls=%async_computation | async-start | bytes 5242880 | tf_op jit(solution)/shard_map/cots/all_to_all | solution.py:325
  64.8 23.9 %collective-permute-start.6 = (bf16[80,2176]{1,0:T(8,128)(2,1)}, bf16[80,2176]{1,0:T(8,128)(2,1)S(1)}, u32[]{:S(2)}, u32[]{:S(2)}) collective-permute-start(bf16[80,2176]{1,0:T(8,128)(2,1)} %get-tuple-element.56), channel_id=1, source_target_pairs={{0,1},{1,0},{2,3},{3,2},{4,5},{5,4},{6,7},{7,6},{8,9},{9,8},{10,11... | collective-permute-start | bytes 1044488 | tf_op jit(solution)/shard_map/far_rows/ppermute | solution.py:22
  66.9 43.9 %collective-permute-start.7 = (bf16[80,2176]{1,0:T(8,128)(2,1)}, bf16[80,2176]{1,0:T(8,128)(2,1)S(1)}, u32[]{:S(2)}, u32[]{:S(2)}) collective-permute-start(bf16[80,2176]{1,0:T(8,128)(2,1)} %get-tuple-element.57), channel_id=1, source_target_pairs={{0,2},{1,3},{2,0},{3,1},{4,6},{5,7},{6,4},{7,5},{8,10},{9,11},{10,... | collective-permute-start | bytes 1044488 | tf_op jit(solution)/shard_map/far_rows/ppermute | solution.py:22
  68.3 48.8 %collective-permute-start.8 = (bf16[80,2176]{1,0:T(8,128)(2,1)}, bf16[80,2176]{1,0:T(8,128)(2,1)}, u32[]{:S(2)}, u32[]{:S(2)}) collective-permute-start(bf16[80,2176]{1,0:T(8,128)(2,1)} %get-tuple-element.58), channel_id=1, source_target_pairs={{0,3},{1,2},{2,1},{3,0},{4,7},{5,6},{6,5},{7,4},{8,11},{9,10},{10,... | collective-permute-start | bytes 1044488 | tf_op jit(solution)/shard_map/far_rows/ppermute | solution.py:22
  68.3 51.6 %collective-permute-start.10 = (bf16[256,2048]{1,0:T(8,128)(2,1)}, bf16[256,2048]{1,0:T(8,128)(2,1)}, u32[]{:S(2)}, u32[]{:S(2)}) collective-permute-start(bf16[256,2048]{1,0:T(8,128)(2,1)} %bitcast.77), channel_id=1, source_target_pairs={{0,8},{1,9},{2,10},{3,11},{4,12},{5,13},{6,14},{7,15},{8,16},{9,17... | collective-permute-start | bytes 3145736 | tf_op jit(solution)/shard_map/x_in/ppermute | solution.py:28
  88.7 22.1 %copy-start.11 = (bf16[80,2176]{1,0:T(8,128)(2,1)}, bf16[80,2176]{1,0:T(8,128)(2,1)S(1)}, u32[]{:S(2)}) copy-start(bf16[80,2176]{1,0:T(8,128)(2,1)S(1)} %collective-permute-done.6.refs_13_) | copy-start | bytes 1044484
  110.8 0.8 copy-start.12
  118.2 13.3 %copy-start.1 = (bf16[8,80,2048]{2,1,0:T(8,128)(2,1)}, bf16[8,80,2048]{2,1,0:T(8,128)(2,1)S(1)}, u32[]{:S(2)}) copy-start(bf16[8,80,2048]{2,1,0:T(8,128)(2,1)S(1)} %all-to-all-done.refs_7_) | copy-start | bytes 7864324
  118.2 48.8 %collective-permute-start.9 = (bf16[256,2048]{1,0:T(8,128)(2,1)}, bf16[256,2048]{1,0:T(8,128)(2,1)}, u32[]{:S(2)}, u32[]{:S(2)}) collective-permute-start(bf16[256,2048]{1,0:T(8,128)(2,1)} %bitcast.78), channel_id=1, source_target_pairs={{0,12},{1,13},{2,14},{3,15},{4,8},{5,9},{6,10},{7,11},{8,20},{9,21... | collective-permute-start | bytes 3145736 | tf_op jit(solution)/shard_map/x_far/ppermute | solution.py:28
  124.1 32.0 %collective-permute-start.11 = (bf16[80,2048]{1,0:T(8,128)(2,1)}, bf16[80,2048]{1,0:T(8,128)(2,1)}, u32[]{:S(2)}, u32[]{:S(2)}) collective-permute-start(bf16[80,2048]{1,0:T(8,128)(2,1)} %get-tuple-element.63), channel_id=1, source_target_pairs={{0,1},{1,0},{2,3},{3,2},{4,5},{5,4},{6,7},{7,6},{8,9},{9,8},{10,11... | collective-permute-start | bytes 983048 | tf_op jit(solution)/shard_map/fown_rows/ppermute | solution.py:22
  124.7 31.4 %collective-permute-start.12 = (bf16[80,2048]{1,0:T(8,128)(2,1)}, bf16[80,2048]{1,0:T(8,128)(2,1)}, u32[]{:S(2)}, u32[]{:S(2)}) collective-permute-start(bf16[80,2048]{1,0:T(8,128)(2,1)} %get-tuple-element.64), channel_id=1, source_target_pairs={{0,2},{1,3},{2,0},{3,1},{4,6},{5,7},{6,4},{7,5},{8,10},{9,11},{10,... | collective-permute-start | bytes 983048 | tf_op jit(solution)/shard_map/fown_rows/ppermute | solution.py:22
  126.2 30.0 %collective-permute-start.13 = (bf16[80,2048]{1,0:T(8,128)(2,1)}, bf16[80,2048]{1,0:T(8,128)(2,1)}, u32[]{:S(2)}, u32[]{:S(2)}) collective-permute-start(bf16[80,2048]{1,0:T(8,128)(2,1)} %get-tuple-element.65), channel_id=1, source_target_pairs={{0,3},{1,2},{2,1},{3,0},{4,7},{5,6},{6,5},{7,4},{8,11},{9,10},{10,... | collective-permute-start | bytes 983048 | tf_op jit(solution)/shard_map/fown_rows/ppermute | solution.py:22
  167.0 74.5 %all-to-all-start.1 = ((bf16[8,80,2176]{2,1,0:T(8,128)(2,1)}), bf16[8,80,2176]{2,1,0:T(8,128)(2,1)S(1)}, u32[]{:S(2)}, u32[]{:S(2)}) async-start(bf16[8,80,2176]{2,1,0:T(8,128)(2,1)} %bitcast.60), calls=%async_computation.1 | async-start | bytes 5570560 | tf_op jit(solution)/shard_map/grads/all_to_all | solution.py:325
  176.1 27.2 %collective-permute-start.18 = (bf16[80,2048]{1,0:T(8,128)(2,1)}, bf16[80,2048]{1,0:T(8,128)(2,1)S(1)}, u32[]{:S(2)}, u32[]{:S(2)}) collective-permute-start(bf16[80,2048]{1,0:T(8,128)(2,1)} %get-tuple-element.70), channel_id=1, source_target_pairs={{0,1},{1,0},{2,3},{3,2},{4,5},{5,4},{6,7},{7,6},{8,9},{9,8},{10,11... | collective-permute-start | bytes 983048 | tf_op jit(solution)/shard_map/ffar_rows/ppermute | solution.py:22
  178.1 48.1 %collective-permute-start.19 = (bf16[80,2048]{1,0:T(8,128)(2,1)}, bf16[80,2048]{1,0:T(8,128)(2,1)S(1)}, u32[]{:S(2)}, u32[]{:S(2)}) collective-permute-start(bf16[80,2048]{1,0:T(8,128)(2,1)} %get-tuple-element.71), channel_id=1, source_target_pairs={{0,2},{1,3},{2,0},{3,1},{4,6},{5,7},{6,4},{7,5},{8,10},{9,11},{10,... | collective-permute-start | bytes 983048 | tf_op jit(solution)/shard_map/ffar_rows/ppermute | solution.py:22
  179.6 52.7 %collective-permute-start.20 = (bf16[80,2048]{1,0:T(8,128)(2,1)}, bf16[80,2048]{1,0:T(8,128)(2,1)S(1)}, u32[]{:S(2)}, u32[]{:S(2)}) collective-permute-start(bf16[80,2048]{1,0:T(8,128)(2,1)} %get-tuple-element.72), channel_id=1, source_target_pairs={{0,3},{1,2},{2,1},{3,0},{4,7},{5,6},{6,5},{7,4},{8,11},{9,10},{10,... | collective-permute-start | bytes 983048 | tf_op jit(solution)/shard_map/ffar_rows/ppermute | solution.py:22
  203.3 29.0 %copy-start.13 = (bf16[80,2048]{1,0:T(8,128)(2,1)}, bf16[80,2048]{1,0:T(8,128)(2,1)S(1)}, u32[]{:S(2)}) copy-start(bf16[80,2048]{1,0:T(8,128)(2,1)S(1)} %collective-permute-done.18.refs_1_) | copy-start | bytes 983044
  226.2 6.1 %copy-start.14 = (bf16[80,2048]{1,0:T(8,128)(2,1)}, bf16[80,2048]{1,0:T(8,128)(2,1)S(1)}, u32[]{:S(2)}) copy-start(bf16[80,2048]{1,0:T(8,128)(2,1)S(1)} %collective-permute-done.19.refs_2_) | copy-start | bytes 983044
  232.3 0.7 copy-start.15
  241.5 1.5 copy-start
  243.0 69.4 %all-to-all-start.2 = ((bf16[8,80,2048]{2,1,0:T(8,128)(2,1)}), bf16[8,80,2048]{2,1,0:T(8,128)(2,1)}, u32[]{:S(2)}, u32[]{:S(2)}) async-start(bf16[8,80,2048]{2,1,0:T(8,128)(2,1)} %forward_far.1), calls=%async_computation.2 | async-start | bytes 5242880 | tf_op jit(solution)/shard_map/outs/all_to_all | solution.py:325
  248.8 1.7 copy-start.6
  248.8 3.1 copy-start.5
  252.6 10.0 %copy-start.7 = (bf16[640,3,256]{0,2,1:T(8,128)(2,1)S(1)}, bf16[640,3,256]{0,2,1:T(8,128)(2,1)}, u32[]{:S(2)}) copy-start(bf16[640,3,256]{0,2,1:T(8,128)(2,1)} %copy.21) | copy-start | bytes 2949124
  252.6 10.0 %copy-start.19 = (bf16[640,2048]{1,0:T(8,128)(2,1)S(1)}, bf16[640,2048]{1,0:T(8,128)(2,1)}, u32[]{:S(2)}) copy-start(bf16[640,2048]{1,0:T(8,128)(2,1)} %get-tuple-element.79) | copy-start | bytes 7864324
  258.7 36.3 %collective-permute-start.15 = (f32[16,2048]{1,0:T(8,128)}, f32[16,2048]{1,0:T(8,128)S(1)}, u32[]{:S(2)}, u32[]{:S(2)}) collective-permute-start(f32[16,2048]{1,0:T(8,128)} %get-tuple-element.67), channel_id=1, source_target_pairs={{0,2},{1,3},{2,0},{3,1},{4,6},{5,7},{6,4},{7,5},{8,10},{9,11},{10,... | collective-permute-start | bytes 393224 | tf_op jit(solution)/shard_map/sums/ppermute | solution.py:22
  261.1 35.2 %collective-permute-start.16 = (f32[16,2048]{1,0:T(8,128)}, f32[16,2048]{1,0:T(8,128)S(1)}, u32[]{:S(2)}, u32[]{:S(2)}) collective-permute-start(f32[16,2048]{1,0:T(8,128)} %get-tuple-element.67), channel_id=1, source_target_pairs={{0,3},{1,2},{2,1},{3,0},{4,7},{5,6},{6,5},{7,4},{8,11},{9,10},{10,... | collective-permute-start | bytes 393224 | tf_op jit(solution)/shard_map/sums/ppermute | solution.py:22
  262.2 34.2 %collective-permute-start.14 = (f32[16,2048]{1,0:T(8,128)}, f32[16,2048]{1,0:T(8,128)S(1)}, u32[]{:S(2)}, u32[]{:S(2)}) collective-permute-start(f32[16,2048]{1,0:T(8,128)} %get-tuple-element.67), channel_id=1, source_target_pairs={{0,1},{1,0},{2,3},{3,2},{4,5},{5,4},{6,7},{7,6},{8,9},{9,8},{10,11... | collective-permute-start | bytes 393224 | tf_op jit(solution)/shard_map/sums/ppermute | solution.py:22
  266.7 4.0 %copy-start.18 = (bf16[640,2048]{1,0:T(8,128)(2,1)S(1)}, bf16[640,2048]{1,0:T(8,128)(2,1)}, u32[]{:S(2)}) copy-start(bf16[640,2048]{1,0:T(8,128)(2,1)} %get-tuple-element.83) | copy-start | bytes 7864324
  274.7 21.7 %copy-start.16 = (f32[16,2048]{1,0:T(8,128)S(1)}, f32[16,2048]{1,0:T(8,128)}, u32[]{:S(2)}) copy-start(f32[16,2048]{1,0:T(8,128)} %get-tuple-element.67) | copy-start | bytes 393220
  274.7 37.7 %copy-start.3 = (bf16[256,640]{1,0:T(8,128)(2,1)S(1)}, bf16[256,640]{1,0:T(8,128)(2,1)}, u32[]{:S(2)}) copy-start(bf16[256,640]{1,0:T(8,128)(2,1)} %spread.1) | copy-start | bytes 983044
  296.4 20.0 %collective-permute-start.17 = (f32[16,2048]{1,0:T(8,128)S(1)}, f32[16,2048]{1,0:T(8,128)S(1)}, u32[]{:S(2)}, u32[]{:S(2)}) collective-permute-start(f32[16,2048]{1,0:T(8,128)S(1)} %add_add_fusion), channel_id=1, source_target_pairs={{0,4},{1,5},{2,6},{3,7},{4,0},{5,1},{6,2},{7,3},{8,12},{9,13},{10,... | collective-permute-start | bytes 393224 | tf_op jit(solution)/shard_map/sums_far/ppermute | solution.py:22

commit v3 on v2

v3 whole, which is shorter than its diff:
```python
import functools

import jax
import jax.numpy as jnp
from jax import lax
from jax.experimental import pallas as pl
from jax.experimental.pallas import tpu as pltpu
from jax.sharding import PartitionSpec as P

EPS = 1e-06
F32 = jnp.float32
BF16 = jnp.bfloat16
VMEM_BYTES = 56 * 1024 * 1024
LANES = 128
SCALE = 64


def hop(block, pipe_step, flip, name):
    pipes, experts = lax.axis_size("pipe"), lax.axis_size("expert")
    with jax.named_scope(name):
        if pipe_step == 0:
            return lax.ppermute(block, "expert", [(e, e ^ flip) for e in range(experts)])
        route = [
            (p * experts + e, ((p + pipe_step) % pipes) * experts + (e ^ flip))
            for p in range(pipes)
            for e in range(experts)
        ]
        return lax.ppermute(block, ("pipe", "expert"), route)


def after(block, *earlier):
    return lax.optimization_barrier((block,) + earlier)[0]


def dot(a, b):
    return jnp.dot(a, b, preferred_element_type=F32)


def dot_t(a, b):
    return lax.dot_general(a, b, (((1,), (1,)), ((), ())), preferred_element_type=F32)


def t_dot(a, b, precision=None):
    dims = (((0,), (0,)), ((), ()))
    return lax.dot_general(a, b, dims, preferred_element_type=F32, precision=precision)


def iota(shape, dim):
    return lax.broadcasted_iota(jnp.int32, shape, dim)


def call(kernel, name, outs, ins, grid=(), in_specs=None, out_specs=None, scratch=(), flops=0):
    whole = pl.BlockSpec(memory_space=pltpu.VMEM)
    moved = sum(a.size * a.dtype.itemsize for a in list(outs) + list(ins))
    return pl.pallas_call(
        kernel,
        out_shape=[jax.ShapeDtypeStruct(o.shape, o.dtype) for o in outs],
        grid=grid,
        in_specs=in_specs or [whole] * len(ins),
        out_specs=out_specs or [whole] * len(outs),
        scratch_shapes=list(scratch),
        compiler_params=pltpu.CompilerParams(vmem_limit_bytes=VMEM_BYTES),
        cost_estimate=pl.CostEstimate(flops=flops // SCALE, bytes_accessed=moved // SCALE, transcendentals=0),
        name=name,
    )(*ins)


def shape(dims, dtype=BF16):
    return jax.ShapeDtypeStruct(tuple(dims), dtype)


def rank_kernel(capacity, top, table_ref, *rank_refs):
    experts, tokens = rank_refs[0].shape
    for batch, rank_ref in enumerate(rank_refs):
        row = 2 * top + batch
        order = jnp.broadcast_to(table_ref[row : row + 1, :], (tokens, tokens))
        before = (order.T < order).astype(F32).astype(BF16)
        chosen = iota((experts, tokens), 0) < 0
        for routes in route_rows(table_ref, batch, top):
            chosen = chosen | (routes == iota((experts, tokens), 0))
        count = dot(chosen.astype(F32).astype(BF16), before)
        rank_ref[...] = jnp.where(chosen & (count < capacity), count.astype(jnp.int32), -1)


def route_rows(ref, batch, top):
    return [ref[batch * top + j : batch * top + j + 1, :] for j in range(top)]


def slot_mask(rank_ref, e, slots):
    rank = rank_ref[e : e + 1, :]
    return iota((slots, rank.shape[1]), 0) == rank


def one_hot(mask):
    return jnp.where(mask, 1.0, 0.0).astype(BF16)


def normalise(x_ref, gain_ref, normed_ref, step=32):
    def part(i, carry):
        rows = pl.ds(pl.multiple_of(i * step, step), step)
        values = x_ref[rows, :].astype(F32)
        scale = lax.rsqrt(jnp.mean(values * values, axis=-1, keepdims=True) + EPS)
        normed_ref[rows, :] = (values * scale * gain_ref[...]).astype(BF16)
        return carry

    lax.fori_loop(0, x_ref.shape[0] // step, part, 0)


def sigmoids(normed_ref, router_ref, routes):
    logits = dot_t(router_ref[...], normed_ref[...])
    everyone = iota(logits.shape, 0)
    picked = [jnp.sum(jnp.where(r == everyone, logits, 0.0), axis=0, keepdims=True) for r in routes]
    return [jax.nn.sigmoid(value) for value in picked]


def side_of(expert, experts, routes, lifted):
    tokens = routes[0].shape[1]
    everyone = iota((experts, tokens), 0)
    total = functools.reduce(jnp.add, lifted)
    slope = jnp.zeros((experts, tokens), F32)
    mine = jnp.zeros((1, tokens), F32)
    for r, value in zip(routes, lifted):
        slope = slope + jnp.where(r == everyone, value * (1.0 - value), 0.0)
        mine = mine + jnp.where(r == expert, value, 0.0)
    acts = slope * (jnp.where(everyone == expert, 1.0 / total, 0.0) - mine / (total * total))
    high = acts.astype(BF16).astype(F32)
    weight = jnp.broadcast_to(mine / total, (LANES - 2 * experts, tokens))
    return jnp.concatenate([high, acts - high, weight], axis=0).astype(BF16)


def put_pieces(me_ref, rank_ref, block_ref, pieces, routes=None, lifted=None):
    width = block_ref.shape[1]
    for k, piece in enumerate(pieces):
        expert = me_ref[0] ^ k
        rank = rank_ref[pl.ds(expert, 1), :]
        hot = one_hot(iota((piece.shape[0], rank.shape[1]), 0) == rank)
        piece[:, :width] = dot(hot, block_ref[...]).astype(BF16)
        if lifted:
            side = side_of(expert, rank_ref.shape[0], routes, lifted)
            piece[:, width:] = dot_t(hot, side).astype(BF16)


def back_rows_kernel(half, top, *refs):
    me_ref, x_ref, gain_ref, router_ref, table_ref, rank_ref = refs[:6]
    pieces, normed_ref = refs[6:-1], refs[-1]
    normalise(x_ref, gain_ref, normed_ref)
    routes = route_rows(table_ref, 1, top)
    lifted = sigmoids(normed_ref, router_ref, routes)
    put_pieces(me_ref, rank_ref, normed_ref, pieces, routes, lifted)


def next_rows_kernel(half, top, *refs):
    me_ref, x_ref, gain_ref, router_ref, table_ref, rank_ref = refs[:6]
    pieces, weight_ref, normed_ref = refs[6 : 6 + half], refs[6 + half], refs[-1]
    normalise(x_ref, gain_ref, normed_ref)
    put_pieces(me_ref, rank_ref, normed_ref, pieces)
    routes = route_rows(table_ref, 0, top)
    lifted = sigmoids(normed_ref, router_ref, routes)
    total = functools.reduce(jnp.add, lifted)
    weight = jnp.zeros(weight_ref.shape, F32)
    for r, value in zip(routes, lifted):
        weight = weight + jnp.where(r == iota(weight.shape, 0), value / total, 0.0)
    weight_ref[...] = weight


def cots_kernel(rank_ref, x_ref, message_ref):
    for e in range(message_ref.shape[0]):
        hot = one_hot(slot_mask(rank_ref, e, message_ref.shape[1]))
        message_ref[e] = dot(hot, x_ref[...]).astype(BF16)


def flat_of(ref):
    return ref[...].reshape(-1, ref.shape[-1])


def each_sender(me_ref, count, slots):
    for k in range(count):
        sender = me_ref[0] ^ k
        yield k, sender, pl.ds(pl.multiple_of(sender * slots, 16), slots)


def expert_kernel(steps, blocks, half, *refs):
    me_ref, gate_a, up_a, down_a, gate_b, up_b, down_b, router_ref, gain_ref, cot_ref = refs[:10]
    pieces, refs = refs[10 : 10 + 2 * half], refs[10 + 2 * half :]
    message_ref, rows_ref, scaled_ref, active_ref, gate_part_ref, up_part_ref, sums_ref = refs[:7]
    side_ref, inner_ref, high_ref, low_ref = refs[7:]
    slots, columns, part = pieces[0].shape[0], gate_b.shape[0], gate_a.shape[1]
    count, width = rows_ref.shape
    experts = router_ref.shape[0]
    step = pl.program_id(0)

    def span_of(first):
        return pl.ds(pl.multiple_of((step - first) * columns, 128), columns)

    @pl.when(step == 0)
    def _():
        for k, sender, rows in each_sender(me_ref, 2 * half, slots):
            rows_ref[rows, :] = pieces[k][:, :width]
            side = pieces[k][:, width:]
            side_ref[rows, :] = side
            scale = side.astype(F32)[:, LANES - 1 :]
            scaled_ref[rows, :] = (scale * cot_ref[sender].astype(F32)).astype(BF16)
        inner_ref[...] = jnp.zeros_like(inner_ref)
        sums_ref[...] = jnp.zeros_like(sums_ref)

    @pl.when(step < steps)
    def _():
        gate = dot(rows_ref[...], gate_a[...])
        upper = dot(rows_ref[...], up_a[...])
        sig = jax.nn.sigmoid(gate)
        act_grad = dot_t(scaled_ref[...], down_a[...])
        active_ref[step] = (gate * sig * upper).astype(BF16)
        gate_part_ref[step] = (act_grad * upper * sig * (1.0 + gate * (1.0 - sig))).astype(BF16)
        up_part_ref[step] = (act_grad * (gate * sig)).astype(BF16)

    @pl.when((step >= steps) & (step < steps + blocks))
    def _():
        result = jnp.zeros((count, columns), F32)
        for f in range(steps):
            result = result + dot(active_ref[f], down_b[f * part : (f + 1) * part, :])
        cot = cot_ref[:, :, span_of(steps)].reshape(count, columns).astype(F32)
        result = result.astype(BF16).astype(F32)
        inner_ref[...] += jnp.sum(cot * result, axis=1, keepdims=True)

    @pl.when(step == steps + blocks)
    def _():
        terms = inner_ref[...].astype(BF16).astype(F32) * side_ref[...].astype(F32)
        high_ref[...] = terms.astype(BF16)
        low_ref[...] = (terms - terms.astype(BF16).astype(F32)).astype(BF16)

    @pl.when(step >= steps + blocks)
    def _():
        span = span_of(steps + blocks)
        rows = rows_ref[:, span]
        router = router_ref[:, span].astype(F32)
        rest = jnp.zeros((LANES - 2 * experts, columns), F32)
        router = jnp.concatenate([router, router, rest], axis=0).astype(BF16)
        total = dot(high_ref[...], router) + dot(low_ref[...], router)
        for f in range(steps):
            units = slice(f * part, (f + 1) * part)
            total = total + dot_t(gate_part_ref[f], gate_b[:, units])
            total = total + dot_t(up_part_ref[f], up_b[:, units])
        message_ref[:, span] = total.astype(BF16)
        terms = t_dot(high_ref[...], rows) + t_dot(low_ref[...], rows)
        sums_ref[:experts, span] = terms[:experts] + terms[experts : 2 * experts]
        gain_sum = jnp.sum(total * rows.astype(F32), axis=0, keepdims=True)
        sums_ref[experts : experts + 1, span] = gain_sum / gain_ref[:, span]


def forward_kernel(half, me_ref, gate_w, up_w, down_w, *refs):
    pieces, (out_ref, rows_ref) = refs[:half], refs[-2:]
    slots = pieces[0].shape[0]
    for k, piece in enumerate(pieces):
        start = pl.multiple_of((me_ref[0] ^ k) % half * slots, 16)
        rows_ref[pl.ds(start, slots), :] = piece[...]
    gate = dot(rows_ref[...], gate_w[...])
    active = (gate * jax.nn.sigmoid(gate) * dot(rows_ref[...], up_w[...])).astype(BF16)
    columns = 512 if out_ref.shape[2] % 512 == 0 else out_ref.shape[2]
    for c in range(0, out_ref.shape[2], columns):
        result = dot(active, down_w[:, c : c + columns]).astype(BF16)
        out_ref[:, :, c : c + columns] = result.reshape(half, slots, columns)


def spread_kernel(slots, rank_ref, weight_ref, spread_ref, flat_ref):
    for e in range(rank_ref.shape[0]):
        mask = slot_mask(rank_ref, e, slots)
        flat_ref[e * slots : (e + 1) * slots, :] = jnp.where(mask, weight_ref[e : e + 1, :], 0.0)
    spread_ref[...] = flat_ref[...].T.astype(BF16)


def source_kernel(hot_ref, xp_ref, dy_ref, gain_ref, *refs):
    grads, grad_ref = refs[:-1], refs[-1]
    dnormed = jnp.zeros(xp_ref.shape, F32)
    for c, ref in enumerate(grads):
        rows = flat_of(ref)
        part = slice(c * rows.shape[0], (c + 1) * rows.shape[0])
        dnormed = dnormed + dot(hot_ref[:, part], rows)
    values = xp_ref[...].astype(F32)
    scale = lax.rsqrt(jnp.mean(values * values, axis=-1, keepdims=True) + EPS)
    bare = values * scale
    lifted_grad = dnormed * gain_ref[...]
    slope = jnp.mean(lifted_grad * bare, axis=-1, keepdims=True)
    grad_ref[...] = (dy_ref[...].astype(F32) + scale * (lifted_grad - bare * slope)).astype(BF16)


def per_device(
    next_input,
    prev_input,
    next_cot,
    gate_weight,
    up_weight,
    down_weight,
    router,
    gain,
    next_routes,
    prev_routes,
    next_priority,
    prev_priority,
):
    experts = router.shape[-1]
    tokens, width = next_input.shape[1:]
    hidden = gate_weight.shape[-1]
    top = next_routes.shape[-1]
    capacity = (5 * top * tokens + 4 * experts - 1) // (4 * experts)
    slots = -(-capacity // 16) * 16
    mats = [gate_weight[0, 0], up_weight[0, 0], down_weight[0, 0]]
    gain_row, router_t = (gain, router[0].T)
    partial = functools.partial
    block, message = shape((tokens, width)), shape((experts, slots, width))
    per_token = shape((experts, tokens), F32)

    def exchange(array, name, groups=None):
        with jax.named_scope(name):
            return lax.all_to_all(array, "expert", 0, 0, tiled=True, axis_index_groups=groups)

    def swap(pieces, name):
        return [piece if k == 0 else hop(piece, 0, k, name) for k, piece in enumerate(pieces)]

    half = lax.axis_size("expert") // 2
    me = lax.axis_index("expert").astype(jnp.int32).reshape(1)
    smem, vmem = pl.BlockSpec(memory_space=pltpu.SMEM), pl.BlockSpec(memory_space=pltpu.VMEM)
    xp = prev_input[0]
    xp_far = hop(xp, 0, half, "xp_far")
    dy_in = hop(next_cot[0], -1, 0, "dy_in")
    x_in = hop(next_input[0], 1, 0, "x_in")
    table = jnp.concatenate(
        [next_routes[0].T, prev_routes[0].T, next_priority, prev_priority], axis=0
    )
    far_table = hop(table, 0, half, "tables")

    def ranks(table, name):
        dims = shape((experts, tokens), jnp.int32)
        return call(partial(rank_kernel, capacity, top), name, [dims] * 2, [table])

    frank, rank = ranks(table, "ranks")
    piece, normed_scratch = shape((slots, width)), pltpu.VMEM((tokens, width), BF16)
    frank_far, rank_far = ranks(far_table, "far_ranks")
    longer_piece = shape((slots, width + LANES))

    def back_rows(x, table, rank, name):
        pieces = call(
            partial(back_rows_kernel, half, top),
            name,
            [longer_piece] * half,
            [me, x, gain_row, router_t, table, rank],
            in_specs=[smem] + [vmem] * 5,
            scratch=[normed_scratch],
        )
        return swap(pieces, name)

    def next_rows(x, table, rank, name):
        outs = call(
            partial(next_rows_kernel, half, top),
            name,
            [piece] * half + [per_token],
            [me, x, gain_row, router_t, table, rank],
            in_specs=[smem] + [vmem] * 5,
            scratch=[normed_scratch],
        )
        return swap(outs[:half], name), outs[0], outs[half]

    own = back_rows(xp, table, rank, "own_rows")
    (cots,) = call(cots_kernel, "cots", [message], [rank, dy_in])
    cots = exchange(after(cots, xp_far, far_table, *own[1:]), "cots")
    far = back_rows(xp_far, far_table, rank_far, "far_rows")
    x_far = hop(after(next_input[0], cots, *far[1:]), 1, half, "x_far")
    fown, _, fweight = next_rows(x_in, table, frank, "fown_rows")
    ffar, ffar_sent, _ = next_rows(x_far, far_table, frank_far, "ffar_rows")

    count = experts * slots
    part = 256 if hidden % 256 == 0 else hidden
    columns = 512 if width % 512 == 0 else width
    steps = hidden // part
    blocks = width // columns
    grid = (steps + 2 * blocks,)

    def whole(dims):
        return pl.BlockSpec(dims.shape, lambda *_: (0,) * len(dims.shape), pipeline_mode=pl.Buffered(1))

    def early(i):
        return jnp.minimum(i, steps - 1)

    def middle(i):
        return jnp.clip(i - steps, 0, blocks - 1)

    def late(i):
        return jnp.maximum(i - steps - blocks, 0)

    across_a = pl.BlockSpec((width, part), lambda i, *_: (0, early(i)))
    down_a = pl.BlockSpec((part, width), lambda i: (early(i), 0))
    across_b = pl.BlockSpec((columns, hidden), lambda i: (late(i), 0))
    down_b = pl.BlockSpec((hidden, columns), lambda i, *_: (0, middle(i)))
    flops = 2 * count * width * hidden
    def spread_of(rank, weight, name):
        return call(
            partial(spread_kernel, slots),
            name,
            [shape((tokens, count))],
            [rank, weight],
            scratch=[pltpu.VMEM((count, tokens), F32)],
        )[0]

    spread = spread_of(frank, fweight, "spread")
    hot = spread_of(rank, jnp.ones((experts, tokens), F32), "hot")
    flat, hidden_shape = shape((count, width)), shape((steps, count, part))
    sums_shape = shape((-(-(experts + 1) // 8) * 8, width), F32)
    grads, flat_rows, scaled, active, gate_part, up_part, sums = call(
        partial(expert_kernel, steps, blocks, half),
        "expert",
        [flat] * 3 + [hidden_shape] * 3 + [sums_shape],
        [me] + mats + mats + [router_t, gain_row, cots] + own + far,
        grid=grid,
        in_specs=[smem, across_a, across_a, down_a, across_b, across_b, down_b]
        + [whole(router_t), whole(gain_row), whole(message)]
        + [whole(longer_piece)] * experts,
        out_specs=[whole(flat)] * 3 + [whole(hidden_shape)] * 3 + [whole(sums_shape)],
        scratch=[
            pltpu.VMEM((count, LANES), BF16),
            pltpu.VMEM((count, 1), F32),
            pltpu.VMEM((count, LANES), BF16),
            pltpu.VMEM((count, LANES), BF16),
        ],
        flops=6 * flops,
    )
    active, gate_part, up_part = (
        jnp.swapaxes(a, 0, 1).reshape(count, hidden) for a in (active, gate_part, up_part)
    )
    grads = grads.reshape(experts, slots, width)
    grads = exchange(after(grads, x_far, hot, spread, *fown[1:]), "grads")
    flat_rows, active = after((flat_rows, active), ffar_sent)
    gate_wgrad = t_dot(flat_rows, gate_part).astype(BF16)
    up_wgrad = t_dot(flat_rows, up_part).astype(BF16)
    down_wgrad = t_dot(active, scaled).astype(BF16)
    packed = [sums[:experts], sums[experts].reshape(experts, width // experts)]
    packed = jnp.concatenate(packed, axis=1)

    def forward_of(pieces, flip, name, *filled):
        return pl.pallas_call(
            partial(forward_kernel, half),
            out_shape=message,
            grid_spec=pltpu.PrefetchScalarGridSpec(
                num_scalar_prefetch=1,
                grid=(1,),
                in_specs=[whole(m) for m in mats]
                + [whole(piece)] * half
                + [pl.BlockSpec(memory_space=pl.ANY)] * len(filled),
                out_specs=pl.BlockSpec(
                    (half, slots, width), lambda i, me_ref: (me_ref[0] // half ^ flip, 0, 0)
                ),
                scratch_shapes=[pltpu.VMEM((count // 2, width), BF16)],
            ),
            input_output_aliases={4 + half: 0} if filled else {},
            compiler_params=pltpu.CompilerParams(vmem_limit_bytes=VMEM_BYTES),
            cost_estimate=pl.CostEstimate(
                flops=3 * flops // 2, bytes_accessed=6 * width * hidden, transcendentals=0
            ),
            name=name,
        )(me, *mats, *pieces, *filled)

    outs = forward_of(fown, 0, "forward_own")
    outs = forward_of(ffar, 1, "forward_far", outs)
    outs = exchange(after(outs, grads, gate_wgrad, up_wgrad, down_wgrad, packed), "outs")
    cuts = 4 if experts % 4 == 0 else 1

    def full(array):
        return pl.BlockSpec(array.shape, lambda i: (0,) * len(array.shape))

    def cut_at(c):
        return pl.BlockSpec((experts // cuts, slots, width), lambda i: (c, 0, 0))

    known = [hot, xp, dy_in, gain_row]
    (grad_in,) = call(
        source_kernel,
        "source",
        [block],
        known + [grads] * cuts,
        grid=(1,),
        in_specs=[full(a) for a in known] + [cut_at(c) for c in range(cuts)],
        out_specs=[full(block)],
    )
    sums = swap([after(packed, grads)] * half, "sums")
    while len(sums) > 1:
        sums = [a + b for a, b in zip(sums[::2], sums[1::2])]
    sums = sums[0] + hop(after(sums[0], grad_in), 0, half, "sums_far")
    outs = after(outs, grad_in)
    forward = (x_in.astype(F32) + dot(spread, outs.reshape(count, width))).astype(BF16)
    return (
        forward[None],
        grad_in[None],
        gate_wgrad[None, None],
        up_wgrad[None, None],
        down_wgrad[None, None],
        sums[:, :width].T[None],
        sums[:, width:].reshape(1, width),
    )


def solution(mesh):
    rows = P("pipe", "expert", None)
    weights = P("pipe", "expert", None, None)
    shared = P("pipe", None, None)
    return jax.shard_map(
        per_device,
        mesh=mesh,
        in_specs=(rows,) * 3
        + (weights,) * 3
        + (shared, P("pipe", None), rows, rows, P("pipe", "expert"), P("pipe", "expert")),
        out_specs=(rows, rows, weights, weights, weights, shared, P("pipe", None)),
        check_vma=False,
    )
```

time: 318 us -> 315 us (level)
  waiting for transfers between devices: 162 us -> 155 us
    all_to_all x3, waiting for transfers between devices: 10.7 us -> 1.02 us  [exchange(): lax.all_to_all(array, 'expert', 0, 0, tiled=True, axis_index_groups=groups)]
    ppermute x18, waiting for transfers between devices: 140 us -> 146 us  [hop(): lax.ppermute(block, 'expert', [(e, e ^ flip) for e in range(experts)])]
    ppermute x3, waiting for transfers between devices: 10.8 us -> 7.41 us  [hop(): return lax.ppermute(block, ('pipe', 'expert'), route)]
    pallas_call x12 -> x11, Pallas kernels: 62.8 us -> 61.4 us  [call(): pl.pallas_call(kernel, out_shape=[jax.ShapeDtypeStruct(o.shape, o.dtype)...]
  transfers between devices with their start and end apart: 24 -> 24, of which waited for: 13 -> 14; matrix products, arithmetic and copies ran while one was open for 7% -> 8% of each run, Pallas kernels for 25% -> 25%
where the time goes in v3:
time: 315 us; the launch traced here: 314 us
  waiting for transfers between devices  155 us (49%)
  Pallas kernels  78.3 us (25%)
  starting transfers between devices  47.5 us (15%)
  matrix products  18.5 us (6%)
  local copies, waits for them, and re-layouts  12.8 us (4%)
    ppermute x18, waiting for transfers between devices, hop(): lax.ppermute(block, 'expert', [(e, e ^ flip) for e in range(experts)])  146 us
    pallas_call x11, Pallas kernels, call(): pl.pallas_call(kernel, out_shape=[jax.ShapeDtypeStruct(o.shape, o.dtype)...  61.4 us
    ppermute x18, starting transfers between devices, hop(): lax.ppermute(block, 'expert', [(e, e ^ flip) for e in range(experts)])  27.7 us
    pallas_call x2, Pallas kernels, forward_of(): pl.pallas_call(partial(forward_kernel, half), out_shape=message, grid_spe...  16.9 us
    all_to_all x3, starting transfers between devices, exchange(): lax.all_to_all(array, 'expert', 0, 0, tiled=True, axis_index_groups=groups)  15.5 us
    dot_general x3, matrix products, t_dot(): lax.dot_general(a, b, dims, preferred_element_type=F32, precision=precision)  14.5 us
    ppermute x3, waiting for transfers between devices, hop(): return lax.ppermute(block, ('pipe', 'expert'), route)  7.41 us
    transpose x3, local copies, waits for them, and re-layouts, per_device(): jnp.swapaxes(a, 0, 1).reshape(count, hidden)  6.73 us
  transfers between devices with their start and end apart: 24, of which 14 were waited for; matrix products, arithmetic and copies ran while one was open for 8% of the time, Pallas kernels for 25%

profile of v3, /device:TPU:0, one launch (start us, length us, event | category | flops | bytes accessed | tf_op | source)
XLA Modules:
  0.0 314.0 jit_solution(15853702292014431243)
XLA Ops:
  0.6 2.5 collective-permute-start.1
  3.1 2.6 collective-permute-start.2
  5.7 1.3 pad_add_fusion.table_ref.refs_4_
  7.0 1.5 ranks.1
  8.6 4.6 %own_rows.1 = (bf16[80,2176]{1,0:T(8,128)(2,1)}, bf16[80,2176]{1,0:T(8,128)(2,1)}, bf16[80,2176]{1,0:T(8,128)(2,1)}, bf16[80,2176]{1,0:T(8,128)(2,1)}) custom-call(s32[1]{0:T(128)} %bitcast.5.refs_0_.me_ref, bf16[256,2048]{1,0:T(8,128)(2,1)} %bitcast.59, f32[1,2048]{1,0:T(1,128)} %gain_ref.1, bf16[8,2048]{1,0:T(8,128)(2,1)} %bitcast.69, ...), custom_call_target="tpu_custom_call" | custom-call | bytes 39008 | tf_op jit(solution)/shard_map/own_rows/pallas_call | solution.py:55
  13.1 1.5 collective-permute-start.4
  14.6 1.6 collective-permute-start.5
  16.2 0.4 collective-permute-start.6
  16.6 1.7 collective-permute-start.3
  18.3 4.3 %cots.1 = bf16[8,80,2048]{2,1,0:T(8,128)(2,1)} custom-call(s32[8,256]{1,0:T(8,128)} %get-tuple-element.46.rank_ref.refs_5_, bf16[256,2048]{1,0:T(8,128)(2,1)} %copy-done.2), custom_call_target="tpu_custom_call" | custom-call | bytes 57472 | tf_op jit(solution)/shard_map/cots/pallas_call | solution.py:55
  22.6 29.0 %collective-permute-done.3.table_ref.refs_4_ = s32[6,256]{1,0:T(8,128)S(1)} collective-permute-done((s32[6,256]{1,0:T(8,128)}, s32[6,256]{1,0:T(8,128)S(1)}, u32[]{:S(2)}, u32[]{:S(2)}) %collective-permute-start.3) | collective-permute-done | bytes 6176 | tf_op jit(solution)/shard_map/tables/ppermute | solution.py:22
  51.7 1.2 collective-permute-done.6.refs_13_
  52.9 0.7 copy-done.9
  53.6 0.3 copy-done.4
  53.9 4.6 %all-to-all-start = ((bf16[8,80,2048]{2,1,0:T(8,128)(2,1)}), bf16[8,80,2048]{2,1,0:T(8,128)(2,1)S(1)}, u32[]{:S(2)}, u32[]{:S(2)}) async-start(bf16[8,80,2048]{2,1,0:T(8,128)(2,1)} %cots.1), calls=%async_computation | async-start | bytes 5242880 | tf_op jit(solution)/shard_map/cots/all_to_all | solution.py:314
  58.6 1.6 far_ranks.1
  60.1 4.6 %far_rows.1 = (bf16[80,2176]{1,0:T(8,128)(2,1)}, bf16[80,2176]{1,0:T(8,128)(2,1)}, bf16[80,2176]{1,0:T(8,128)(2,1)}, bf16[80,2176]{1,0:T(8,128)(2,1)}) custom-call(s32[1]{0:T(128)} %bitcast.5.refs_0_.me_ref, bf16[256,2048]{1,0:T(8,128)(2,1)} %copy-done.4, f32[1,2048]{1,0:T(1,128)} %gain_ref.1, bf16[8,2048]{1,0:T(8,128)(2,1)} %bitcast.70, ...), custom_call_target="tpu_custom_call" | custom-call | bytes 39008 | tf_op jit(solution)/shard_map/far_rows/pallas_call | solution.py:55
  64.7 2.0 collective-permute-start.7
  66.8 1.5 collective-permute-start.8
  68.2 20.4 %collective-permute-done.7.refs_15_ = bf16[80,2176]{1,0:T(8,128)(2,1)S(1)} collective-permute-done((bf16[80,2176]{1,0:T(8,128)(2,1)}, bf16[80,2176]{1,0:T(8,128)(2,1)S(1)}, u32[]{:S(2)}, u32[]{:S(2)}) %collective-permute-start.7) | collective-permute-done | bytes 348192 | tf_op jit(solution)/shard_map/far_rows/ppermute | solution.py:22
  88.6 22.1 %collective-permute-done.8.refs_16_ = bf16[80,2176]{1,0:T(8,128)(2,1)S(1)} collective-permute-done((bf16[80,2176]{1,0:T(8,128)(2,1)}, bf16[80,2176]{1,0:T(8,128)(2,1)S(1)}, u32[]{:S(2)}, u32[]{:S(2)}) %collective-permute-start.8) | collective-permute-done | bytes 348192 | tf_op jit(solution)/shard_map/far_rows/ppermute | solution.py:22
  110.7 0.7 copy-done.11
  111.5 5.7 %collective-permute-done.9.refs_17_ = bf16[80,2176]{1,0:T(8,128)(2,1)} collective-permute-done((bf16[80,2176]{1,0:T(8,128)(2,1)}, bf16[80,2176]{1,0:T(8,128)(2,1)}, u32[]{:S(2)}, u32[]{:S(2)}) %collective-permute-start.9) | collective-permute-done | bytes 348192 | tf_op jit(solution)/shard_map/far_rows/ppermute | solution.py:22
  117.1 1.0 all-to-all-done.refs_9_
  118.1 1.8 collective-permute-start.10
  120.0 4.1 %fown_rows.1 = (bf16[80,2048]{1,0:T(8,128)(2,1)}, bf16[80,2048]{1,0:T(8,128)(2,1)}, bf16[80,2048]{1,0:T(8,128)(2,1)}, bf16[80,2048]{1,0:T(8,128)(2,1)}, f32[8,256]{1,0:T(8,128)}) custom-call(s32[1]{0:T(128)} %bitcast.5.refs_0_.me_ref, bf16[256,2048]{1,0:T(8,128)(2,1)} %collective-permute-done.refs_1_, f32[1,2048]{1,0:T(1,128)} %gain_ref.1, ...), custom_call_target="tpu_custom_call" | custom-call | bytes 37856 | tf_op jit(solution)/shard_map/fown_rows/pallas_call | solution.py:55
  124.0 0.6 collective-permute-start.14
  124.6 1.5 collective-permute-start.15
  126.1 1.4 collective-permute-start.16
  127.5 0.6 broadcast_in_dim.21.weight_ref
  128.1 1.6 hot.1.hot_ref
  129.7 1.6 spread.1
  131.3 28.2 %expert.1 = (bf16[640,2048]{1,0:T(8,128)(2,1)}, bf16[640,2048]{1,0:T(8,128)(2,1)}, bf16[640,2048]{1,0:T(8,128)(2,1)}, bf16[3,640,256]{2,1,0:T(8,128)(2,1)}, bf16...) custom-call(s32[1]{0:T(128)} %bitcast.5.refs_0_.me_ref, bf16[2048,768]{1,0:T(8,128)(2,1)} %bitcast.46, ...), custom_call_target="tpu_custom_call" | custom-call | flops 188743680 | bytes 551040 | tf_op jit(solution)/shard_map/expert/pallas_call | solution.py:55
  159.5 7.4 %collective-permute-done.10.refs_1_ = bf16[256,2048]{1,0:T(8,128)(2,1)} collective-permute-done((bf16[256,2048]{1,0:T(8,128)(2,1)}, bf16[256,2048]{1,0:T(8,128)(2,1)}, u32[]{:S(2)}, u32[]{:S(2)}) %collective-permute-start.10) | collective-permute-done | bytes 1048608 | tf_op jit(solution)/shard_map/x_far/ppermute | solution.py:28
  166.9 5.2 %all-to-all-start.1 = ((bf16[8,80,2048]{2,1,0:T(8,128)(2,1)}), bf16[8,80,2048]{2,1,0:T(8,128)(2,1)S(1)}, u32[]{:S(2)}, u32[]{:S(2)}) async-start(bf16[8,80,2048]{2,1,0:T(8,128)(2,1)} %bitcast.61), calls=%async_computation.1 | async-start | bytes 5242880 | tf_op jit(solution)/shard_map/grads/all_to_all | solution.py:314
  172.2 8.4 %forward_own.1.refs_4_ = bf16[8,80,2048]{2,1,0:T(8,128)(2,1)} custom-call(s32[1]{0:T(128)} %bitcast.5.refs_0_.me_ref, bf16[2048,768]{1,0:T(8,128)(2,1)} %bitcast.48, bf16[2048,768]{1,0:T(8,128)(2,1)} %bitcast.52, bf16[768,2048]{1,0:T(8,128)(2,1)} %bitcast.56, bf16[80,2048]{1,0:T(8,128)(2,1)} %get-tuple-element.61.refs_0_, ...), custom_call_target="tpu_custom_call" | custom-call | flops 3019898880 | bytes 9437184 | tf_op jit(solution)/shard_map/forward_own/pallas_call | solution.py:438
  180.6 2.3 copy.20
  182.9 2.2 copy.22
  185.1 2.2 copy.21
  187.4 4.1 %ffar_rows.1 = (bf16[80,2048]{1,0:T(8,128)(2,1)}, bf16[80,2048]{1,0:T(8,128)(2,1)}, bf16[80,2048]{1,0:T(8,128)(2,1)}, bf16[80,2048]{1,0:T(8,128)(2,1)}, f32[8,256]{1,0:T(8,128)}) custom-call(s32[1]{0:T(128)} %bitcast.5.refs_0_.me_ref, bf16[256,2048]{1,0:T(8,128)(2,1)} %collective-permute-done.10.refs_1_, f32[1,2048]{1,0:T(1,128)} %gain_ref.1, ...), custom_call_target="tpu_custom_call" | custom-call | bytes 37856 | tf_op jit(solution)/shard_map/ffar_rows/pallas_call | solution.py:55
  191.4 2.0 collective-permute-start.11
  193.5 1.5 collective-permute-start.12
  194.9 6.5 %convolution_convert_fusion.1 = bf16[2048,768]{1,0:T(8,128)(2,1)} fusion(bf16[640,2048]{1,0:T(8,128)(2,1)} %get-tuple-element.71, bf16[640,768]{0,1:T(8,128)(2,1)} %bitcast.68), kind=kOutput, calls=%fused_computation.1 | convolution fusion | flops 2014838784 | bytes 6750208 | tf_op jit(solution)/shard_map/dot_general | solution.py:45
  201.4 4.1 %convolution_convert_fusion.2 = bf16[2048,768]{1,0:T(8,128)(2,1)} fusion(bf16[640,2048]{1,0:T(8,128)(2,1)S(1)} %copy-done.18, bf16[640,768]{0,1:T(8,128)(2,1)S(1)} %bitcast.67), kind=kOutput, calls=%fused_computation.2 | convolution fusion | flops 2014838784 | bytes 6750208 | tf_op jit(solution)/shard_map/dot_general | solution.py:45
  205.5 4.0 %convolution_convert_fusion = bf16[768,2048]{1,0:T(8,128)(2,1)} fusion(bf16[640,768]{0,1:T(8,128)(2,1)S(1)} %bitcast.66, bf16[640,2048]{1,0:T(8,128)(2,1)S(1)} %copy-done.17), kind=kOutput, calls=%fused_computation | convolution fusion | flops 2014838784 | bytes 6750208 | tf_op jit(solution)/shard_map/dot_general | solution.py:45
  209.5 2.7 collective-permute-done.11.refs_1_
  212.2 11.3 %collective-permute-done.12.refs_2_ = bf16[80,2048]{1,0:T(8,128)(2,1)S(1)} collective-permute-done((bf16[80,2048]{1,0:T(8,128)(2,1)}, bf16[80,2048]{1,0:T(8,128)(2,1)S(1)}, u32[]{:S(2)}, u32[]{:S(2)}) %collective-permute-start.12) | collective-permute-done | bytes 327712 | tf_op jit(solution)/shard_map/ffar_rows/ppermute | solution.py:22
  223.6 6.0 %collective-permute-done.13.refs_3_ = bf16[80,2048]{1,0:T(8,128)(2,1)S(1)} collective-permute-done((bf16[80,2048]{1,0:T(8,128)(2,1)}, bf16[80,2048]{1,0:T(8,128)(2,1)S(1)}, u32[]{:S(2)}, u32[]{:S(2)}) %collective-permute-start.13) | collective-permute-done | bytes 327712 | tf_op jit(solution)/shard_map/ffar_rows/ppermute | solution.py:22
  229.6 0.7 copy-done.14
  230.4 8.5 %forward_far.1 = bf16[8,80,2048]{2,1,0:T(8,128)(2,1)} custom-call(s32[1]{0:T(128)} %bitcast.5.refs_0_.me_ref, bf16[2048,768]{1,0:T(8,128)(2,1)} %bitcast.49, bf16[2048,768]{1,0:T(8,128)(2,1)} %bitcast.53, bf16[768,2048]{1,0:T(8,128)(2,1)} %bitcast.57, bf16[80,2048]{1,0:T(8,128)(2,1)} %get-tuple-element.57.refs_0_, ...), custom_call_target="tpu_custom_call", output_to_operand_aliasing={{}: (8, {})} | custom-call | flops 3019898880 | bytes 9437184 | tf_op jit(solution)/shard_map/forward_far/pallas_call | solution.py:438
  238.8 1.6 copy-done
  240.4 5.7 %all-to-all-start.2 = ((bf16[8,80,2048]{2,1,0:T(8,128)(2,1)}), bf16[8,80,2048]{2,1,0:T(8,128)(2,1)}, u32[]{:S(2)}, u32[]{:S(2)}) async-start(bf16[8,80,2048]{2,1,0:T(8,128)(2,1)} %forward_far.1), calls=%async_computation.2 | async-start | bytes 5242880 | tf_op jit(solution)/shard_map/outs/all_to_all | solution.py:314
  246.1 2.0 collective-permute-start.17
  248.1 1.5 collective-permute-start.18
  249.5 0.4 collective-permute-start.19
  249.9 5.3 %source.1 = bf16[256,2048]{1,0:T(8,128)(2,1)} custom-call(bf16[256,640]{1,0:T(8,128)(2,1)} %hot.1.hot_ref, bf16[256,2048]{1,0:T(8,128)(2,1)} %bitcast.60, bf16[256,2048]{1,0:T(8,128)(2,1)} %copy-done.2, f32[1,2048]{1,0:T(1,128)} %gain_ref.1, bf16[8,80,2048]{2,1,0:T(8,128)(2,1)} %copy-done, bf16[8,80,2048]{2,1,0:T(8,128)(2,1)} %copy-done, ...), custom_call_target="tpu_custom_call" | custom-call | bytes 218240 | tf_op jit(solution)/shard_map/source/pallas_call | solution.py:55
  255.2 12.5 %collective-permute-done.17 = f32[8,2304]{1,0:T(8,128)S(1)} collective-permute-done((f32[8,2304]{1,0:T(8,128)S(1)}, f32[8,2304]{1,0:T(8,128)S(1)}, u32[]{:S(2)}, u32[]{:S(2)}) %collective-permute-start.17) | collective-permute-done | bytes 73760 | tf_op jit(solution)/shard_map/sums/ppermute | solution.py:22
  267.7 22.7 %collective-permute-done.18 = f32[8,2304]{1,0:T(8,128)S(1)} collective-permute-done((f32[8,2304]{1,0:T(8,128)S(1)}, f32[8,2304]{1,0:T(8,128)S(1)}, u32[]{:S(2)}, u32[]{:S(2)}) %collective-permute-start.18) | collective-permute-done | bytes 73760 | tf_op jit(solution)/shard_map/sums/ppermute | solution.py:22
  290.4 0.8 collective-permute-done.19
  291.2 5.6 %collective-permute-start.20 = (f32[8,2304]{1,0:T(8,128)S(1)}, f32[8,2304]{1,0:T(8,128)S(1)}, u32[]{:S(2)}, u32[]{:S(2)}) collective-permute-start(f32[8,2304]{1,0:T(8,128)S(1)} %add_add_fusion), channel_id=1, source_target_pairs={{0,4},{1,5},{2,6},{3,7},{4,0},{5,1},{6,2},{7,3},{8,12},{9,13},{10,... | collective-permute-start | bytes 221192 | tf_op jit(solution)/shard_map/sums_far/ppermute | solution.py:22
  296.8 11.9 %collective-permute-done.20 = f32[8,2304]{1,0:T(8,128)S(1)} collective-permute-done((f32[8,2304]{1,0:T(8,128)S(1)}, f32[8,2304]{1,0:T(8,128)S(1)}, u32[]{:S(2)}, u32[]{:S(2)}) %collective-permute-start.20) | collective-permute-done | bytes 73760 | tf_op jit(solution)/shard_map/sums_far/ppermute | solution.py:22
  308.8 0.6 copy.23
  309.4 0.6 slice_bitcast_fusion
  310.0 4.0 %fusion = bf16[1,256,2048]{2,1,0:T(8,128)(2,1)} fusion(bf16[256,2048]{1,0:T(8,128)(2,1)} %collective-permute-done.refs_1_, bf16[256,640]{1,0:T(8,128)(2,1)S(1)} %copy-done.3, bf16[640,2048]{1,0:T(8,128)(2,1)} %bitcast.21), kind=kOutput, calls=%fused_computation.4 | convolution fusion | flops 672661504 | bytes 5046272 | tf_op jit(solution)/shard_map/dot_general | solution.py:36
  (53 shorter events, 0.2 us)
Async XLA Ops:
  0.6 16.0 %collective-permute-start.1 = (bf16[256,2048]{1,0:T(8,128)(2,1)}, bf16[256,2048]{1,0:T(8,128)(2,1)S(1)}, u32[]{:S(2)}, u32[]{:S(2)}) collective-permute-start(bf16[256,2048]{1,0:T(8,128)(2,1)} %bitcast.77), channel_id=1, source_target_pairs={{0,24},{1,25},{2,26},{3,27},{4,28},{5,29},{6,30},{7,31},{8,0},{9,1... | collective-permute-start | bytes 3145736 | tf_op jit(solution)/shard_map/dy_in/ppermute | solution.py:28
  3.1 49.8 %collective-permute-start.2 = (bf16[256,2048]{1,0:T(8,128)(2,1)}, bf16[256,2048]{1,0:T(8,128)(2,1)S(1)}, u32[]{:S(2)}, u32[]{:S(2)}) collective-permute-start(bf16[256,2048]{1,0:T(8,128)(2,1)} %bitcast.58), channel_id=1, source_target_pairs={{0,4},{1,5},{2,6},{3,7},{4,0},{5,1},{6,2},{7,3},{8,12},{9,13},{10,... | collective-permute-start | bytes 3145736 | tf_op jit(solution)/shard_map/xp_far/ppermute | solution.py:22
  13.1 38.5 %collective-permute-start.4 = (bf16[80,2176]{1,0:T(8,128)(2,1)}, bf16[80,2176]{1,0:T(8,128)(2,1)S(1)}, u32[]{:S(2)}, u32[]{:S(2)}) collective-permute-start(bf16[80,2176]{1,0:T(8,128)(2,1)} %get-tuple-element.47), channel_id=1, source_target_pairs={{0,1},{1,0},{2,3},{3,2},{4,5},{5,4},{6,7},{7,6},{8,9},{9,8},{10,11... | collective-permute-start | bytes 1044488 | tf_op jit(solution)/shard_map/own_rows/ppermute | solution.py:22
  14.6 37.0 %collective-permute-start.5 = (bf16[80,2176]{1,0:T(8,128)(2,1)}, bf16[80,2176]{1,0:T(8,128)(2,1)S(1)}, u32[]{:S(2)}, u32[]{:S(2)}) collective-permute-start(bf16[80,2176]{1,0:T(8,128)(2,1)} %get-tuple-element.48), channel_id=1, source_target_pairs={{0,2},{1,3},{2,0},{3,1},{4,6},{5,7},{6,4},{7,5},{8,10},{9,11},{10,... | collective-permute-start | bytes 1044488 | tf_op jit(solution)/shard_map/own_rows/ppermute | solution.py:22
  16.2 36.6 %collective-permute-start.6 = (bf16[80,2176]{1,0:T(8,128)(2,1)}, bf16[80,2176]{1,0:T(8,128)(2,1)S(1)}, u32[]{:S(2)}, u32[]{:S(2)}) collective-permute-start(bf16[80,2176]{1,0:T(8,128)(2,1)} %get-tuple-element.49), channel_id=1, source_target_pairs={{0,3},{1,2},{2,1},{3,0},{4,7},{5,6},{6,5},{7,4},{8,11},{9,10},{10,... | collective-permute-start | bytes 1044488 | tf_op jit(solution)/shard_map/own_rows/ppermute | solution.py:22
  16.6 1.7 copy-start.2
  16.6 35.0 %collective-permute-start.3 = (s32[6,256]{1,0:T(8,128)}, s32[6,256]{1,0:T(8,128)S(1)}, u32[]{:S(2)}, u32[]{:S(2)}) collective-permute-start(s32[6,256]{1,0:T(8,128)} %pad_add_fusion.table_ref.refs_4_), channel_id=1, source_target_pairs={{0,4},{1,5},{2,6},{3,7},{4,0},{5,1},{6,2},{7,3},{8,12},{9,13},{10,... | collective-permute-start | bytes 18440 | tf_op jit(solution)/shard_map/tables/ppermute | solution.py:22
  51.6 7.0 %copy-start.15 = (s32[6,256]{1,0:T(8,128)}, s32[6,256]{1,0:T(8,128)S(1)}, u32[]{:S(2)}) copy-start(s32[6,256]{1,0:T(8,128)S(1)} %collective-permute-done.3.table_ref.refs_4_) | copy-start | bytes 18436
  51.6 79.7 %copy-start.7 = (bf16[80,2176]{1,0:T(8,128)(2,1)}, bf16[80,2176]{1,0:T(8,128)(2,1)S(1)}, u32[]{:S(2)}) copy-start(bf16[80,2176]{1,0:T(8,128)(2,1)S(1)} %collective-permute-done.4.refs_11_) | copy-start | bytes 1044484
  51.6 79.7 %copy-start.8 = (bf16[80,2176]{1,0:T(8,128)(2,1)}, bf16[80,2176]{1,0:T(8,128)(2,1)S(1)}, u32[]{:S(2)}) copy-start(bf16[80,2176]{1,0:T(8,128)(2,1)S(1)} %collective-permute-done.5.refs_12_) | copy-start | bytes 1044484
  52.9 0.7 copy-start.9
  52.9 1.1 copy-start.4
  53.9 64.2 %all-to-all-start = ((bf16[8,80,2048]{2,1,0:T(8,128)(2,1)}), bf16[8,80,2048]{2,1,0:T(8,128)(2,1)S(1)}, u32[]{:S(2)}, u32[]{:S(2)}) async-start(bf16[8,80,2048]{2,1,0:T(8,128)(2,1)} %cots.1), calls=%async_computation | async-start | bytes 5242880 | tf_op jit(solution)/shard_map/cots/all_to_all | solution.py:314
  64.7 23.9 %collective-permute-start.7 = (bf16[80,2176]{1,0:T(8,128)(2,1)}, bf16[80,2176]{1,0:T(8,128)(2,1)S(1)}, u32[]{:S(2)}, u32[]{:S(2)}) collective-permute-start(bf16[80,2176]{1,0:T(8,128)(2,1)} %get-tuple-element.52), channel_id=1, source_target_pairs={{0,1},{1,0},{2,3},{3,2},{4,5},{5,4},{6,7},{7,6},{8,9},{9,8},{10,11... | collective-permute-start | bytes 1044488 | tf_op jit(solution)/shard_map/far_rows/ppermute | solution.py:22
  66.8 44.0 %collective-permute-start.8 = (bf16[80,2176]{1,0:T(8,128)(2,1)}, bf16[80,2176]{1,0:T(8,128)(2,1)S(1)}, u32[]{:S(2)}, u32[]{:S(2)}) collective-permute-start(bf16[80,2176]{1,0:T(8,128)(2,1)} %get-tuple-element.53), channel_id=1, source_target_pairs={{0,2},{1,3},{2,0},{3,1},{4,6},{5,7},{6,4},{7,5},{8,10},{9,11},{10,... | collective-permute-start | bytes 1044488 | tf_op jit(solution)/shard_map/far_rows/ppermute | solution.py:22
  68.2 48.9 %collective-permute-start.9 = (bf16[80,2176]{1,0:T(8,128)(2,1)}, bf16[80,2176]{1,0:T(8,128)(2,1)}, u32[]{:S(2)}, u32[]{:S(2)}) collective-permute-start(bf16[80,2176]{1,0:T(8,128)(2,1)} %get-tuple-element.54), channel_id=1, source_target_pairs={{0,3},{1,2},{2,1},{3,0},{4,7},{5,6},{6,5},{7,4},{8,11},{9,10},{10,... | collective-permute-start | bytes 1044488 | tf_op jit(solution)/shard_map/far_rows/ppermute | solution.py:22
  68.2 51.7 %collective-permute-start = (bf16[256,2048]{1,0:T(8,128)(2,1)}, bf16[256,2048]{1,0:T(8,128)(2,1)}, u32[]{:S(2)}, u32[]{:S(2)}) collective-permute-start(bf16[256,2048]{1,0:T(8,128)(2,1)} %bitcast.78), channel_id=1, source_target_pairs={{0,8},{1,9},{2,10},{3,11},{4,12},{5,13},{6,14},{7,15},{8,16},{9,17... | collective-permute-start | bytes 3145736 | tf_op jit(solution)/shard_map/x_in/ppermute | solution.py:28
  88.6 22.1 %copy-start.10 = (bf16[80,2176]{1,0:T(8,128)(2,1)}, bf16[80,2176]{1,0:T(8,128)(2,1)S(1)}, u32[]{:S(2)}) copy-start(bf16[80,2176]{1,0:T(8,128)(2,1)S(1)} %collective-permute-done.7.refs_15_) | copy-start | bytes 1044484
  110.7 0.7 copy-start.11
  118.1 13.2 %copy-start.1 = (bf16[8,80,2048]{2,1,0:T(8,128)(2,1)}, bf16[8,80,2048]{2,1,0:T(8,128)(2,1)S(1)}, u32[]{:S(2)}) copy-start(bf16[8,80,2048]{2,1,0:T(8,128)(2,1)S(1)} %all-to-all-done.refs_9_) | copy-start | bytes 7864324
  118.1 48.8 %collective-permute-start.10 = (bf16[256,2048]{1,0:T(8,128)(2,1)}, bf16[256,2048]{1,0:T(8,128)(2,1)}, u32[]{:S(2)}, u32[]{:S(2)}) collective-permute-start(bf16[256,2048]{1,0:T(8,128)(2,1)} %bitcast.79), channel_id=1, source_target_pairs={{0,12},{1,13},{2,14},{3,15},{4,8},{5,9},{6,10},{7,11},{8,20},{9,21... | collective-permute-start | bytes 3145736 | tf_op jit(solution)/shard_map/x_far/ppermute | solution.py:28
  124.0 35.5 %collective-permute-start.14 = (bf16[80,2048]{1,0:T(8,128)(2,1)}, bf16[80,2048]{1,0:T(8,128)(2,1)}, u32[]{:S(2)}, u32[]{:S(2)}) collective-permute-start(bf16[80,2048]{1,0:T(8,128)(2,1)} %get-tuple-element.62), channel_id=1, source_target_pairs={{0,1},{1,0},{2,3},{3,2},{4,5},{5,4},{6,7},{7,6},{8,9},{9,8},{10,11... | collective-permute-start | bytes 983048 | tf_op jit(solution)/shard_map/fown_rows/ppermute | solution.py:22
  124.6 34.9 %collective-permute-start.15 = (bf16[80,2048]{1,0:T(8,128)(2,1)}, bf16[80,2048]{1,0:T(8,128)(2,1)}, u32[]{:S(2)}, u32[]{:S(2)}) collective-permute-start(bf16[80,2048]{1,0:T(8,128)(2,1)} %get-tuple-element.63), channel_id=1, source_target_pairs={{0,2},{1,3},{2,0},{3,1},{4,6},{5,7},{6,4},{7,5},{8,10},{9,11},{10,... | collective-permute-start | bytes 983048 | tf_op jit(solution)/shard_map/fown_rows/ppermute | solution.py:22
  126.1 33.5 %collective-permute-start.16 = (bf16[80,2048]{1,0:T(8,128)(2,1)}, bf16[80,2048]{1,0:T(8,128)(2,1)}, u32[]{:S(2)}, u32[]{:S(2)}) collective-permute-start(bf16[80,2048]{1,0:T(8,128)(2,1)} %get-tuple-element.64), channel_id=1, source_target_pairs={{0,3},{1,2},{2,1},{3,0},{4,7},{5,6},{6,5},{7,4},{8,11},{9,10},{10,... | collective-permute-start | bytes 983048 | tf_op jit(solution)/shard_map/fown_rows/ppermute | solution.py:22
  166.9 71.9 %all-to-all-start.1 = ((bf16[8,80,2048]{2,1,0:T(8,128)(2,1)}), bf16[8,80,2048]{2,1,0:T(8,128)(2,1)S(1)}, u32[]{:S(2)}, u32[]{:S(2)}) async-start(bf16[8,80,2048]{2,1,0:T(8,128)(2,1)} %bitcast.61), calls=%async_computation.1 | async-start | bytes 5242880 | tf_op jit(solution)/shard_map/grads/all_to_all | solution.py:314
  172.2 8.4 %copy-start.16 = (f32[16,2048]{1,0:T(8,128)S(1)}, f32[16,2048]{1,0:T(8,128)}, u32[]{:S(2)}) copy-start(f32[16,2048]{1,0:T(8,128)} %get-tuple-element.76) | copy-start | bytes 393220
  191.4 20.8 %collective-permute-start.11 = (bf16[80,2048]{1,0:T(8,128)(2,1)}, bf16[80,2048]{1,0:T(8,128)(2,1)S(1)}, u32[]{:S(2)}, u32[]{:S(2)}) collective-permute-start(bf16[80,2048]{1,0:T(8,128)(2,1)} %get-tuple-element.58), channel_id=1, source_target_pairs={{0,1},{1,0},{2,3},{3,2},{4,5},{5,4},{6,7},{7,6},{8,9},{9,8},{10,11... | collective-permute-start | bytes 983048 | tf_op jit(solution)/shard_map/ffar_rows/ppermute | solution.py:22
  193.5 30.1 %collective-permute-start.12 = (bf16[80,2048]{1,0:T(8,128)(2,1)}, bf16[80,2048]{1,0:T(8,128)(2,1)S(1)}, u32[]{:S(2)}, u32[]{:S(2)}) collective-permute-start(bf16[80,2048]{1,0:T(8,128)(2,1)} %get-tuple-element.59), channel_id=1, source_target_pairs={{0,2},{1,3},{2,0},{3,1},{4,6},{5,7},{6,4},{7,5},{8,10},{9,11},{10,... | collective-permute-start | bytes 983048 | tf_op jit(solution)/shard_map/ffar_rows/ppermute | solution.py:22
  194.9 34.7 %collective-permute-start.13 = (bf16[80,2048]{1,0:T(8,128)(2,1)}, bf16[80,2048]{1,0:T(8,128)(2,1)S(1)}, u32[]{:S(2)}, u32[]{:S(2)}) collective-permute-start(bf16[80,2048]{1,0:T(8,128)(2,1)} %get-tuple-element.60), channel_id=1, source_target_pairs={{0,3},{1,2},{2,1},{3,0},{4,7},{5,6},{6,5},{7,4},{8,11},{9,10},{10,... | collective-permute-start | bytes 983048 | tf_op jit(solution)/shard_map/ffar_rows/ppermute | solution.py:22
  194.9 6.5 %copy-start.6 = (bf16[640,3,256]{0,2,1:T(8,128)(2,1)S(1)}, bf16[640,3,256]{0,2,1:T(8,128)(2,1)}, u32[]{:S(2)}) copy-start(bf16[640,3,256]{0,2,1:T(8,128)(2,1)} %copy.21) | copy-start | bytes 2949124
  194.9 6.5 %copy-start.18 = (bf16[640,2048]{1,0:T(8,128)(2,1)S(1)}, bf16[640,2048]{1,0:T(8,128)(2,1)}, u32[]{:S(2)}) copy-start(bf16[640,2048]{1,0:T(8,128)(2,1)} %get-tuple-element.71) | copy-start | bytes 7864324
  201.4 4.1 %copy-start.5 = (bf16[640,3,256]{0,2,1:T(8,128)(2,1)S(1)}, bf16[640,3,256]{0,2,1:T(8,128)(2,1)}, u32[]{:S(2)}) copy-start(bf16[640,3,256]{0,2,1:T(8,128)(2,1)} %copy.20) | copy-start | bytes 2949124
  201.4 4.1 %copy-start.17 = (bf16[640,2048]{1,0:T(8,128)(2,1)S(1)}, bf16[640,2048]{1,0:T(8,128)(2,1)}, u32[]{:S(2)}) copy-start(bf16[640,2048]{1,0:T(8,128)(2,1)} %get-tuple-element.75) | copy-start | bytes 7864324
  212.2 17.4 %copy-start.12 = (bf16[80,2048]{1,0:T(8,128)(2,1)}, bf16[80,2048]{1,0:T(8,128)(2,1)S(1)}, u32[]{:S(2)}) copy-start(bf16[80,2048]{1,0:T(8,128)(2,1)S(1)} %collective-permute-done.11.refs_1_) | copy-start | bytes 983044
  223.6 6.1 %copy-start.13 = (bf16[80,2048]{1,0:T(8,128)(2,1)}, bf16[80,2048]{1,0:T(8,128)(2,1)S(1)}, u32[]{:S(2)}) copy-start(bf16[80,2048]{1,0:T(8,128)(2,1)S(1)} %collective-permute-done.12.refs_2_) | copy-start | bytes 983044
  229.6 0.7 copy-start.14
  238.8 1.6 copy-start
  240.4 69.6 %all-to-all-start.2 = ((bf16[8,80,2048]{2,1,0:T(8,128)(2,1)}), bf16[8,80,2048]{2,1,0:T(8,128)(2,1)}, u32[]{:S(2)}, u32[]{:S(2)}) async-start(bf16[8,80,2048]{2,1,0:T(8,128)(2,1)} %forward_far.1), calls=%async_computation.2 | async-start | bytes 5242880 | tf_op jit(solution)/shard_map/outs/all_to_all | solution.py:314
  246.1 64.0 %copy-start.3 = (bf16[256,640]{1,0:T(8,128)(2,1)S(1)}, bf16[256,640]{1,0:T(8,128)(2,1)}, u32[]{:S(2)}) copy-start(bf16[256,640]{1,0:T(8,128)(2,1)} %spread.1) | copy-start | bytes 983044
  246.1 21.6 %collective-permute-start.17 = (f32[8,2304]{1,0:T(8,128)S(1)}, f32[8,2304]{1,0:T(8,128)S(1)}, u32[]{:S(2)}, u32[]{:S(2)}) collective-permute-start(f32[8,2304]{1,0:T(8,128)S(1)} %pad_maximum_fusion), channel_id=1, source_target_pairs={{0,1},{1,0},{2,3},{3,2},{4,5},{5,4},{6,7},{7,6},{8,9},{9,8},{10,11... | collective-permute-start | bytes 221192 | tf_op jit(solution)/shard_map/sums/ppermute | solution.py:22
  248.1 42.3 %collective-permute-start.18 = (f32[8,2304]{1,0:T(8,128)S(1)}, f32[8,2304]{1,0:T(8,128)S(1)}, u32[]{:S(2)}, u32[]{:S(2)}) collective-permute-start(f32[8,2304]{1,0:T(8,128)S(1)} %pad_maximum_fusion), channel_id=1, source_target_pairs={{0,2},{1,3},{2,0},{3,1},{4,6},{5,7},{6,4},{7,5},{8,10},{9,11},{10,... | collective-permute-start | bytes 221192 | tf_op jit(solution)/shard_map/sums/ppermute | solution.py:22
  249.5 41.7 %collective-permute-start.19 = (f32[8,2304]{1,0:T(8,128)S(1)}, f32[8,2304]{1,0:T(8,128)S(1)}, u32[]{:S(2)}, u32[]{:S(2)}) collective-permute-start(f32[8,2304]{1,0:T(8,128)S(1)} %pad_maximum_fusion), channel_id=1, source_target_pairs={{0,3},{1,2},{2,1},{3,0},{4,7},{5,6},{6,5},{7,4},{8,11},{9,10},{10,... | collective-permute-start | bytes 221192 | tf_op jit(solution)/shard_map/sums/ppermute | solution.py:22
  291.2 17.5 %collective-permute-start.20 = (f32[8,2304]{1,0:T(8,128)S(1)}, f32[8,2304]{1,0:T(8,128)S(1)}, u32[]{:S(2)}, u32[]{:S(2)}) collective-permute-start(f32[8,2304]{1,0:T(8,128)S(1)} %add_add_fusion), channel_id=1, source_target_pairs={{0,4},{1,5},{2,6},{3,7},{4,0},{5,1},{6,2},{7,3},{8,12},{9,13},{10,... | collective-permute-start | bytes 221192 | tf_op jit(solution)/shard_map/sums_far/ppermute | solution.py:22

commit v4 on v3

--- a/solution.py
+++ b/solution.py
@@ -11,6 +11,7 @@
 F32 = jnp.float32
 BF16 = jnp.bfloat16
 VMEM_BYTES = 56 * 1024 * 1024
+SMALL_BYTES = 24 * 1024 * 1024
 LANES = 128
 SCALE = 64
 
@@ -49,7 +50,7 @@
     return lax.broadcasted_iota(jnp.int32, shape, dim)
 
 
-def call(kernel, name, outs, ins, grid=(), in_specs=None, out_specs=None, scratch=(), flops=0):
+def call(kernel, name, outs, ins, grid=(), in_specs=None, out_specs=None, scratch=(), flops=0, limit=SMALL_BYTES):
     whole = pl.BlockSpec(memory_space=pltpu.VMEM)
     moved = sum(a.size * a.dtype.itemsize for a in list(outs) + list(ins))
     return pl.pallas_call(
@@ -59,7 +60,7 @@
         in_specs=in_specs or [whole] * len(ins),
         out_specs=out_specs or [whole] * len(outs),
         scratch_shapes=list(scratch),
-        compiler_params=pltpu.CompilerParams(vmem_limit_bytes=VMEM_BYTES),
+        compiler_params=pltpu.CompilerParams(vmem_limit_bytes=limit),
         cost_estimate=pl.CostEstimate(flops=flops // SCALE, bytes_accessed=moved // SCALE, transcendentals=0),
         name=name,
     )(*ins)
@@ -247,7 +248,7 @@
         sums_ref[experts : experts + 1, span] = gain_sum / gain_ref[:, span]
 
 
-def forward_kernel(half, me_ref, gate_w, up_w, down_w, *refs):
+def forward_kernel(half, flip, me_ref, gate_w, up_w, down_w, *refs):
     pieces, (out_ref, rows_ref) = refs[:half], refs[-2:]
     slots = pieces[0].shape[0]
     for k, piece in enumerate(pieces):
@@ -258,7 +259,8 @@
     columns = 512 if out_ref.shape[2] % 512 == 0 else out_ref.shape[2]
     for c in range(0, out_ref.shape[2], columns):
         result = dot(active, down_w[:, c : c + columns]).astype(BF16)
-        out_ref[:, :, c : c + columns] = result.reshape(half, slots, columns)
+        senders = pl.ds((me_ref[0] // half ^ flip) * half, half)
+        out_ref[senders, :, c : c + columns] = result.reshape(half, slots, columns)
 
 
 def spread_kernel(slots, rank_ref, weight_ref, spread_ref, flat_ref):
@@ -421,6 +423,7 @@
             pltpu.VMEM((count, LANES), BF16),
         ],
         flops=6 * flops,
+        limit=VMEM_BYTES,
     )
     active, gate_part, up_part = (
         jnp.swapaxes(a, 0, 1).reshape(count, hidden) for a in (active, gate_part, up_part)
@@ -436,21 +439,13 @@
 
     def forward_of(pieces, flip, name, *filled):
         return pl.pallas_call(
-            partial(forward_kernel, half),
+            partial(forward_kernel, half, flip),
             out_shape=message,
-            grid_spec=pltpu.PrefetchScalarGridSpec(
-                num_scalar_prefetch=1,
-                grid=(1,),
-                in_specs=[whole(m) for m in mats]
-                + [whole(piece)] * half
-                + [pl.BlockSpec(memory_space=pl.ANY)] * len(filled),
-                out_specs=pl.BlockSpec(
-                    (half, slots, width), lambda i, me_ref: (me_ref[0] // half ^ flip, 0, 0)
-                ),
-                scratch_shapes=[pltpu.VMEM((count // 2, width), BF16)],
-            ),
+            in_specs=[smem] + [vmem] * (3 + half + len(filled)),
+            out_specs=vmem,
+            scratch_shapes=[pltpu.VMEM((count // 2, width), BF16)],
             input_output_aliases={4 + half: 0} if filled else {},
-            compiler_params=pltpu.CompilerParams(vmem_limit_bytes=VMEM_BYTES),
+            compiler_params=pltpu.CompilerParams(vmem_limit_bytes=SMALL_BYTES),
             cost_estimate=pl.CostEstimate(
                 flops=3 * flops // 2, bytes_accessed=6 * width * hidden, transcendentals=0
             ),

time: 315 us -> 310 us (0.984)
  Pallas kernels: 78.3 us -> 51.7 us
  local copies, waits for them, and re-layouts: 12.8 us -> 33.2 us
    unnamed x40 -> x88, local copies, waits for them, and re-layouts: 4.77 us -> 25.8 us
    pallas_call x11, Pallas kernels: 61.4 us -> 45.1 us  [call(): pl.pallas_call(kernel, out_shape=[jax.ShapeDtypeStruct(o.shape, o.dtype)...]
    pallas_call x2, Pallas kernels: 16.9 us -> 6.61 us  [forward_of(): pl.pallas_call(partial(forward_kernel, half, flip), out_shape=message, in...]
  transfers between devices with their start and end apart: 24 -> 24, of which waited for: 14 -> 13; matrix products, arithmetic and copies ran while one was open for 8% -> 8% of each run, Pallas kernels for 25% -> 17%
where the time goes in v4:
time: 310 us; the launch traced here: 309 us
  waiting for transfers between devices  155 us (50%)
  Pallas kernels  51.7 us (17%)
  starting transfers between devices  49.1 us (16%)
  local copies, waits for them, and re-layouts  33.2 us (11%)
  matrix products  18.5 us (6%)
    ppermute x18, waiting for transfers between devices, hop(): lax.ppermute(block, 'expert', [(e, e ^ flip) for e in range(experts)])  144 us
    pallas_call x11, Pallas kernels, call(): pl.pallas_call(kernel, out_shape=[jax.ShapeDtypeStruct(o.shape, o.dtype)...  45.1 us
    ppermute x18, starting transfers between devices, hop(): lax.ppermute(block, 'expert', [(e, e ^ flip) for e in range(experts)])  28.4 us
    unnamed x88, local copies, waits for them, and re-layouts  25.8 us
    all_to_all x3, starting transfers between devices, exchange(): lax.all_to_all(array, 'expert', 0, 0, tiled=True, axis_index_groups=groups)  16.5 us
    dot_general x3, matrix products, t_dot(): lax.dot_general(a, b, dims, preferred_element_type=F32, precision=precision)  14.5 us
    ppermute x3, waiting for transfers between devices, hop(): return lax.ppermute(block, ('pipe', 'expert'), route)  9.99 us
    transpose x3, local copies, waits for them, and re-layouts, per_device(): jnp.swapaxes(a, 0, 1).reshape(count, hidden)  6.77 us
  transfers between devices with their start and end apart: 24, of which 13 were waited for; matrix products, arithmetic and copies ran while one was open for 8% of the time, Pallas kernels for 17%

profile of v4, /device:TPU:0, one launch (start us, length us, event | category | flops | bytes accessed | tf_op | source)
XLA Modules:
  0.0 309.2 jit_solution(6839690560931868263)
XLA Ops:
  0.6 2.5 collective-permute-start.1
  3.1 2.6 collective-permute-start.2
  6.7 1.2 copy-done.11
  7.9 0.8 copy-done.16
  9.4 2.6 own_rows.1
  12.7 1.5 collective-permute-start.4
  14.2 1.6 collective-permute-start.5
  16.2 2.1 collective-permute-start.3
  18.3 3.1 cots.1
  21.4 30.2 %collective-permute-done.3.table_ref.refs_4_ = s32[6,256]{1,0:T(8,128)S(1)} collective-permute-done((s32[6,256]{1,0:T(8,128)S(1)}, s32[6,256]{1,0:T(8,128)S(1)}, u32[]{:S(2)}, u32[]{:S(2)}) %collective-permute-start.3) | collective-permute-done | bytes 6176 | tf_op jit(solution)/shard_map/tables/ppermute | solution.py:23
  51.7 0.7 copy-done.35
  53.2 5.7 %all-to-all-start = ((bf16[8,80,2048]{2,1,0:T(8,128)(2,1)}), bf16[8,80,2048]{2,1,0:T(8,128)(2,1)}, u32[]{:S(2)}, u32[]{:S(2)}) async-start(bf16[8,80,2048]{2,1,0:T(8,128)(2,1)} %cots.1), calls=%async_computation | async-start | bytes 5242880 | tf_op jit(solution)/shard_map/cots/all_to_all | solution.py:316
  59.1 2.6 far_rows.1
  61.7 2.1 collective-permute-start.7
  63.8 1.5 collective-permute-start.8
  65.4 23.5 %collective-permute-done.7.refs_15_ = bf16[80,2176]{1,0:T(8,128)(2,1)S(1)} collective-permute-done((bf16[80,2176]{1,0:T(8,128)(2,1)S(1)}, bf16[80,2176]{1,0:T(8,128)(2,1)S(1)}, u32[]{:S(2)}, u32[]{:S(2)}) %collective-permute-start.7) | collective-permute-done | bytes 348192 | tf_op jit(solution)/shard_map/far_rows/ppermute | solution.py:23
  88.9 22.1 %collective-permute-done.8.refs_16_ = bf16[80,2176]{1,0:T(8,128)(2,1)S(1)} collective-permute-done((bf16[80,2176]{1,0:T(8,128)(2,1)S(1)}, bf16[80,2176]{1,0:T(8,128)(2,1)S(1)}, u32[]{:S(2)}, u32[]{:S(2)}) %collective-permute-start.8) | collective-permute-done | bytes 348192 | tf_op jit(solution)/shard_map/far_rows/ppermute | solution.py:23
  111.0 6.5 %collective-permute-done.9.refs_17_ = bf16[80,2176]{1,0:T(8,128)(2,1)S(1)} collective-permute-done((bf16[80,2176]{1,0:T(8,128)(2,1)S(1)}, bf16[80,2176]{1,0:T(8,128)(2,1)S(1)}, u32[]{:S(2)}, u32[]{:S(2)}) %collective-permute-start.9) | collective-permute-done | bytes 348192 | tf_op jit(solution)/shard_map/far_rows/ppermute | solution.py:23
  117.5 1.2 all-to-all-done.refs_9_
  118.6 1.7 collective-permute-start.10
  120.4 2.2 fown_rows.1
  123.9 0.9 collective-permute-start.15
  124.8 2.0 collective-permute-start.16
  127.2 28.2 %expert.1 = (bf16[640,2048]{1,0:T(8,128)(2,1)}, bf16[640,2048]{1,0:T(8,128)(2,1)}, bf16[640,2048]{1,0:T(8,128)(2,1)}, bf16[3,640,256]{2,1,0:T(8,128)(2,1)}, bf16...) custom-call(s32[1]{0:T(128)} %bitcast.5.refs_0_.me_ref, bf16[2048,768]{1,0:T(8,128)(2,1)} %bitcast.46, ...), custom_call_target="tpu_custom_call" | custom-call | flops 188743680 | bytes 551040 | tf_op jit(solution)/shard_map/expert/pallas_call | solution.py:56
  155.4 0.7 copy-done.23
  157.6 10.0 %collective-permute-done.10.refs_1_ = bf16[256,2048]{1,0:T(8,128)(2,1)S(1)} collective-permute-done((bf16[256,2048]{1,0:T(8,128)(2,1)}, bf16[256,2048]{1,0:T(8,128)(2,1)S(1)}, u32[]{:S(2)}, u32[]{:S(2)}) %collective-permute-start.10) | collective-permute-done | bytes 1048608 | tf_op jit(solution)/shard_map/x_far/ppermute | solution.py:29
  167.6 1.0 copy-done.14
  168.5 4.9 %all-to-all-start.1 = ((bf16[8,80,2048]{2,1,0:T(8,128)(2,1)}), bf16[8,80,2048]{2,1,0:T(8,128)(2,1)S(1)}, u32[]{:S(2)}, u32[]{:S(2)}) async-start(bf16[8,80,2048]{2,1,0:T(8,128)(2,1)} %bitcast.66), calls=%async_computation.1 | async-start | bytes 5242880 | tf_op jit(solution)/shard_map/grads/all_to_all | solution.py:316
  173.4 1.9 copy-done
  175.3 1.9 copy-done.2
  177.2 1.9 copy-done.4
  179.1 1.0 copy-done.22
  180.1 1.0 copy-done.24
  181.0 1.0 copy-done.26
  182.0 1.0 copy-done.28
  183.0 3.3 %forward_own.1.refs_4_ = bf16[8,80,2048]{2,1,0:T(8,128)(2,1)S(1)} custom-call(s32[1]{0:T(128)} %bitcast.5.refs_0_.me_ref, bf16[2048,768]{1,0:T(8,128)(2,1)S(1)} %bitcast.48, bf16[2048,768]{1,0:T(8,128)(2,1)S(1)} %bitcast.52, bf16[768,2048]{1,0:T(8,128)(2,1)S(1)} %bitcast.56, bf16[80,2048]{1,0:T(8,128)(2,1)S(1)} %copy-done.22, ...), custom_call_target="tpu_custom_call" | custom-call | flops 3019898880 | bytes 9437184 | tf_op jit(solution)/shard_map/forward_own/pallas_call | solution.py:441
  186.3 1.5 copy-done.6
  187.9 2.2 copy.20
  190.1 2.3 copy.22
  192.4 2.3 copy.21
  194.7 1.2 copy-done.15
  195.9 2.8 ffar_rows.1
  198.7 2.0 collective-permute-start.11
  200.7 1.5 collective-permute-start.12
  202.2 6.5 %convolution_convert_fusion.1 = bf16[2048,768]{1,0:T(8,128)(2,1)} fusion(bf16[640,2048]{1,0:T(8,128)(2,1)} %get-tuple-element.71, bf16[640,768]{0,1:T(8,128)(2,1)} %bitcast.73), kind=kOutput, calls=%fused_computation.1 | convolution fusion | flops 2014838784 | bytes 6750208 | tf_op jit(solution)/shard_map/dot_general | solution.py:46
  208.7 4.1 %convolution_convert_fusion.2 = bf16[2048,768]{1,0:T(8,128)(2,1)} fusion(bf16[640,2048]{1,0:T(8,128)(2,1)S(1)} %copy-done.42, bf16[640,768]{0,1:T(8,128)(2,1)S(1)} %bitcast.72), kind=kOutput, calls=%fused_computation.2 | convolution fusion | flops 2014838784 | bytes 6750208 | tf_op jit(solution)/shard_map/dot_general | solution.py:46
  212.8 4.0 %convolution_convert_fusion = bf16[768,2048]{1,0:T(8,128)(2,1)} fusion(bf16[640,768]{0,1:T(8,128)(2,1)S(1)} %bitcast.71, bf16[640,2048]{1,0:T(8,128)(2,1)S(1)} %copy-done.41), kind=kOutput, calls=%fused_computation | convolution fusion | flops 2014838784 | bytes 6750208 | tf_op jit(solution)/shard_map/dot_general | solution.py:46
  216.8 2.8 collective-permute-done.11.refs_1_
  219.6 5.1 %collective-permute-done.12.refs_2_ = bf16[80,2048]{1,0:T(8,128)(2,1)S(1)} collective-permute-done((bf16[80,2048]{1,0:T(8,128)(2,1)S(1)}, bf16[80,2048]{1,0:T(8,128)(2,1)S(1)}, u32[]{:S(2)}, u32[]{:S(2)}) %collective-permute-start.12) | collective-permute-done | bytes 327712 | tf_op jit(solution)/shard_map/ffar_rows/ppermute | solution.py:23
  224.7 5.9 %collective-permute-done.13.refs_3_ = bf16[80,2048]{1,0:T(8,128)(2,1)S(1)} collective-permute-done((bf16[80,2048]{1,0:T(8,128)(2,1)S(1)}, bf16[80,2048]{1,0:T(8,128)(2,1)S(1)}, u32[]{:S(2)}, u32[]{:S(2)}) %collective-permute-start.13) | collective-permute-done | bytes 327712 | tf_op jit(solution)/shard_map/ffar_rows/ppermute | solution.py:23
  230.6 3.3 %forward_far.1 = bf16[8,80,2048]{2,1,0:T(8,128)(2,1)S(1)} custom-call(s32[1]{0:T(128)} %bitcast.5.refs_0_.me_ref, bf16[2048,768]{1,0:T(8,128)(2,1)S(1)} %bitcast.49, bf16[2048,768]{1,0:T(8,128)(2,1)S(1)} %bitcast.53, bf16[768,2048]{1,0:T(8,128)(2,1)S(1)} %bitcast.57, bf16[80,2048]{1,0:T(8,128)(2,1)S(1)} %get-tuple-element.57.refs_0_, ...), custom_call_target="tpu_custom_call", output_to_operand_aliasing={{}: (8, {})} | custom-call | flops 3019898880 | bytes 9437184 | tf_op jit(solution)/shard_map/forward_far/pallas_call | solution.py:441
  234.0 1.5 copy-done.8
  235.5 5.9 %all-to-all-start.2 = ((bf16[8,80,2048]{2,1,0:T(8,128)(2,1)}), bf16[8,80,2048]{2,1,0:T(8,128)(2,1)}, u32[]{:S(2)}, u32[]{:S(2)}) async-start(bf16[8,80,2048]{2,1,0:T(8,128)(2,1)} %copy-done.8), calls=%async_computation.2 | async-start | bytes 5242880 | tf_op jit(solution)/shard_map/outs/all_to_all | solution.py:316
  241.4 2.0 collective-permute-start.17
  243.4 1.5 collective-permute-start.18
  245.2 1.2 copy-done.10
  246.4 1.2 copy-done.12
  247.6 2.8 source.1
  250.5 12.4 %collective-permute-done.17 = f32[8,2304]{1,0:T(8,128)S(1)} collective-permute-done((f32[8,2304]{1,0:T(8,128)S(1)}, f32[8,2304]{1,0:T(8,128)S(1)}, u32[]{:S(2)}, u32[]{:S(2)}) %collective-permute-start.17) | collective-permute-done | bytes 73760 | tf_op jit(solution)/shard_map/sums/ppermute | solution.py:23
  262.9 22.6 %collective-permute-done.18 = f32[8,2304]{1,0:T(8,128)S(1)} collective-permute-done((f32[8,2304]{1,0:T(8,128)S(1)}, f32[8,2304]{1,0:T(8,128)S(1)}, u32[]{:S(2)}, u32[]{:S(2)}) %collective-permute-start.18) | collective-permute-done | bytes 73760 | tf_op jit(solution)/shard_map/sums/ppermute | solution.py:23
  285.5 0.8 collective-permute-done.19
  286.3 5.8 %collective-permute-start.20 = (f32[8,2304]{1,0:T(8,128)S(1)}, f32[8,2304]{1,0:T(8,128)S(1)}, u32[]{:S(2)}, u32[]{:S(2)}) collective-permute-start(f32[8,2304]{1,0:T(8,128)S(1)} %add_add_fusion), channel_id=1, source_target_pairs={{0,4},{1,5},{2,6},{3,7},{4,0},{5,1},{6,2},{7,3},{8,12},{9,13},{10,... | collective-permute-start | bytes 221192 | tf_op jit(solution)/shard_map/sums_far/ppermute | solution.py:23
  292.1 11.8 %collective-permute-done.20 = f32[8,2304]{1,0:T(8,128)S(1)} collective-permute-done((f32[8,2304]{1,0:T(8,128)S(1)}, f32[8,2304]{1,0:T(8,128)S(1)}, u32[]{:S(2)}, u32[]{:S(2)}) %collective-permute-start.20) | collective-permute-done | bytes 73760 | tf_op jit(solution)/shard_map/sums_far/ppermute | solution.py:23
  305.2 4.0 %fusion = bf16[1,256,2048]{2,1,0:T(8,128)(2,1)} fusion(bf16[256,2048]{1,0:T(8,128)(2,1)} %copy-done.13, bf16[256,640]{1,0:T(8,128)(2,1)S(1)} %spread.1, bf16[640,2048]{1,0:T(8,128)(2,1)} %bitcast.21), kind=kOutput, calls=%fused_computation.4 | convolution fusion | flops 672661504 | bytes 5046272 | tf_op jit(solution)/shard_map/dot_general | solution.py:37
  (101 shorter events, 8.8 us)
Async XLA Ops:
  0.6 15.5 %collective-permute-start.1 = (bf16[256,2048]{1,0:T(8,128)(2,1)}, bf16[256,2048]{1,0:T(8,128)(2,1)S(1)}, u32[]{:S(2)}, u32[]{:S(2)}) collective-permute-start(bf16[256,2048]{1,0:T(8,128)(2,1)} %bitcast.77), channel_id=1, source_target_pairs={{0,24},{1,25},{2,26},{3,27},{4,28},{5,29},{6,30},{7,31},{8,0},{9,1... | collective-permute-start | bytes 3145736 | tf_op jit(solution)/shard_map/dy_in/ppermute | solution.py:29
  3.1 50.1 %collective-permute-start.2 = (bf16[256,2048]{1,0:T(8,128)(2,1)}, bf16[256,2048]{1,0:T(8,128)(2,1)S(1)}, u32[]{:S(2)}, u32[]{:S(2)}) collective-permute-start(bf16[256,2048]{1,0:T(8,128)(2,1)} %bitcast.58), channel_id=1, source_target_pairs={{0,4},{1,5},{2,6},{3,7},{4,0},{5,1},{6,2},{7,3},{8,12},{9,13},{10,... | collective-permute-start | bytes 3145736 | tf_op jit(solution)/shard_map/xp_far/ppermute | solution.py:23
  6.7 1.2 copy-start.11
  7.9 0.8 copy-start.16
  11.9 0.7 copy-start.19
  12.7 39.0 %collective-permute-start.4 = (bf16[80,2176]{1,0:T(8,128)(2,1)S(1)}, bf16[80,2176]{1,0:T(8,128)(2,1)S(1)}, u32[]{:S(2)}, u32[]{:S(2)}) collective-permute-start(bf16[80,2176]{1,0:T(8,128)(2,1)S(1)} %get-tuple-element.47), channel_id=1, source_target_pairs={{0,1},{1,0},{2,3},{3,2},{4,5},{5,4},{6,7},{7,6},{8,9},{9,8},{10,11... | collective-permute-start | bytes 1044488 | tf_op jit(solution)/shard_map/own_rows/ppermute | solution.py:23
  14.2 37.5 %collective-permute-start.5 = (bf16[80,2176]{1,0:T(8,128)(2,1)S(1)}, bf16[80,2176]{1,0:T(8,128)(2,1)S(1)}, u32[]{:S(2)}, u32[]{:S(2)}) collective-permute-start(bf16[80,2176]{1,0:T(8,128)(2,1)S(1)} %get-tuple-element.48), channel_id=1, source_target_pairs={{0,2},{1,3},{2,0},{3,1},{4,6},{5,7},{6,4},{7,5},{8,10},{9,11},{10,... | collective-permute-start | bytes 1044488 | tf_op jit(solution)/shard_map/own_rows/ppermute | solution.py:23
  15.8 35.9 %collective-permute-start.6 = (bf16[80,2176]{1,0:T(8,128)(2,1)S(1)}, bf16[80,2176]{1,0:T(8,128)(2,1)S(1)}, u32[]{:S(2)}, u32[]{:S(2)}) collective-permute-start(bf16[80,2176]{1,0:T(8,128)(2,1)S(1)} %get-tuple-element.49), channel_id=1, source_target_pairs={{0,3},{1,2},{2,1},{3,0},{4,7},{5,6},{6,5},{7,4},{8,11},{9,10},{10,... | collective-permute-start | bytes 1044488 | tf_op jit(solution)/shard_map/own_rows/ppermute | solution.py:23
  16.2 37.0 %copy-start.9 = (bf16[256,2048]{1,0:T(8,128)(2,1)}, bf16[256,2048]{1,0:T(8,128)(2,1)S(1)}, u32[]{:S(2)}) copy-start(bf16[256,2048]{1,0:T(8,128)(2,1)S(1)} %collective-permute-done.1.x_ref.dy_ref) | copy-start | bytes 3145732
  16.2 35.5 %collective-permute-start.3 = (s32[6,256]{1,0:T(8,128)S(1)}, s32[6,256]{1,0:T(8,128)S(1)}, u32[]{:S(2)}, u32[]{:S(2)}) collective-permute-start(s32[6,256]{1,0:T(8,128)S(1)} %pad_add_fusion.table_ref.refs_4_), channel_id=1, source_target_pairs={{0,4},{1,5},{2,6},{3,7},{4,0},{5,1},{6,2},{7,3},{8,12},{9,13},{10,... | collective-permute-start | bytes 18440 | tf_op jit(solution)/shard_map/tables/ppermute | solution.py:23
  21.4 37.7 %copy-start.17 = (bf16[1,2048,8]{1,2,0:T(8,128)(2,1)S(1)}, bf16[1,2048,8]{1,2,0:T(8,128)(2,1)}, u32[]{:S(2)}) copy-start(bf16[1,2048,8]{1,2,0:T(8,128)(2,1)} %param.18) | copy-start | bytes 98308
  21.4 37.7 %copy-start.30 = (f32[1,2048]{1,0:T(1,128)S(1)}, f32[1,2048]{1,0:T(1,128)}, u32[]{:S(2)}) copy-start(f32[1,2048]{1,0:T(1,128)} %gain_ref.1) | copy-start | bytes 24580
  51.6 1.5 copy-start.34
  51.6 0.8 copy-start.35
  52.4 0.7 copy-start.36
  53.2 65.5 %all-to-all-start = ((bf16[8,80,2048]{2,1,0:T(8,128)(2,1)}), bf16[8,80,2048]{2,1,0:T(8,128)(2,1)}, u32[]{:S(2)}, u32[]{:S(2)}) async-start(bf16[8,80,2048]{2,1,0:T(8,128)(2,1)} %cots.1), calls=%async_computation | async-start | bytes 5242880 | tf_op jit(solution)/shard_map/cots/all_to_all | solution.py:316
  61.7 65.4 %copy-start.20 = (bf16[80,2176]{1,0:T(8,128)(2,1)}, bf16[80,2176]{1,0:T(8,128)(2,1)S(1)}, u32[]{:S(2)}) copy-start(bf16[80,2176]{1,0:T(8,128)(2,1)S(1)} %get-tuple-element.66.refs_14_) | copy-start | bytes 1044484
  61.7 27.1 %collective-permute-start.7 = (bf16[80,2176]{1,0:T(8,128)(2,1)S(1)}, bf16[80,2176]{1,0:T(8,128)(2,1)S(1)}, u32[]{:S(2)}, u32[]{:S(2)}) collective-permute-start(bf16[80,2176]{1,0:T(8,128)(2,1)S(1)} %get-tuple-element.52), channel_id=1, source_target_pairs={{0,1},{1,0},{2,3},{3,2},{4,5},{5,4},{6,7},{7,6},{8,9},{9,8},{10,11... | collective-permute-start | bytes 1044488 | tf_op jit(solution)/shard_map/far_rows/ppermute | solution.py:23
  63.8 47.1 %collective-permute-start.8 = (bf16[80,2176]{1,0:T(8,128)(2,1)S(1)}, bf16[80,2176]{1,0:T(8,128)(2,1)S(1)}, u32[]{:S(2)}, u32[]{:S(2)}) collective-permute-start(bf16[80,2176]{1,0:T(8,128)(2,1)S(1)} %get-tuple-element.53), channel_id=1, source_target_pairs={{0,2},{1,3},{2,0},{3,1},{4,6},{5,7},{6,4},{7,5},{8,10},{9,11},{10,... | collective-permute-start | bytes 1044488 | tf_op jit(solution)/shard_map/far_rows/ppermute | solution.py:23
  65.3 52.2 %collective-permute-start.9 = (bf16[80,2176]{1,0:T(8,128)(2,1)S(1)}, bf16[80,2176]{1,0:T(8,128)(2,1)S(1)}, u32[]{:S(2)}, u32[]{:S(2)}) collective-permute-start(bf16[80,2176]{1,0:T(8,128)(2,1)S(1)} %get-tuple-element.54), channel_id=1, source_target_pairs={{0,3},{1,2},{2,1},{3,0},{4,7},{5,6},{6,5},{7,4},{8,11},{9,10},{10,... | collective-permute-start | bytes 1044488 | tf_op jit(solution)/shard_map/far_rows/ppermute | solution.py:23
  65.4 55.0 %collective-permute-start = (bf16[256,2048]{1,0:T(8,128)(2,1)}, bf16[256,2048]{1,0:T(8,128)(2,1)S(1)}, u32[]{:S(2)}, u32[]{:S(2)}) collective-permute-start(bf16[256,2048]{1,0:T(8,128)(2,1)} %bitcast.78), channel_id=1, source_target_pairs={{0,8},{1,9},{2,10},{3,11},{4,12},{5,13},{6,14},{7,15},{8,16},{9,17... | collective-permute-start | bytes 3145736 | tf_op jit(solution)/shard_map/x_in/ppermute | solution.py:29
  88.9 38.3 %copy-start.37 = (bf16[80,2176]{1,0:T(8,128)(2,1)}, bf16[80,2176]{1,0:T(8,128)(2,1)S(1)}, u32[]{:S(2)}) copy-start(bf16[80,2176]{1,0:T(8,128)(2,1)S(1)} %collective-permute-done.7.refs_15_) | copy-start | bytes 1044484
  110.9 16.2 %copy-start.38 = (bf16[80,2176]{1,0:T(8,128)(2,1)}, bf16[80,2176]{1,0:T(8,128)(2,1)S(1)}, u32[]{:S(2)}) copy-start(bf16[80,2176]{1,0:T(8,128)(2,1)S(1)} %collective-permute-done.8.refs_16_) | copy-start | bytes 1044484
  117.5 9.7 %copy-start.39 = (bf16[80,2176]{1,0:T(8,128)(2,1)}, bf16[80,2176]{1,0:T(8,128)(2,1)S(1)}, u32[]{:S(2)}) copy-start(bf16[80,2176]{1,0:T(8,128)(2,1)S(1)} %collective-permute-done.9.refs_17_) | copy-start | bytes 1044484
  118.6 48.9 %collective-permute-start.10 = (bf16[256,2048]{1,0:T(8,128)(2,1)}, bf16[256,2048]{1,0:T(8,128)(2,1)S(1)}, u32[]{:S(2)}, u32[]{:S(2)}) collective-permute-start(bf16[256,2048]{1,0:T(8,128)(2,1)} %bitcast.79), channel_id=1, source_target_pairs={{0,12},{1,13},{2,14},{3,15},{4,8},{5,9},{6,10},{7,11},{8,20},{9,21... | collective-permute-start | bytes 3145736 | tf_op jit(solution)/shard_map/x_far/ppermute | solution.py:29
  120.4 35.0 %copy-start.13 = (bf16[256,2048]{1,0:T(8,128)(2,1)}, bf16[256,2048]{1,0:T(8,128)(2,1)S(1)}, u32[]{:S(2)}) copy-start(bf16[256,2048]{1,0:T(8,128)(2,1)S(1)} %collective-permute-done.refs_1_) | copy-start | bytes 3145732
  122.6 0.7 copy-start.21
  123.3 32.1 %collective-permute-start.14 = (bf16[80,2048]{1,0:T(8,128)(2,1)S(1)}, bf16[80,2048]{1,0:T(8,128)(2,1)S(1)}, u32[]{:S(2)}, u32[]{:S(2)}) collective-permute-start(bf16[80,2048]{1,0:T(8,128)(2,1)S(1)} %get-tuple-element.62), channel_id=1, source_target_pairs={{0,1},{1,0},{2,3},{3,2},{4,5},{5,4},{6,7},{7,6},{8,9},{9,8},{10,11... | collective-permute-start | bytes 983048 | tf_op jit(solution)/shard_map/fown_rows/ppermute | solution.py:23
  123.9 32.2 %collective-permute-start.15 = (bf16[80,2048]{1,0:T(8,128)(2,1)S(1)}, bf16[80,2048]{1,0:T(8,128)(2,1)S(1)}, u32[]{:S(2)}, u32[]{:S(2)}) collective-permute-start(bf16[80,2048]{1,0:T(8,128)(2,1)S(1)} %get-tuple-element.63), channel_id=1, source_target_pairs={{0,2},{1,3},{2,0},{3,1},{4,6},{5,7},{6,4},{7,5},{8,10},{9,11},{10,... | collective-permute-start | bytes 983048 | tf_op jit(solution)/shard_map/fown_rows/ppermute | solution.py:23
  124.8 32.1 %collective-permute-start.16 = (bf16[80,2048]{1,0:T(8,128)(2,1)S(1)}, bf16[80,2048]{1,0:T(8,128)(2,1)S(1)}, u32[]{:S(2)}, u32[]{:S(2)}) collective-permute-start(bf16[80,2048]{1,0:T(8,128)(2,1)S(1)} %get-tuple-element.64), channel_id=1, source_target_pairs={{0,3},{1,2},{2,1},{3,0},{4,7},{5,6},{6,5},{7,4},{8,11},{9,10},{10,... | collective-permute-start | bytes 983048 | tf_op jit(solution)/shard_map/fown_rows/ppermute | solution.py:23
  155.4 0.8 copy-start.23
  167.6 1.0 copy-start.14
  168.5 66.9 %all-to-all-start.1 = ((bf16[8,80,2048]{2,1,0:T(8,128)(2,1)}), bf16[8,80,2048]{2,1,0:T(8,128)(2,1)S(1)}, u32[]{:S(2)}, u32[]{:S(2)}) async-start(bf16[8,80,2048]{2,1,0:T(8,128)(2,1)} %bitcast.66), calls=%async_computation.1 | async-start | bytes 5242880 | tf_op jit(solution)/shard_map/grads/all_to_all | solution.py:316
  173.4 1.9 copy-start
  175.3 1.9 copy-start.2
  177.2 1.9 copy-start.4
  179.1 1.0 copy-start.22
  180.1 1.0 copy-start.24
  181.0 1.0 copy-start.26
  182.0 1.0 copy-start.28
  183.0 4.8 %copy-start.40 = (f32[16,2048]{1,0:T(8,128)S(1)}, f32[16,2048]{1,0:T(8,128)}, u32[]{:S(2)}) copy-start(f32[16,2048]{1,0:T(8,128)} %get-tuple-element.76) | copy-start | bytes 393220
  186.3 1.6 copy-start.6
  187.9 6.8 %copy-start.18 = (bf16[1,2048,8]{1,2,0:T(8,128)(2,1)S(1)}, bf16[1,2048,8]{1,2,0:T(8,128)(2,1)}, u32[]{:S(2)}) copy-start(bf16[1,2048,8]{1,2,0:T(8,128)(2,1)} %param.18) | copy-start | bytes 98308
  187.9 6.8 %copy-start.31 = (f32[1,2048]{1,0:T(1,128)S(1)}, f32[1,2048]{1,0:T(1,128)}, u32[]{:S(2)}) copy-start(f32[1,2048]{1,0:T(1,128)} %gain_ref.1) | copy-start | bytes 24580
  194.7 1.2 copy-start.15
  198.7 20.8 %collective-permute-start.11 = (bf16[80,2048]{1,0:T(8,128)(2,1)S(1)}, bf16[80,2048]{1,0:T(8,128)(2,1)S(1)}, u32[]{:S(2)}, u32[]{:S(2)}) collective-permute-start(bf16[80,2048]{1,0:T(8,128)(2,1)S(1)} %get-tuple-element.58), channel_id=1, source_target_pairs={{0,1},{1,0},{2,3},{3,2},{4,5},{5,4},{6,7},{7,6},{8,9},{9,8},{10,11... | collective-permute-start | bytes 983048 | tf_op jit(solution)/shard_map/ffar_rows/ppermute | solution.py:23
  200.7 23.9 %collective-permute-start.12 = (bf16[80,2048]{1,0:T(8,128)(2,1)S(1)}, bf16[80,2048]{1,0:T(8,128)(2,1)S(1)}, u32[]{:S(2)}, u32[]{:S(2)}) collective-permute-start(bf16[80,2048]{1,0:T(8,128)(2,1)S(1)} %get-tuple-element.59), channel_id=1, source_target_pairs={{0,2},{1,3},{2,0},{3,1},{4,6},{5,7},{6,4},{7,5},{8,10},{9,11},{10,... | collective-permute-start | bytes 983048 | tf_op jit(solution)/shard_map/ffar_rows/ppermute | solution.py:23
  202.2 28.4 %collective-permute-start.13 = (bf16[80,2048]{1,0:T(8,128)(2,1)S(1)}, bf16[80,2048]{1,0:T(8,128)(2,1)S(1)}, u32[]{:S(2)}, u32[]{:S(2)}) collective-permute-start(bf16[80,2048]{1,0:T(8,128)(2,1)S(1)} %get-tuple-element.60), channel_id=1, source_target_pairs={{0,3},{1,2},{2,1},{3,0},{4,7},{5,6},{6,5},{7,4},{8,11},{9,10},{10,... | collective-permute-start | bytes 983048 | tf_op jit(solution)/shard_map/ffar_rows/ppermute | solution.py:23
  202.2 6.5 %copy-start.33 = (bf16[640,3,256]{0,2,1:T(8,128)(2,1)S(1)}, bf16[640,3,256]{0,2,1:T(8,128)(2,1)}, u32[]{:S(2)}) copy-start(bf16[640,3,256]{0,2,1:T(8,128)(2,1)} %copy.21) | copy-start | bytes 2949124
  202.2 6.5 %copy-start.42 = (bf16[640,2048]{1,0:T(8,128)(2,1)S(1)}, bf16[640,2048]{1,0:T(8,128)(2,1)}, u32[]{:S(2)}) copy-start(bf16[640,2048]{1,0:T(8,128)(2,1)} %get-tuple-element.71) | copy-start | bytes 7864324
  208.7 4.1 %copy-start.32 = (bf16[640,3,256]{0,2,1:T(8,128)(2,1)S(1)}, bf16[640,3,256]{0,2,1:T(8,128)(2,1)}, u32[]{:S(2)}) copy-start(bf16[640,3,256]{0,2,1:T(8,128)(2,1)} %copy.20) | copy-start | bytes 2949124
  208.7 4.1 %copy-start.41 = (bf16[640,2048]{1,0:T(8,128)(2,1)S(1)}, bf16[640,2048]{1,0:T(8,128)(2,1)}, u32[]{:S(2)}) copy-start(bf16[640,2048]{1,0:T(8,128)(2,1)} %get-tuple-element.75) | copy-start | bytes 7864324
  208.7 21.9 %copy-start.7 = (bf16[8,80,2048]{2,1,0:T(8,128)(2,1)S(1)}, bf16[8,80,2048]{2,1,0:T(8,128)(2,1)}, u32[]{:S(2)}) copy-start(bf16[8,80,2048]{2,1,0:T(8,128)(2,1)} %copy-done.6) | copy-start | bytes 7864324
  212.8 17.8 %copy-start.1 = (bf16[1,1,2048,768]{3,2,1,0:T(8,128)(2,1)S(1)}, bf16[1,1,2048,768]{3,2,1,0:T(8,128)(2,1)}, u32[]{:S(2)}) copy-start(bf16[1,1,2048,768]{3,2,1,0:T(8,128)(2,1)} %param.15) | copy-start | bytes 9437188
  212.8 17.8 %copy-start.3 = (bf16[1,1,2048,768]{3,2,1,0:T(8,128)(2,1)S(1)}, bf16[1,1,2048,768]{3,2,1,0:T(8,128)(2,1)}, u32[]{:S(2)}) copy-start(bf16[1,1,2048,768]{3,2,1,0:T(8,128)(2,1)} %param.16) | copy-start | bytes 9437188
  212.8 17.8 %copy-start.5 = (bf16[1,1,768,2048]{3,2,1,0:T(8,128)(2,1)S(1)}, bf16[1,1,768,2048]{3,2,1,0:T(8,128)(2,1)}, u32[]{:S(2)}) copy-start(bf16[1,1,768,2048]{3,2,1,0:T(8,128)(2,1)} %param.17) | copy-start | bytes 9437188
  234.0 1.5 copy-start.8
  235.5 69.7 %all-to-all-start.2 = ((bf16[8,80,2048]{2,1,0:T(8,128)(2,1)}), bf16[8,80,2048]{2,1,0:T(8,128)(2,1)}, u32[]{:S(2)}, u32[]{:S(2)}) async-start(bf16[8,80,2048]{2,1,0:T(8,128)(2,1)} %copy-done.8), calls=%async_computation.2 | async-start | bytes 5242880 | tf_op jit(solution)/shard_map/outs/all_to_all | solution.py:316
  241.4 21.5 %collective-permute-start.17 = (f32[8,2304]{1,0:T(8,128)S(1)}, f32[8,2304]{1,0:T(8,128)S(1)}, u32[]{:S(2)}, u32[]{:S(2)}) collective-permute-start(f32[8,2304]{1,0:T(8,128)S(1)} %pad_maximum_fusion), channel_id=1, source_target_pairs={{0,1},{1,0},{2,3},{3,2},{4,5},{5,4},{6,7},{7,6},{8,9},{9,8},{10,11... | collective-permute-start | bytes 221192 | tf_op jit(solution)/shard_map/sums/ppermute | solution.py:23
  243.4 42.1 %collective-permute-start.18 = (f32[8,2304]{1,0:T(8,128)S(1)}, f32[8,2304]{1,0:T(8,128)S(1)}, u32[]{:S(2)}, u32[]{:S(2)}) collective-permute-start(f32[8,2304]{1,0:T(8,128)S(1)} %pad_maximum_fusion), channel_id=1, source_target_pairs={{0,2},{1,3},{2,0},{3,1},{4,6},{5,7},{6,4},{7,5},{8,10},{9,11},{10,... | collective-permute-start | bytes 221192 | tf_op jit(solution)/shard_map/sums/ppermute | solution.py:23
  244.9 41.4 %collective-permute-start.19 = (f32[8,2304]{1,0:T(8,128)S(1)}, f32[8,2304]{1,0:T(8,128)S(1)}, u32[]{:S(2)}, u32[]{:S(2)}) collective-permute-start(f32[8,2304]{1,0:T(8,128)S(1)} %pad_maximum_fusion), channel_id=1, source_target_pairs={{0,3},{1,2},{2,1},{3,0},{4,7},{5,6},{6,5},{7,4},{8,11},{9,10},{10,... | collective-permute-start | bytes 221192 | tf_op jit(solution)/shard_map/sums/ppermute | solution.py:23
  245.2 1.2 copy-start.10
  246.4 1.2 copy-start.12
  286.3 17.6 %collective-permute-start.20 = (f32[8,2304]{1,0:T(8,128)S(1)}, f32[8,2304]{1,0:T(8,128)S(1)}, u32[]{:S(2)}, u32[]{:S(2)}) collective-permute-start(f32[8,2304]{1,0:T(8,128)S(1)} %add_add_fusion), channel_id=1, source_target_pairs={{0,4},{1,5},{2,6},{3,7},{4,0},{5,1},{6,2},{7,3},{8,12},{9,13},{10,... | collective-permute-start | bytes 221192 | tf_op jit(solution)/shard_map/sums_far/ppermute | solution.py:23
  (3 other events, 2.2 us)

commit v5 on v4

--- a/solution.py
+++ b/solution.py
@@ -323,12 +323,12 @@
     smem, vmem = pl.BlockSpec(memory_space=pltpu.SMEM), pl.BlockSpec(memory_space=pltpu.VMEM)
     xp = prev_input[0]
     xp_far = hop(xp, 0, half, "xp_far")
-    dy_in = hop(next_cot[0], -1, 0, "dy_in")
-    x_in = hop(next_input[0], 1, 0, "x_in")
     table = jnp.concatenate(
         [next_routes[0].T, prev_routes[0].T, next_priority, prev_priority], axis=0
     )
     far_table = hop(table, 0, half, "tables")
+    dy_in = hop(after(next_cot[0], table), -1, 0, "dy_in")
+    x_in = hop(after(next_input[0], xp_far), 1, 0, "x_in")
 
     def ranks(table, name):
         dims = shape((experts, tokens), jnp.int32)

time: 310 us -> 311 us (level)
  transfers between devices with their start and end apart: 24 -> 24, of which waited for: 13 -> 14; matrix products, arithmetic and copies ran while one was open for 8% -> 7% of each run, Pallas kernels for 17% -> 17%
where the time goes in v5:
time: 311 us; the launch traced here: 310 us
  waiting for transfers between devices  155 us (50%)
  Pallas kernels  51.7 us (17%)
  starting transfers between devices  49.7 us (16%)
  local copies, waits for them, and re-layouts  33.2 us (11%)
  matrix products  18.5 us (6%)
    ppermute x18, waiting for transfers between devices, hop(): lax.ppermute(block, 'expert', [(e, e ^ flip) for e in range(experts)])  144 us
    pallas_call x11, Pallas kernels, call(): pl.pallas_call(kernel, out_shape=[jax.ShapeDtypeStruct(o.shape, o.dtype)...  45.1 us
    ppermute x18, starting transfers between devices, hop(): lax.ppermute(block, 'expert', [(e, e ^ flip) for e in range(experts)])  28.9 us
    unnamed x88, local copies, waits for them, and re-layouts  25.8 us
    all_to_all x3, starting transfers between devices, exchange(): lax.all_to_all(array, 'expert', 0, 0, tiled=True, axis_index_groups=groups)  16.5 us
    dot_general x3, matrix products, t_dot(): lax.dot_general(a, b, dims, preferred_element_type=F32, precision=precision)  14.5 us
    ppermute x3, waiting for transfers between devices, hop(): return lax.ppermute(block, ('pipe', 'expert'), route)  10.3 us
    transpose x3, local copies, waits for them, and re-layouts, per_device(): jnp.swapaxes(a, 0, 1).reshape(count, hidden)  6.77 us
  transfers between devices with their start and end apart: 24, of which 14 were waited for; matrix products, arithmetic and copies ran while one was open for 7% of the time, Pallas kernels for 17%

profile of v5, /device:TPU:0, one launch (start us, length us, event | category | flops | bytes accessed | tf_op | source)
XLA Modules:
  0.0 309.9 jit_solution(12500887580420768047)
XLA Ops:
  1.4 2.5 collective-permute-start.2
  3.8 2.6 collective-permute-start
  6.7 1.2 copy-done.11
  7.9 0.8 copy-done.16
  9.4 2.6 own_rows.1
  12.7 1.5 collective-permute-start.4
  14.2 1.6 collective-permute-start.5
  16.5 2.6 collective-permute-start.3
  19.1 3.1 cots.1
  22.1 30.2 %collective-permute-done.3.table_ref.refs_4_ = s32[6,256]{1,0:T(8,128)S(1)} collective-permute-done((s32[6,256]{1,0:T(8,128)S(1)}, s32[6,256]{1,0:T(8,128)S(1)}, u32[]{:S(2)}, u32[]{:S(2)}) %collective-permute-start.3) | collective-permute-done | bytes 6176 | tf_op jit(solution)/shard_map/tables/ppermute | solution.py:23
  52.4 0.7 copy-done.35
  53.9 5.8 %all-to-all-start = ((bf16[8,80,2048]{2,1,0:T(8,128)(2,1)}), bf16[8,80,2048]{2,1,0:T(8,128)(2,1)}, u32[]{:S(2)}, u32[]{:S(2)}) async-start(bf16[8,80,2048]{2,1,0:T(8,128)(2,1)} %cots.1), calls=%async_computation | async-start | bytes 5242880 | tf_op jit(solution)/shard_map/cots/all_to_all | solution.py:316
  59.9 2.6 far_rows.1
  62.5 2.1 collective-permute-start.7
  64.6 1.5 collective-permute-start.8
  66.1 23.5 %collective-permute-done.7.refs_15_ = bf16[80,2176]{1,0:T(8,128)(2,1)S(1)} collective-permute-done((bf16[80,2176]{1,0:T(8,128)(2,1)S(1)}, bf16[80,2176]{1,0:T(8,128)(2,1)S(1)}, u32[]{:S(2)}, u32[]{:S(2)}) %collective-permute-start.7) | collective-permute-done | bytes 348192 | tf_op jit(solution)/shard_map/far_rows/ppermute | solution.py:23
  89.6 22.1 %collective-permute-done.8.refs_16_ = bf16[80,2176]{1,0:T(8,128)(2,1)S(1)} collective-permute-done((bf16[80,2176]{1,0:T(8,128)(2,1)S(1)}, bf16[80,2176]{1,0:T(8,128)(2,1)S(1)}, u32[]{:S(2)}, u32[]{:S(2)}) %collective-permute-start.8) | collective-permute-done | bytes 348192 | tf_op jit(solution)/shard_map/far_rows/ppermute | solution.py:23
  111.7 6.5 %collective-permute-done.9.refs_17_ = bf16[80,2176]{1,0:T(8,128)(2,1)S(1)} collective-permute-done((bf16[80,2176]{1,0:T(8,128)(2,1)S(1)}, bf16[80,2176]{1,0:T(8,128)(2,1)S(1)}, u32[]{:S(2)}, u32[]{:S(2)}) %collective-permute-start.9) | collective-permute-done | bytes 348192 | tf_op jit(solution)/shard_map/far_rows/ppermute | solution.py:23
  118.2 1.2 all-to-all-done.refs_9_
  119.4 1.7 collective-permute-start.10
  121.1 2.2 fown_rows.1
  124.6 0.9 collective-permute-start.15
  125.5 2.0 collective-permute-start.16
  127.9 28.2 %expert.1 = (bf16[640,2048]{1,0:T(8,128)(2,1)}, bf16[640,2048]{1,0:T(8,128)(2,1)}, bf16[640,2048]{1,0:T(8,128)(2,1)}, bf16[3,640,256]{2,1,0:T(8,128)(2,1)}, bf16...) custom-call(s32[1]{0:T(128)} %bitcast.6.refs_0_.me_ref, bf16[2048,768]{1,0:T(8,128)(2,1)} %bitcast.46, ...), custom_call_target="tpu_custom_call" | custom-call | flops 188743680 | bytes 551040 | tf_op jit(solution)/shard_map/expert/pallas_call | solution.py:56
  156.1 0.7 copy-done.23
  158.3 10.0 %collective-permute-done.10.refs_1_ = bf16[256,2048]{1,0:T(8,128)(2,1)S(1)} collective-permute-done((bf16[256,2048]{1,0:T(8,128)(2,1)}, bf16[256,2048]{1,0:T(8,128)(2,1)S(1)}, u32[]{:S(2)}, u32[]{:S(2)}) %collective-permute-start.10) | collective-permute-done | bytes 1048608 | tf_op jit(solution)/shard_map/x_far/ppermute | solution.py:29
  168.3 1.0 copy-done.14
  169.3 4.9 %all-to-all-start.1 = ((bf16[8,80,2048]{2,1,0:T(8,128)(2,1)}), bf16[8,80,2048]{2,1,0:T(8,128)(2,1)S(1)}, u32[]{:S(2)}, u32[]{:S(2)}) async-start(bf16[8,80,2048]{2,1,0:T(8,128)(2,1)} %bitcast.66), calls=%async_computation.1 | async-start | bytes 5242880 | tf_op jit(solution)/shard_map/grads/all_to_all | solution.py:316
  174.2 1.9 copy-done
  176.0 1.9 copy-done.2
  177.9 1.9 copy-done.4
  179.8 1.0 copy-done.22
  180.8 1.0 copy-done.24
  181.8 1.0 copy-done.26
  182.7 1.0 copy-done.28
  183.7 3.3 %forward_own.1.refs_4_ = bf16[8,80,2048]{2,1,0:T(8,128)(2,1)S(1)} custom-call(s32[1]{0:T(128)} %bitcast.6.refs_0_.me_ref, bf16[2048,768]{1,0:T(8,128)(2,1)S(1)} %bitcast.48, bf16[2048,768]{1,0:T(8,128)(2,1)S(1)} %bitcast.52, bf16[768,2048]{1,0:T(8,128)(2,1)S(1)} %bitcast.56, bf16[80,2048]{1,0:T(8,128)(2,1)S(1)} %copy-done.22, ...), custom_call_target="tpu_custom_call" | custom-call | flops 3019898880 | bytes 9437184 | tf_op jit(solution)/shard_map/forward_own/pallas_call | solution.py:441
  187.0 1.5 copy-done.6
  188.6 2.2 copy.20
  190.9 2.3 copy.22
  193.1 2.3 copy.21
  195.4 1.2 copy-done.15
  196.7 2.8 ffar_rows.1
  199.5 2.0 collective-permute-start.11
  201.5 1.5 collective-permute-start.12
  202.9 6.5 %convolution_convert_fusion.1 = bf16[2048,768]{1,0:T(8,128)(2,1)} fusion(bf16[640,2048]{1,0:T(8,128)(2,1)} %get-tuple-element.75, bf16[640,768]{0,1:T(8,128)(2,1)} %bitcast.73), kind=kOutput, calls=%fused_computation.1 | convolution fusion | flops 2014838784 | bytes 6750208 | tf_op jit(solution)/shard_map/dot_general | solution.py:46
  209.5 4.1 %convolution_convert_fusion.2 = bf16[2048,768]{1,0:T(8,128)(2,1)} fusion(bf16[640,2048]{1,0:T(8,128)(2,1)S(1)} %copy-done.42, bf16[640,768]{0,1:T(8,128)(2,1)S(1)} %bitcast.72), kind=kOutput, calls=%fused_computation.2 | convolution fusion | flops 2014838784 | bytes 6750208 | tf_op jit(solution)/shard_map/dot_general | solution.py:46
  213.6 4.0 %convolution_convert_fusion = bf16[768,2048]{1,0:T(8,128)(2,1)} fusion(bf16[640,768]{0,1:T(8,128)(2,1)S(1)} %bitcast.71, bf16[640,2048]{1,0:T(8,128)(2,1)S(1)} %copy-done.41), kind=kOutput, calls=%fused_computation | convolution fusion | flops 2014838784 | bytes 6750208 | tf_op jit(solution)/shard_map/dot_general | solution.py:46
  217.5 2.8 collective-permute-done.11.refs_1_
  220.3 5.1 %collective-permute-done.12.refs_2_ = bf16[80,2048]{1,0:T(8,128)(2,1)S(1)} collective-permute-done((bf16[80,2048]{1,0:T(8,128)(2,1)S(1)}, bf16[80,2048]{1,0:T(8,128)(2,1)S(1)}, u32[]{:S(2)}, u32[]{:S(2)}) %collective-permute-start.12) | collective-permute-done | bytes 327712 | tf_op jit(solution)/shard_map/ffar_rows/ppermute | solution.py:23
  225.4 5.9 %collective-permute-done.13.refs_3_ = bf16[80,2048]{1,0:T(8,128)(2,1)S(1)} collective-permute-done((bf16[80,2048]{1,0:T(8,128)(2,1)S(1)}, bf16[80,2048]{1,0:T(8,128)(2,1)S(1)}, u32[]{:S(2)}, u32[]{:S(2)}) %collective-permute-start.13) | collective-permute-done | bytes 327712 | tf_op jit(solution)/shard_map/ffar_rows/ppermute | solution.py:23
  231.4 3.3 %forward_far.1 = bf16[8,80,2048]{2,1,0:T(8,128)(2,1)S(1)} custom-call(s32[1]{0:T(128)} %bitcast.6.refs_0_.me_ref, bf16[2048,768]{1,0:T(8,128)(2,1)S(1)} %bitcast.49, bf16[2048,768]{1,0:T(8,128)(2,1)S(1)} %bitcast.53, bf16[768,2048]{1,0:T(8,128)(2,1)S(1)} %bitcast.57, bf16[80,2048]{1,0:T(8,128)(2,1)S(1)} %get-tuple-element.61.refs_0_, ...), custom_call_target="tpu_custom_call", output_to_operand_aliasing={{}: (8, {})} | custom-call | flops 3019898880 | bytes 9437184 | tf_op jit(solution)/shard_map/forward_far/pallas_call | solution.py:441
  234.7 1.5 copy-done.8
  236.2 5.9 %all-to-all-start.2 = ((bf16[8,80,2048]{2,1,0:T(8,128)(2,1)}), bf16[8,80,2048]{2,1,0:T(8,128)(2,1)}, u32[]{:S(2)}, u32[]{:S(2)}) async-start(bf16[8,80,2048]{2,1,0:T(8,128)(2,1)} %copy-done.8), calls=%async_computation.2 | async-start | bytes 5242880 | tf_op jit(solution)/shard_map/outs/all_to_all | solution.py:316
  242.1 2.0 collective-permute-start.17
  244.2 1.5 collective-permute-start.18
  245.9 1.2 copy-done.10
  247.2 1.2 copy-done.12
  248.4 2.8 source.1
  251.2 12.4 %collective-permute-done.17 = f32[8,2304]{1,0:T(8,128)S(1)} collective-permute-done((f32[8,2304]{1,0:T(8,128)S(1)}, f32[8,2304]{1,0:T(8,128)S(1)}, u32[]{:S(2)}, u32[]{:S(2)}) %collective-permute-start.17) | collective-permute-done | bytes 73760 | tf_op jit(solution)/shard_map/sums/ppermute | solution.py:23
  263.6 22.6 %collective-permute-done.18 = f32[8,2304]{1,0:T(8,128)S(1)} collective-permute-done((f32[8,2304]{1,0:T(8,128)S(1)}, f32[8,2304]{1,0:T(8,128)S(1)}, u32[]{:S(2)}, u32[]{:S(2)}) %collective-permute-start.18) | collective-permute-done | bytes 73760 | tf_op jit(solution)/shard_map/sums/ppermute | solution.py:23
  286.2 0.8 collective-permute-done.19
  287.0 5.9 %collective-permute-start.20 = (f32[8,2304]{1,0:T(8,128)S(1)}, f32[8,2304]{1,0:T(8,128)S(1)}, u32[]{:S(2)}, u32[]{:S(2)}) collective-permute-start(f32[8,2304]{1,0:T(8,128)S(1)} %add_add_fusion), channel_id=1, source_target_pairs={{0,4},{1,5},{2,6},{3,7},{4,0},{5,1},{6,2},{7,3},{8,12},{9,13},{10,... | collective-permute-start | bytes 221192 | tf_op jit(solution)/shard_map/sums_far/ppermute | solution.py:23
  292.9 11.8 %collective-permute-done.20 = f32[8,2304]{1,0:T(8,128)S(1)} collective-permute-done((f32[8,2304]{1,0:T(8,128)S(1)}, f32[8,2304]{1,0:T(8,128)S(1)}, u32[]{:S(2)}, u32[]{:S(2)}) %collective-permute-start.20) | collective-permute-done | bytes 73760 | tf_op jit(solution)/shard_map/sums_far/ppermute | solution.py:23
  305.9 4.0 %fusion = bf16[1,256,2048]{2,1,0:T(8,128)(2,1)} fusion(bf16[256,2048]{1,0:T(8,128)(2,1)} %copy-done.13, bf16[256,640]{1,0:T(8,128)(2,1)S(1)} %spread.1, bf16[640,2048]{1,0:T(8,128)(2,1)} %bitcast.21), kind=kOutput, calls=%fused_computation.4 | convolution fusion | flops 672661504 | bytes 5046272 | tf_op jit(solution)/shard_map/dot_general | solution.py:37
  (101 shorter events, 9.1 us)
Async XLA Ops:
  1.4 15.1 %collective-permute-start.2 = (bf16[256,2048]{1,0:T(8,128)(2,1)}, bf16[256,2048]{1,0:T(8,128)(2,1)S(1)}, u32[]{:S(2)}, u32[]{:S(2)}) collective-permute-start(bf16[256,2048]{1,0:T(8,128)(2,1)} %bitcast.77), channel_id=1, source_target_pairs={{0,24},{1,25},{2,26},{3,27},{4,28},{5,29},{6,30},{7,31},{8,0},{9,1... | collective-permute-start | bytes 3145736 | tf_op jit(solution)/shard_map/dy_in/ppermute | solution.py:29
  3.8 50.0 %collective-permute-start = (bf16[256,2048]{1,0:T(8,128)(2,1)}, bf16[256,2048]{1,0:T(8,128)(2,1)S(1)}, u32[]{:S(2)}, u32[]{:S(2)}) collective-permute-start(bf16[256,2048]{1,0:T(8,128)(2,1)} %bitcast.58), channel_id=1, source_target_pairs={{0,4},{1,5},{2,6},{3,7},{4,0},{5,1},{6,2},{7,3},{8,12},{9,13},{10,... | collective-permute-start | bytes 3145736 | tf_op jit(solution)/shard_map/xp_far/ppermute | solution.py:23
  6.7 1.2 copy-start.11
  7.9 0.8 copy-start.16
  11.9 0.7 copy-start.19
  12.7 39.7 %collective-permute-start.4 = (bf16[80,2176]{1,0:T(8,128)(2,1)S(1)}, bf16[80,2176]{1,0:T(8,128)(2,1)S(1)}, u32[]{:S(2)}, u32[]{:S(2)}) collective-permute-start(bf16[80,2176]{1,0:T(8,128)(2,1)S(1)} %get-tuple-element.51), channel_id=1, source_target_pairs={{0,1},{1,0},{2,3},{3,2},{4,5},{5,4},{6,7},{7,6},{8,9},{9,8},{10,11... | collective-permute-start | bytes 1044488 | tf_op jit(solution)/shard_map/own_rows/ppermute | solution.py:23
  14.2 38.2 %collective-permute-start.5 = (bf16[80,2176]{1,0:T(8,128)(2,1)S(1)}, bf16[80,2176]{1,0:T(8,128)(2,1)S(1)}, u32[]{:S(2)}, u32[]{:S(2)}) collective-permute-start(bf16[80,2176]{1,0:T(8,128)(2,1)S(1)} %get-tuple-element.52), channel_id=1, source_target_pairs={{0,2},{1,3},{2,0},{3,1},{4,6},{5,7},{6,4},{7,5},{8,10},{9,11},{10,... | collective-permute-start | bytes 1044488 | tf_op jit(solution)/shard_map/own_rows/ppermute | solution.py:23
  15.7 36.6 %collective-permute-start.6 = (bf16[80,2176]{1,0:T(8,128)(2,1)S(1)}, bf16[80,2176]{1,0:T(8,128)(2,1)S(1)}, u32[]{:S(2)}, u32[]{:S(2)}) collective-permute-start(bf16[80,2176]{1,0:T(8,128)(2,1)S(1)} %get-tuple-element.53), channel_id=1, source_target_pairs={{0,3},{1,2},{2,1},{3,0},{4,7},{5,6},{6,5},{7,4},{8,11},{9,10},{10,... | collective-permute-start | bytes 1044488 | tf_op jit(solution)/shard_map/own_rows/ppermute | solution.py:23
  16.5 37.4 %copy-start.9 = (bf16[256,2048]{1,0:T(8,128)(2,1)}, bf16[256,2048]{1,0:T(8,128)(2,1)S(1)}, u32[]{:S(2)}) copy-start(bf16[256,2048]{1,0:T(8,128)(2,1)S(1)} %collective-permute-done.2.x_ref.dy_ref) | copy-start | bytes 3145732
  16.5 35.9 %collective-permute-start.3 = (s32[6,256]{1,0:T(8,128)S(1)}, s32[6,256]{1,0:T(8,128)S(1)}, u32[]{:S(2)}, u32[]{:S(2)}) collective-permute-start(s32[6,256]{1,0:T(8,128)S(1)} %pad_add_fusion.table_ref.refs_4_), channel_id=1, source_target_pairs={{0,4},{1,5},{2,6},{3,7},{4,0},{5,1},{6,2},{7,3},{8,12},{9,13},{10,... | collective-permute-start | bytes 18440 | tf_op jit(solution)/shard_map/tables/ppermute | solution.py:23
  22.1 37.7 %copy-start.17 = (bf16[1,2048,8]{1,2,0:T(8,128)(2,1)S(1)}, bf16[1,2048,8]{1,2,0:T(8,128)(2,1)}, u32[]{:S(2)}) copy-start(bf16[1,2048,8]{1,2,0:T(8,128)(2,1)} %param.18) | copy-start | bytes 98308
  22.1 37.7 %copy-start.30 = (f32[1,2048]{1,0:T(1,128)S(1)}, f32[1,2048]{1,0:T(1,128)}, u32[]{:S(2)}) copy-start(f32[1,2048]{1,0:T(1,128)} %gain_ref.1) | copy-start | bytes 24580
  52.3 1.5 copy-start.34
  52.3 0.8 copy-start.35
  53.1 0.7 copy-start.36
  53.9 65.5 %all-to-all-start = ((bf16[8,80,2048]{2,1,0:T(8,128)(2,1)}), bf16[8,80,2048]{2,1,0:T(8,128)(2,1)}, u32[]{:S(2)}, u32[]{:S(2)}) async-start(bf16[8,80,2048]{2,1,0:T(8,128)(2,1)} %cots.1), calls=%async_computation | async-start | bytes 5242880 | tf_op jit(solution)/shard_map/cots/all_to_all | solution.py:316
  62.5 65.4 %copy-start.20 = (bf16[80,2176]{1,0:T(8,128)(2,1)}, bf16[80,2176]{1,0:T(8,128)(2,1)S(1)}, u32[]{:S(2)}) copy-start(bf16[80,2176]{1,0:T(8,128)(2,1)S(1)} %get-tuple-element.70.refs_14_) | copy-start | bytes 1044484
  62.5 27.1 %collective-permute-start.7 = (bf16[80,2176]{1,0:T(8,128)(2,1)S(1)}, bf16[80,2176]{1,0:T(8,128)(2,1)S(1)}, u32[]{:S(2)}, u32[]{:S(2)}) collective-permute-start(bf16[80,2176]{1,0:T(8,128)(2,1)S(1)} %get-tuple-element.56), channel_id=1, source_target_pairs={{0,1},{1,0},{2,3},{3,2},{4,5},{5,4},{6,7},{7,6},{8,9},{9,8},{10,11... | collective-permute-start | bytes 1044488 | tf_op jit(solution)/shard_map/far_rows/ppermute | solution.py:23
  64.6 47.1 %collective-permute-start.8 = (bf16[80,2176]{1,0:T(8,128)(2,1)S(1)}, bf16[80,2176]{1,0:T(8,128)(2,1)S(1)}, u32[]{:S(2)}, u32[]{:S(2)}) collective-permute-start(bf16[80,2176]{1,0:T(8,128)(2,1)S(1)} %get-tuple-element.57), channel_id=1, source_target_pairs={{0,2},{1,3},{2,0},{3,1},{4,6},{5,7},{6,4},{7,5},{8,10},{9,11},{10,... | collective-permute-start | bytes 1044488 | tf_op jit(solution)/shard_map/far_rows/ppermute | solution.py:23
  66.0 52.2 %collective-permute-start.9 = (bf16[80,2176]{1,0:T(8,128)(2,1)S(1)}, bf16[80,2176]{1,0:T(8,128)(2,1)S(1)}, u32[]{:S(2)}, u32[]{:S(2)}) collective-permute-start(bf16[80,2176]{1,0:T(8,128)(2,1)S(1)} %get-tuple-element.58), channel_id=1, source_target_pairs={{0,3},{1,2},{2,1},{3,0},{4,7},{5,6},{6,5},{7,4},{8,11},{9,10},{10,... | collective-permute-start | bytes 1044488 | tf_op jit(solution)/shard_map/far_rows/ppermute | solution.py:23
  66.1 55.0 %collective-permute-start.1 = (bf16[256,2048]{1,0:T(8,128)(2,1)}, bf16[256,2048]{1,0:T(8,128)(2,1)S(1)}, u32[]{:S(2)}, u32[]{:S(2)}) collective-permute-start(bf16[256,2048]{1,0:T(8,128)(2,1)} %bitcast.78), channel_id=1, source_target_pairs={{0,8},{1,9},{2,10},{3,11},{4,12},{5,13},{6,14},{7,15},{8,16},{9,17... | collective-permute-start | bytes 3145736 | tf_op jit(solution)/shard_map/x_in/ppermute | solution.py:29
  89.6 38.3 %copy-start.37 = (bf16[80,2176]{1,0:T(8,128)(2,1)}, bf16[80,2176]{1,0:T(8,128)(2,1)S(1)}, u32[]{:S(2)}) copy-start(bf16[80,2176]{1,0:T(8,128)(2,1)S(1)} %collective-permute-done.7.refs_15_) | copy-start | bytes 1044484
  111.7 16.2 %copy-start.38 = (bf16[80,2176]{1,0:T(8,128)(2,1)}, bf16[80,2176]{1,0:T(8,128)(2,1)S(1)}, u32[]{:S(2)}) copy-start(bf16[80,2176]{1,0:T(8,128)(2,1)S(1)} %collective-permute-done.8.refs_16_) | copy-start | bytes 1044484
  118.2 9.7 %copy-start.39 = (bf16[80,2176]{1,0:T(8,128)(2,1)}, bf16[80,2176]{1,0:T(8,128)(2,1)S(1)}, u32[]{:S(2)}) copy-start(bf16[80,2176]{1,0:T(8,128)(2,1)S(1)} %collective-permute-done.9.refs_17_) | copy-start | bytes 1044484
  119.4 48.9 %collective-permute-start.10 = (bf16[256,2048]{1,0:T(8,128)(2,1)}, bf16[256,2048]{1,0:T(8,128)(2,1)S(1)}, u32[]{:S(2)}, u32[]{:S(2)}) collective-permute-start(bf16[256,2048]{1,0:T(8,128)(2,1)} %bitcast.79), channel_id=1, source_target_pairs={{0,12},{1,13},{2,14},{3,15},{4,8},{5,9},{6,10},{7,11},{8,20},{9,21... | collective-permute-start | bytes 3145736 | tf_op jit(solution)/shard_map/x_far/ppermute | solution.py:29
  121.1 35.0 %copy-start.13 = (bf16[256,2048]{1,0:T(8,128)(2,1)}, bf16[256,2048]{1,0:T(8,128)(2,1)S(1)}, u32[]{:S(2)}) copy-start(bf16[256,2048]{1,0:T(8,128)(2,1)S(1)} %collective-permute-done.1.refs_1_) | copy-start | bytes 3145732
  123.3 0.7 copy-start.21
  124.1 32.1 %collective-permute-start.14 = (bf16[80,2048]{1,0:T(8,128)(2,1)S(1)}, bf16[80,2048]{1,0:T(8,128)(2,1)S(1)}, u32[]{:S(2)}, u32[]{:S(2)}) collective-permute-start(bf16[80,2048]{1,0:T(8,128)(2,1)S(1)} %get-tuple-element.66), channel_id=1, source_target_pairs={{0,1},{1,0},{2,3},{3,2},{4,5},{5,4},{6,7},{7,6},{8,9},{9,8},{10,11... | collective-permute-start | bytes 983048 | tf_op jit(solution)/shard_map/fown_rows/ppermute | solution.py:23
  124.6 32.2 %collective-permute-start.15 = (bf16[80,2048]{1,0:T(8,128)(2,1)S(1)}, bf16[80,2048]{1,0:T(8,128)(2,1)S(1)}, u32[]{:S(2)}, u32[]{:S(2)}) collective-permute-start(bf16[80,2048]{1,0:T(8,128)(2,1)S(1)} %get-tuple-element.67), channel_id=1, source_target_pairs={{0,2},{1,3},{2,0},{3,1},{4,6},{5,7},{6,4},{7,5},{8,10},{9,11},{10,... | collective-permute-start | bytes 983048 | tf_op jit(solution)/shard_map/fown_rows/ppermute | solution.py:23
  125.5 32.1 %collective-permute-start.16 = (bf16[80,2048]{1,0:T(8,128)(2,1)S(1)}, bf16[80,2048]{1,0:T(8,128)(2,1)S(1)}, u32[]{:S(2)}, u32[]{:S(2)}) collective-permute-start(bf16[80,2048]{1,0:T(8,128)(2,1)S(1)} %get-tuple-element.68), channel_id=1, source_target_pairs={{0,3},{1,2},{2,1},{3,0},{4,7},{5,6},{6,5},{7,4},{8,11},{9,10},{10,... | collective-permute-start | bytes 983048 | tf_op jit(solution)/shard_map/fown_rows/ppermute | solution.py:23
  156.1 0.8 copy-start.23
  168.3 1.0 copy-start.14
  169.3 66.9 %all-to-all-start.1 = ((bf16[8,80,2048]{2,1,0:T(8,128)(2,1)}), bf16[8,80,2048]{2,1,0:T(8,128)(2,1)S(1)}, u32[]{:S(2)}, u32[]{:S(2)}) async-start(bf16[8,80,2048]{2,1,0:T(8,128)(2,1)} %bitcast.66), calls=%async_computation.1 | async-start | bytes 5242880 | tf_op jit(solution)/shard_map/grads/all_to_all | solution.py:316
  174.2 1.9 copy-start
  176.0 1.9 copy-start.2
  177.9 1.9 copy-start.4
  179.8 1.0 copy-start.22
  180.8 1.0 copy-start.24
  181.8 1.0 copy-start.26
  182.7 1.0 copy-start.28
  183.7 4.8 %copy-start.40 = (f32[16,2048]{1,0:T(8,128)S(1)}, f32[16,2048]{1,0:T(8,128)}, u32[]{:S(2)}) copy-start(f32[16,2048]{1,0:T(8,128)} %get-tuple-element.80) | copy-start | bytes 393220
  187.0 1.6 copy-start.6
  188.6 6.8 %copy-start.18 = (bf16[1,2048,8]{1,2,0:T(8,128)(2,1)S(1)}, bf16[1,2048,8]{1,2,0:T(8,128)(2,1)}, u32[]{:S(2)}) copy-start(bf16[1,2048,8]{1,2,0:T(8,128)(2,1)} %param.18) | copy-start | bytes 98308
  188.6 6.8 %copy-start.31 = (f32[1,2048]{1,0:T(1,128)S(1)}, f32[1,2048]{1,0:T(1,128)}, u32[]{:S(2)}) copy-start(f32[1,2048]{1,0:T(1,128)} %gain_ref.1) | copy-start | bytes 24580
  195.4 1.2 copy-start.15
  199.5 20.9 %collective-permute-start.11 = (bf16[80,2048]{1,0:T(8,128)(2,1)S(1)}, bf16[80,2048]{1,0:T(8,128)(2,1)S(1)}, u32[]{:S(2)}, u32[]{:S(2)}) collective-permute-start(bf16[80,2048]{1,0:T(8,128)(2,1)S(1)} %get-tuple-element.62), channel_id=1, source_target_pairs={{0,1},{1,0},{2,3},{3,2},{4,5},{5,4},{6,7},{7,6},{8,9},{9,8},{10,11... | collective-permute-start | bytes 983048 | tf_op jit(solution)/shard_map/ffar_rows/ppermute | solution.py:23
  201.5 23.9 %collective-permute-start.12 = (bf16[80,2048]{1,0:T(8,128)(2,1)S(1)}, bf16[80,2048]{1,0:T(8,128)(2,1)S(1)}, u32[]{:S(2)}, u32[]{:S(2)}) collective-permute-start(bf16[80,2048]{1,0:T(8,128)(2,1)S(1)} %get-tuple-element.63), channel_id=1, source_target_pairs={{0,2},{1,3},{2,0},{3,1},{4,6},{5,7},{6,4},{7,5},{8,10},{9,11},{10,... | collective-permute-start | bytes 983048 | tf_op jit(solution)/shard_map/ffar_rows/ppermute | solution.py:23
  202.9 28.4 %collective-permute-start.13 = (bf16[80,2048]{1,0:T(8,128)(2,1)S(1)}, bf16[80,2048]{1,0:T(8,128)(2,1)S(1)}, u32[]{:S(2)}, u32[]{:S(2)}) collective-permute-start(bf16[80,2048]{1,0:T(8,128)(2,1)S(1)} %get-tuple-element.64), channel_id=1, source_target_pairs={{0,3},{1,2},{2,1},{3,0},{4,7},{5,6},{6,5},{7,4},{8,11},{9,10},{10,... | collective-permute-start | bytes 983048 | tf_op jit(solution)/shard_map/ffar_rows/ppermute | solution.py:23
  202.9 6.5 %copy-start.33 = (bf16[640,3,256]{0,2,1:T(8,128)(2,1)S(1)}, bf16[640,3,256]{0,2,1:T(8,128)(2,1)}, u32[]{:S(2)}) copy-start(bf16[640,3,256]{0,2,1:T(8,128)(2,1)} %copy.21) | copy-start | bytes 2949124
  202.9 6.5 %copy-start.42 = (bf16[640,2048]{1,0:T(8,128)(2,1)S(1)}, bf16[640,2048]{1,0:T(8,128)(2,1)}, u32[]{:S(2)}) copy-start(bf16[640,2048]{1,0:T(8,128)(2,1)} %get-tuple-element.75) | copy-start | bytes 7864324
  209.4 4.1 %copy-start.32 = (bf16[640,3,256]{0,2,1:T(8,128)(2,1)S(1)}, bf16[640,3,256]{0,2,1:T(8,128)(2,1)}, u32[]{:S(2)}) copy-start(bf16[640,3,256]{0,2,1:T(8,128)(2,1)} %copy.20) | copy-start | bytes 2949124
  209.4 4.1 %copy-start.41 = (bf16[640,2048]{1,0:T(8,128)(2,1)S(1)}, bf16[640,2048]{1,0:T(8,128)(2,1)}, u32[]{:S(2)}) copy-start(bf16[640,2048]{1,0:T(8,128)(2,1)} %get-tuple-element.79) | copy-start | bytes 7864324
  209.4 21.9 %copy-start.7 = (bf16[8,80,2048]{2,1,0:T(8,128)(2,1)S(1)}, bf16[8,80,2048]{2,1,0:T(8,128)(2,1)}, u32[]{:S(2)}) copy-start(bf16[8,80,2048]{2,1,0:T(8,128)(2,1)} %copy-done.6) | copy-start | bytes 7864324
  213.5 17.8 %copy-start.1 = (bf16[1,1,2048,768]{3,2,1,0:T(8,128)(2,1)S(1)}, bf16[1,1,2048,768]{3,2,1,0:T(8,128)(2,1)}, u32[]{:S(2)}) copy-start(bf16[1,1,2048,768]{3,2,1,0:T(8,128)(2,1)} %param.15) | copy-start | bytes 9437188
  213.5 17.8 %copy-start.3 = (bf16[1,1,2048,768]{3,2,1,0:T(8,128)(2,1)S(1)}, bf16[1,1,2048,768]{3,2,1,0:T(8,128)(2,1)}, u32[]{:S(2)}) copy-start(bf16[1,1,2048,768]{3,2,1,0:T(8,128)(2,1)} %param.16) | copy-start | bytes 9437188
  213.5 17.8 %copy-start.5 = (bf16[1,1,768,2048]{3,2,1,0:T(8,128)(2,1)S(1)}, bf16[1,1,768,2048]{3,2,1,0:T(8,128)(2,1)}, u32[]{:S(2)}) copy-start(bf16[1,1,768,2048]{3,2,1,0:T(8,128)(2,1)} %param.17) | copy-start | bytes 9437188
  234.7 1.5 copy-start.8
  236.2 69.7 %all-to-all-start.2 = ((bf16[8,80,2048]{2,1,0:T(8,128)(2,1)}), bf16[8,80,2048]{2,1,0:T(8,128)(2,1)}, u32[]{:S(2)}, u32[]{:S(2)}) async-start(bf16[8,80,2048]{2,1,0:T(8,128)(2,1)} %copy-done.8), calls=%async_computation.2 | async-start | bytes 5242880 | tf_op jit(solution)/shard_map/outs/all_to_all | solution.py:316
  242.1 21.5 %collective-permute-start.17 = (f32[8,2304]{1,0:T(8,128)S(1)}, f32[8,2304]{1,0:T(8,128)S(1)}, u32[]{:S(2)}, u32[]{:S(2)}) collective-permute-start(f32[8,2304]{1,0:T(8,128)S(1)} %pad_maximum_fusion), channel_id=1, source_target_pairs={{0,1},{1,0},{2,3},{3,2},{4,5},{5,4},{6,7},{7,6},{8,9},{9,8},{10,11... | collective-permute-start | bytes 221192 | tf_op jit(solution)/shard_map/sums/ppermute | solution.py:23
  244.2 42.1 %collective-permute-start.18 = (f32[8,2304]{1,0:T(8,128)S(1)}, f32[8,2304]{1,0:T(8,128)S(1)}, u32[]{:S(2)}, u32[]{:S(2)}) collective-permute-start(f32[8,2304]{1,0:T(8,128)S(1)} %pad_maximum_fusion), channel_id=1, source_target_pairs={{0,2},{1,3},{2,0},{3,1},{4,6},{5,7},{6,4},{7,5},{8,10},{9,11},{10,... | collective-permute-start | bytes 221192 | tf_op jit(solution)/shard_map/sums/ppermute | solution.py:23
  245.6 41.4 %collective-permute-start.19 = (f32[8,2304]{1,0:T(8,128)S(1)}, f32[8,2304]{1,0:T(8,128)S(1)}, u32[]{:S(2)}, u32[]{:S(2)}) collective-permute-start(f32[8,2304]{1,0:T(8,128)S(1)} %pad_maximum_fusion), channel_id=1, source_target_pairs={{0,3},{1,2},{2,1},{3,0},{4,7},{5,6},{6,5},{7,4},{8,11},{9,10},{10,... | collective-permute-start | bytes 221192 | tf_op jit(solution)/shard_map/sums/ppermute | solution.py:23
  245.9 1.2 copy-start.10
  247.2 1.2 copy-start.12
  287.0 17.6 %collective-permute-start.20 = (f32[8,2304]{1,0:T(8,128)S(1)}, f32[8,2304]{1,0:T(8,128)S(1)}, u32[]{:S(2)}, u32[]{:S(2)}) collective-permute-start(f32[8,2304]{1,0:T(8,128)S(1)} %add_add_fusion), channel_id=1, source_target_pairs={{0,4},{1,5},{2,6},{3,7},{4,0},{5,1},{6,2},{7,3},{8,12},{9,13},{10,... | collective-permute-start | bytes 221192 | tf_op jit(solution)/shard_map/sums_far/ppermute | solution.py:23
  (3 other events, 2.2 us)
